TPU v7x, 256 devices: a whole 4x4x8 slice. The times are simulated.
256 devices in a mesh: track: 8 (over z_hi, y), tm: 32 (over z_lo, x, core).
Axes of the slice: x: 4, y: 4, z: 8 (z_hi: 2, z_lo: 4; z = z_hi * 4 + z_lo), core: 2. Of those that a mesh axis runs over, the one named last changes fastest.
Arguments:
- track_query: bfloat16 [16, 4096, 1024], P('track', 'tm'), may hold values from -6 to 6
- track_key: bfloat16 [16, 4096, 1024], P('track', 'tm'), may hold values from -6 to 6
- track_value: bfloat16 [16, 4096, 1024], P('track', 'tm'), may hold values from -6 to 6
- log_decay: float32 [16, 8, 4096], P('track', None, 'tm'), may hold values from -2.3 to 0
- valid_length: int32 [16], replicated, may hold values from 1024 to 4096, as said below
- initial_state: bfloat16 [16, 8, 128, 128], P('track'), may hold values from -24 to 24
- cross_query: bfloat16 [16, 4096, 1024], P('track', 'tm'), may hold values from -5 to 5
- cross_key: bfloat16 [16, 4096, 1024], P('track', 'tm'), may hold values from -5 to 5
- grad_out: bfloat16 [16, 4096, 1024], P('track', 'tm'), may hold values from -6 to 6
Outputs:
- grad_query: bfloat16 [16, 4096, 1024], P('track', 'tm')
- grad_key: bfloat16 [16, 4096, 1024], P('track', 'tm')
- grad_value: bfloat16 [16, 4096, 1024], P('track', 'tm')
- grad_cross_query: bfloat16 [16, 4096, 1024], P('track', 'tm')
- grad_cross_key: bfloat16 [16, 4096, 1024], P('track', 'tm')
Inputs may be any that keep to these rules, and one draw needn't show every extreme that they name: `valid_length`: multiples of 128; one track has 4096 valid steps and one has exactly 1024.
All inputs are finite; a program needn't handle non-finite values.
Results may differ from a plain program's by a relative error of at most 0.005.
Values may be sent and summed in bfloat16 or wider, within the bound.
No kernel may reach another device: no remote copies, remote signals or barrier semaphores. Data moves between devices by JAX's collectives and lax.ppermute only.
A program may use at most 192 MiB of HBM per device.

v0:
```python
import jax
import jax.numpy as jnp
from jax import lax
from jax.sharding import PartitionSpec as P

EPSILON = 1e-06
HIGHEST_PRECISION = lax.Precision.HIGHEST


def prefix_2(value, axis, join, neutral, backward):
    count, mine = (lax.axis_size(axis), lax.axis_index(axis))
    pieces = jax.tree.map(lambda part: lax.all_gather(part, axis), value)
    if backward:
        pieces = jax.tree.map(lambda part: part[::-1], pieces)
        mine = count - 1 - mine
    running = jax.tree.map(
        lambda part, zero: jnp.full_like(part, 0) + jnp.asarray(zero, part.dtype), value, neutral
    )

    def lap(position, running):
        longer = join(running, jax.tree.map(lambda part: part[position], pieces))
        return jax.tree.map(lambda new, old: jnp.where(position < mine, new, old), longer, running)

    return lax.fori_loop(0, count - 1, lap, running)


def carry_combine(earlier, later):
    return (earlier[0] * later[0], later[0][:, :, None, None] * earlier[1] + later[1])


def per_device(
    track_query,
    track_key,
    track_value,
    log_decay,
    valid_length,
    initial_state,
    cross_query,
    cross_key,
    grad_out,
):
    local_tracks, local_time, model_width = track_query.shape
    head_count = log_decay.shape[1]
    head_size = model_width // head_count
    block_rows = min(128, local_time)
    blocks = local_time // block_rows
    group_size = lax.axis_size("track")
    all_tracks = valid_length.shape[0]
    time_first = lax.axis_index("tm") * local_time
    track_ids = lax.axis_index("track") * local_tracks + jnp.arange(local_tracks)
    picked = jnp.arange(all_tracks)[None, :] == track_ids[:, None]
    own_length = jnp.sum(jnp.where(picked, valid_length[None, :], 0), axis=1)
    time_index = time_first + jnp.arange(local_time)
    valid_rows = (time_index[None, :] < own_length[:, None]).astype(jnp.float32)
    five_dims = (local_tracks, blocks, block_rows, head_count, head_size)
    query_blocks = track_query.reshape(five_dims)
    key_masked = (track_key * valid_rows[:, :, None].astype(jnp.bfloat16)).reshape(five_dims)
    value_blocks = track_value.reshape(five_dims)
    query_float = query_blocks.astype(jnp.float32)
    key_float = key_masked.astype(jnp.float32)
    value_float = value_blocks.astype(jnp.float32)
    mask_rows = valid_rows.reshape(local_tracks, blocks, block_rows)[..., None, None]
    within = jnp.cumsum(log_decay.reshape(local_tracks, head_count, blocks, block_rows), axis=-1)
    lower_mask = jnp.arange(block_rows)[:, None] >= jnp.arange(block_rows)[None, :]
    decay_matrix = jnp.exp(
        jnp.where(lower_mask, within[..., :, None] - within[..., None, :], -jnp.inf)
    )
    to_end_rows = jnp.transpose(jnp.exp(within[..., -1:] - within), (0, 2, 3, 1))[..., None]
    from_start_rows = jnp.transpose(jnp.exp(within), (0, 2, 3, 1))[..., None]
    block_decay = jnp.exp(within[..., -1])
    device_decay = jnp.exp(jnp.sum(log_decay, axis=-1))
    scores = (
        jnp.einsum(
            "xnthc,xnshc->xhnts", query_blocks, key_masked, preferred_element_type=jnp.float32
        )
        * decay_matrix
    )
    intra_out = jnp.einsum("xhnts,xnshd->xnthd", scores, value_float, precision=HIGHEST_PRECISION)
    block_states = jnp.einsum(
        "xnshc,xnshd->xhncd", key_float * to_end_rows, value_float, precision=HIGHEST_PRECISION
    )
    zero_state = jnp.zeros((local_tracks, head_count, head_size, head_size), jnp.float32)
    partial_value = [zero_state]
    lead_in = [jnp.ones_like(device_decay)]
    position = 0
    partial_value.append(
        block_decay[:, :, position, None, None] * partial_value[-1] + block_states[:, :, position]
    )
    lead_in.append(lead_in[-1] * block_decay[:, :, position])
    prefix = prefix_2(
        (device_decay, partial_value[-1]),
        "tm",
        carry_combine,
        (jnp.ones_like(device_decay), jnp.zeros_like(zero_state)),
        False,
    )
    state_in = prefix[1] + prefix[0][:, :, None, None] * initial_state.astype(jnp.float32)
    start_states = jnp.stack([partial_value[0] + lead_in[0][:, :, None, None] * state_in], axis=2)
    outputs = intra_out + from_start_rows * jnp.einsum(
        "xnthc,xhncd->xnthd", query_float, start_states, precision=HIGHEST_PRECISION
    )
    mean_square = jnp.mean(outputs * outputs, axis=-1, keepdims=True)
    inverse = 1.0 / jnp.sqrt(mean_square + EPSILON)
    four_dims = (local_tracks, local_time, head_count, head_size)
    normed = (outputs * inverse * mask_rows).astype(jnp.bfloat16).reshape(four_dims)
    query_cross = cross_query.reshape(four_dims)
    key_cross = cross_key.reshape(four_dims)
    grad_rows = grad_out.reshape(four_dims)
    normed_x, query_x, key_x, grad_x = (
        lax.all_to_all(normed, "track", split_axis=1, concat_axis=0, tiled=True),
        lax.all_to_all(query_cross, "track", split_axis=1, concat_axis=0, tiled=True),
        lax.all_to_all(key_cross, "track", split_axis=1, concat_axis=0, tiled=True),
        lax.all_to_all(grad_rows, "track", split_axis=1, concat_axis=0, tiled=True),
    )
    time_rows = local_time // group_size
    block_times = time_first + lax.axis_index("track") * time_rows + jnp.arange(time_rows)
    key_valid = block_times[None, :] < valid_length[:, None]
    scale_root = float(head_size) ** 0.5
    logits = (
        jnp.einsum("irhc,jrhc->rhij", query_x, key_x, preferred_element_type=jnp.float32)
        / scale_root
    )
    logits = jnp.where(jnp.transpose(key_valid)[:, None, None, :], logits, -1e30)
    row_max = jnp.max(logits, axis=-1, keepdims=True)
    weights = jnp.exp(logits - row_max)
    weights = weights / jnp.sum(weights, axis=-1, keepdims=True)
    grad_masked_half = grad_x * key_valid.astype(jnp.bfloat16)[:, :, None, None]
    grad_masked = grad_masked_half.astype(jnp.float32)
    grad_weights = jnp.einsum(
        "irhc,jrhc->rhij", grad_masked_half, normed_x, preferred_element_type=jnp.float32
    )
    grad_logits = (
        weights
        * (grad_weights - jnp.sum(weights * grad_weights, axis=-1, keepdims=True))
        / scale_root
    )
    grad_normed = jnp.einsum(
        "rhij,irhc->jrhc", weights, grad_masked, precision=HIGHEST_PRECISION
    ).astype(jnp.bfloat16)
    grad_query_x = jnp.einsum(
        "rhij,jrhc->irhc", grad_logits, key_x.astype(jnp.float32), precision=HIGHEST_PRECISION
    ).astype(jnp.bfloat16)
    grad_key_x = jnp.einsum(
        "rhij,irhc->jrhc", grad_logits, query_x.astype(jnp.float32), precision=HIGHEST_PRECISION
    ).astype(jnp.bfloat16)
    grad_normed_t, grad_query_t, grad_key_t = (
        lax.all_to_all(grad_normed, "track", split_axis=0, concat_axis=1, tiled=True),
        lax.all_to_all(grad_query_x, "track", split_axis=0, concat_axis=1, tiled=True),
        lax.all_to_all(grad_key_x, "track", split_axis=0, concat_axis=1, tiled=True),
    )
    grad_unit = grad_normed_t.astype(jnp.float32).reshape(five_dims)
    along_output = jnp.sum(grad_unit * outputs, axis=-1, keepdims=True)
    grad_outputs = mask_rows * (
        inverse * grad_unit - inverse * inverse * inverse / head_size * along_output * outputs
    )
    grad_scores = (
        jnp.einsum("xnthd,xnshd->xhnts", grad_outputs, value_float, precision=HIGHEST_PRECISION)
        * decay_matrix
    )
    to_state = jnp.einsum(
        "xnthc,xnthd->xhncd",
        query_float * from_start_rows,
        grad_outputs,
        precision=HIGHEST_PRECISION,
    )
    local_grad = [zero_state]
    position = 0
    local_grad.insert(
        0, to_state[:, :, position] + block_decay[:, :, position, None, None] * local_grad[0]
    )
    tail_decay = jnp.ones_like(device_decay)
    end_grad = prefix_2(
        (device_decay, local_grad[0]),
        "tm",
        carry_combine,
        (jnp.ones_like(device_decay), jnp.zeros_like(zero_state)),
        True,
    )[1]
    out_grads = jnp.stack([local_grad[1] + tail_decay[:, :, None, None] * end_grad], axis=2)
    grad_query = jnp.einsum(
        "xhnts,xnshc->xnthc", grad_scores, key_float, precision=HIGHEST_PRECISION
    )
    grad_query = grad_query + from_start_rows * jnp.einsum(
        "xnthd,xhncd->xnthc", grad_outputs, start_states, precision=HIGHEST_PRECISION
    )
    grad_key = jnp.einsum(
        "xhnts,xnthc->xnshc", grad_scores, query_float, precision=HIGHEST_PRECISION
    )
    grad_key = (
        grad_key
        + to_end_rows
        * jnp.einsum("xnshd,xhncd->xnshc", value_float, out_grads, precision=HIGHEST_PRECISION)
    ) * mask_rows
    grad_value = jnp.einsum("xhnts,xnthd->xnshd", scores, grad_outputs, precision=HIGHEST_PRECISION)
    grad_value = grad_value + to_end_rows * jnp.einsum(
        "xnshc,xhncd->xnshd", key_float, out_grads, precision=HIGHEST_PRECISION
    )
    flat_shape = (local_tracks, local_time, model_width)
    return (
        grad_query.astype(jnp.bfloat16).reshape(flat_shape),
        grad_key.astype(jnp.bfloat16).reshape(flat_shape),
        grad_value.astype(jnp.bfloat16).reshape(flat_shape),
        grad_query_t.reshape(flat_shape),
        grad_key_t.reshape(flat_shape),
    )


def solution(mesh):
    placed = (
        P("track", "tm", None),
        P("track", "tm", None),
        P("track", "tm", None),
        P("track", None, "tm"),
        P(),
        P("track", None, None, None),
        P("track", "tm", None),
        P("track", "tm", None),
        P("track", "tm", None),
    )
    return jax.shard_map(
        per_device,
        mesh=mesh,
        in_specs=placed,
        out_specs=(
            P("track", "tm", None),
            P("track", "tm", None),
            P("track", "tm", None),
            P("track", "tm", None),
            P("track", "tm", None),
        ),
        check_vma=False,
    )
```

profile of v0, /device:TPU:1, one launch (start us, length us, event | category | flops | bytes accessed | tf_op | source)
XLA Modules:
  0.0 606.4 jit_solution(11515392250774700342)
XLA Ops:
  15.1 11.6 %all-to-all-start.1 = ((bf16[2,128,8,128]{3,2,0,1:T(8,128)(2,1)}), bf16[2,128,8,128]{3,2,0,1:T(8,128)(2,1)S(1)}, u32[]{:S(2)}, u32[]{:S(2)}) async-start(bf16[2,128,8,128]{3,2,0,1:T(8,128)(2,1)} %copy.232), calls=%async_computation.1 | async-start | bytes 1048576 | tf_op jit(solution)/shard_map/all_to_all | solution.py:111
  28.8 14.2 %all-to-all-done.1 = bf16[2,128,8,128]{3,2,0,1:T(8,128)(2,1)S(1)} async-done(((bf16[2,128,8,128]{3,2,0,1:T(8,128)(2,1)}), bf16[2,128,8,128]{3,2,0,1:T(8,128)(2,1)S(1)}, u32[]{:S(2)}, u32[]{:S(2)}) %all-to-all-start.1) | async-done | bytes 524320 | tf_op jit(solution)/shard_map/all_to_all | solution.py:111
  43.0 4.2 all-to-all-start.2
  49.2 16.5 %all-to-all-done.2 = bf16[2,128,8,128]{3,2,0,1:T(8,128)(2,1)S(1)} async-done(((bf16[2,128,8,128]{3,2,0,1:T(8,128)(2,1)}), bf16[2,128,8,128]{3,2,0,1:T(8,128)(2,1)S(1)}, u32[]{:S(2)}, u32[]{:S(2)}) %all-to-all-start.2) | async-done | bytes 524320 | tf_op jit(solution)/shard_map/all_to_all | solution.py:112
  65.8 3.8 all-to-all-start
  72.1 13.3 %all-to-all-done = bf16[2,128,8,128]{3,2,0,1:T(8,128)(2,1)S(1)} async-done(((bf16[2,128,8,128]{3,2,0,1:T(8,128)(2,1)}), bf16[2,128,8,128]{3,2,0,1:T(8,128)(2,1)S(1)}, u32[]{:S(2)}, u32[]{:S(2)}) %all-to-all-start) | async-done | bytes 524320 | tf_op jit(solution)/shard_map/all_to_all | solution.py:113
  89.2 3.9 all-to-all-start.3
  95.2 63.4 %all-gather.3 = f32[32,2,8]{2,1,0:T(2,128)S(1)} all-gather(f32[1,2,8]{2,1,0:T(2,128)S(1)} %exponential_bitcast_fusion.2), channel_id=2, replica_groups=mesh['track'=8,'tm'=32] {'tm'}, dimensions={0}, use_global_device_ids=true | all-gather | bytes 2112 | tf_op jit(solution)/shard_map/all_gather | solution.py:12
  158.6 2.5 fusion.2
  165.8 78.9 %all-gather.7.cloned.1.call-done = f32[64,8,128,128]{3,2,1,0:T(8,128)} async-done(((f32[2,8,128,128]{3,2,1,0:T(8,128)}), f32[64,8,128,128]{3,2,1,0:T(8,128)}) %all-gather.7.cloned.1.call-update) | async-done | bytes 33554448 | tf_op jit(solution)/shard_map/all_gather | solution.py:12
  244.7 46.6 %while.30 = (s32[]{:T(128)}, f32[2,8]{1,0:T(2,128)S(1)}, f32[2,8,128,128]{3,2,1,0:T(8,128)S(1)}, s32[]{:T(128)}, f32[32,2,8]{2,1,0:T(2,128)S(1)}, /*index=5*/f32[32,2,8,128,128]{4,3,2,1,0:T(8,128)}, s32[]{:T(128)}, s32[]{:T(128)}) while((s32[]{:T(128)}, f32[2,8]{1,0:T(2,128)S(1)}, f32[2,8,128,128]{3,2,1,0:T(8,128)S(1)}, s32[]{:T(128)}, ...), condition=%wide.region_4.5_spmd.clone, body=%wide.region_3.4_spmd.clone.sunk | while | flops 1048628 | bytes 3146163 | solution.py:24
  291.3 2.1 fusion.8
  293.5 2.2 multiply_reduce_fusion.2
  297.8 3.3 convolution_add_fusion
  302.6 26.9 %all_to_all.111 = bf16[2,128,8,128]{3,2,0,1:T(8,128)(2,1)S(1)} all-to-all(bf16[2,128,8,128]{3,2,0,1:T(8,128)(2,1)S(1)} %copy.209), channel_id=1, replica_groups=mesh['track'=8,'tm'=32] {'track'}, dimensions={1} | all-to-all | bytes 1048576 | tf_op jit(solution)/shard_map/all_to_all | solution.py:110
  330.0 2.0 multiply_reduce_fusion
  333.0 2.4 fusion.18
  336.3 3.9 all-to-all-start.6
  340.2 2.8 fusion.17
  344.0 17.2 %all-to-all-done.6 = bf16[16,16,8,128]{3,2,1,0:T(8,128)(2,1)S(1)} async-done(((bf16[16,16,8,128]{3,2,1,0:T(8,128)(2,1)}), bf16[16,16,8,128]{3,2,1,0:T(8,128)(2,1)S(1)}, u32[]{:S(2)}, u32[]{:S(2)}) %all-to-all-start.6) | async-done | bytes 524320 | tf_op jit(solution)/shard_map/all_to_all | solution.py:149
  361.2 4.4 all-to-all-start.5
  365.6 2.1 convolution_multiply_fusion
  370.4 3.5 fusion.15
  373.9 2.0 copy.217
  378.1 7.7 %all-to-all-done.5 = bf16[16,16,8,128]{3,2,1,0:T(8,128)(2,1)} async-done(((bf16[16,16,8,128]{3,2,1,0:T(8,128)(2,1)}), bf16[16,16,8,128]{3,2,1,0:T(8,128)(2,1)}, u32[]{:S(2)}, u32[]{:S(2)}) %all-to-all-start.5) | async-done | bytes 524320 | tf_op jit(solution)/shard_map/all_to_all | solution.py:148
  387.9 129.6 %all-gather.9.cloned.1.call-done = f32[64,8,128,128]{3,2,1,0:T(8,128)} async-done(((f32[2,8,128,128]{3,2,1,0:T(8,128)}), f32[64,8,128,128]{3,2,1,0:T(8,128)}) %all-gather.9.cloned.1.call-update) | async-done | bytes 33554448 | tf_op jit(solution)/shard_map/all_gather | solution.py:12
  517.5 23.1 %rev.7 = f32[32,2,8,128,128]{4,3,2,1,0:T(8,128)} reverse(f32[32,2,8,128,128]{4,3,2,1,0:T(8,128)} %bitcast.217), dimensions={0} | reverse | bytes 67108864 | tf_op jit(solution)/shard_map/rev | solution.py:14
  540.6 46.4 %while.31 = (s32[]{:T(128)}, f32[2,8,128,128]{3,2,1,0:T(8,128)S(1)}, s32[]{:T(128)}, f32[32,2,8]{2,1,0:T(2,128)S(1)}, f32[32,2,8,128,128]{4,3,2,1,0:T(8,128)}, /*index=5*/s32[]{:T(128)}, s32[]{:T(128)}) while((s32[]{:T(128)}, f32[2,8,128,128]{3,2,1,0:T(8,128)S(1)}, s32[]{:T(128)}, f32[32,2,8]{2,1,0:T(2,128)S(1)}, ...), condition=%wide.region_10.11_spmd.clone, body=%wide.region_9.10_spmd.clone.sunk | while | flops 1048580 | bytes 3146025 | solution.py:24
  587.0 2.1 fusion.12
  589.1 2.2 fusion.11
  591.3 3.5 fusion.13
  595.8 2.8 fusion.14
  (204 shorter events, 132.0 us)
Async XLA Ops:
  7.2 4.2 copy-start
  7.2 237.5 %all-gather.7.cloned.1.call-start = ((), (), s32[]{:S(2)}) async-start(), calls=%async_computation.7 | async-start | bytes 34603008 | tf_op jit(solution)/shard_map/all_gather | solution.py:12
  9.9 83.2 %copy-start.4 = (bf16[2,128,8,128]{1,3,2,0:T(8,128)(2,1)}, bf16[2,128,8,128]{1,3,2,0:T(8,128)(2,1)S(1)}, u32[]{:S(2)}) copy-start(bf16[2,128,8,128]{1,3,2,0:T(8,128)(2,1)S(1)} %copy.198) | copy-start | bytes 1572868
  15.1 27.8 %all-to-all-start.1 = ((bf16[2,128,8,128]{3,2,0,1:T(8,128)(2,1)}), bf16[2,128,8,128]{3,2,0,1:T(8,128)(2,1)S(1)}, u32[]{:S(2)}, u32[]{:S(2)}) async-start(bf16[2,128,8,128]{3,2,0,1:T(8,128)(2,1)} %copy.232), calls=%async_computation.1 | async-start | bytes 1048576 | tf_op jit(solution)/shard_map/all_to_all | solution.py:111
  43.0 22.8 %all-to-all-start.2 = ((bf16[2,128,8,128]{3,2,0,1:T(8,128)(2,1)}), bf16[2,128,8,128]{3,2,0,1:T(8,128)(2,1)S(1)}, u32[]{:S(2)}, u32[]{:S(2)}) async-start(bf16[2,128,8,128]{3,2,0,1:T(8,128)(2,1)} %copy.234), calls=%async_computation.2 | async-start | bytes 1048576 | tf_op jit(solution)/shard_map/all_to_all | solution.py:112
  65.8 19.7 %all-to-all-start = ((bf16[2,128,8,128]{3,2,0,1:T(8,128)(2,1)}), bf16[2,128,8,128]{3,2,0,1:T(8,128)(2,1)S(1)}, u32[]{:S(2)}, u32[]{:S(2)}) async-start(bf16[2,128,8,128]{3,2,0,1:T(8,128)(2,1)} %copy.231), calls=%async_computation | async-start | bytes 1048576 | tf_op jit(solution)/shard_map/all_to_all | solution.py:113
  71.6 89.6 %copy-start.7 = (bf16[8,2,16,8,128]{4,1,0,3,2:T(2,128)(2,1)}, bf16[8,2,16,8,128]{4,1,0,3,2:T(2,128)(2,1)S(1)}, u32[]{:S(2)}) copy-start(bf16[8,2,16,8,128]{4,1,0,3,2:T(2,128)(2,1)S(1)} %copy.187) | copy-start | bytes 1572868
  72.1 21.0 %copy-start.6 = (bf16[8,2,16,8,128]{4,1,0,3,2:T(2,128)(2,1)}, bf16[8,2,16,8,128]{4,1,0,3,2:T(2,128)(2,1)S(1)}, u32[]{:S(2)}) copy-start(bf16[8,2,16,8,128]{4,1,0,3,2:T(2,128)(2,1)S(1)} %copy.190) | copy-start | bytes 1572868
  86.0 3.2 copy-start.10
  86.4 1.0 copy-start.5
  89.2 72.0 %all-to-all-start.3 = ((bf16[16,16,8,128]{3,2,1,0:T(8,128)(2,1)}), bf16[16,16,8,128]{3,2,1,0:T(8,128)(2,1)S(1)}, u32[]{:S(2)}, u32[]{:S(2)}) async-start(bf16[16,16,8,128]{3,2,1,0:T(8,128)(2,1)} %copy.191), calls=%async_computation.3 | async-start | bytes 1048576 | tf_op jit(solution)/shard_map/all_to_all | solution.py:147
  93.1 424.4 %all-gather.9.cloned.1.call-start = ((), (), s32[]{:S(2)}) async-start(), calls=%async_computation.8 | async-start | bytes 34603008 | tf_op jit(solution)/shard_map/all_gather | solution.py:12
  161.2 0.8 copy-start.8
  296.8 1.0 copy-start.1
  332.0 1.0 copy-start.11
  336.3 24.8 %all-to-all-start.6 = ((bf16[16,16,8,128]{3,2,1,0:T(8,128)(2,1)}), bf16[16,16,8,128]{3,2,1,0:T(8,128)(2,1)S(1)}, u32[]{:S(2)}, u32[]{:S(2)}) async-start(bf16[16,16,8,128]{3,2,1,0:T(8,128)(2,1)} %copy.215), calls=%async_computation.6 | async-start | bytes 1048576 | tf_op jit(solution)/shard_map/all_to_all | solution.py:149
  361.2 4.4 copy-start.9
  361.2 24.6 %all-to-all-start.5 = ((bf16[16,16,8,128]{3,2,1,0:T(8,128)(2,1)}), bf16[16,16,8,128]{3,2,1,0:T(8,128)(2,1)}, u32[]{:S(2)}, u32[]{:S(2)}) async-start(bf16[16,16,8,128]{3,2,1,0:T(8,128)(2,1)} %copy.213), calls=%async_computation.5 | async-start | bytes 1048576 | tf_op jit(solution)/shard_map/all_to_all | solution.py:148
  367.7 1.0 copy-start.3
  517.5 73.8 %copy-start.2 = (f32[2,1,128,8,128]{2,4,3,0,1:T(8,128)S(1)}, f32[2,1,128,8,128]{2,4,3,0,1:T(8,128)}, u32[]{:S(2)}) copy-start(f32[2,1,128,8,128]{2,4,3,0,1:T(8,128)} %copy-done.1) | copy-start | bytes 3145732
Sparse Core Ops, SparseCore 0:
  13.2 231.4 all-gather.6
  301.2 216.2 all-gather.8
where the time goes:
time: 611 us; the launch traced here: 606 us
  waiting for transfers between devices  277 us (45%)
  other arithmetic  99.5 us (16%)
  blocking collectives  90.3 us (15%)
  local copies, waits for them, and re-layouts  52.8 us (9%)
  matrix products  38.3 us (6%)
  starting transfers between devices  31.8 us (5%)
  between operations  14.4 us (2%)
    all_gather x2, waiting for transfers between devices, prefix_2(): pieces = jax.tree.map(lambda part: lax.all_gather(part, axis), value)  208 us
    select_n x93, other arithmetic, lap(): jnp.where(position < mine, new, old)  90.9 us
    all_gather x1, blocking collectives, prefix_2(): pieces = jax.tree.map(lambda part: lax.all_gather(part, axis), value)  63.4 us
    all_to_all x1, blocking collectives, per_device(): lax.all_to_all(normed, 'track', split_axis=1, concat_axis=0, tiled=True)  26.9 us
    rev x2, local copies, waits for them, and re-layouts, prefix_2(): pieces = jax.tree.map(lambda part: part[::-1], pieces)  23.1 us
    all_to_all x1, waiting for transfers between devices, per_device(): lax.all_to_all(grad_key_x, 'track', split_axis=0, concat_axis=1, tiled=True)  17.2 us
    all_to_all x1, waiting for transfers between devices, per_device(): lax.all_to_all(key_cross, 'track', split_axis=1, concat_axis=0, tiled=True)  16.5 us
    all_to_all x1, waiting for transfers between devices, per_device(): lax.all_to_all(query_cross, 'track', split_axis=1, concat_axis=0, tiled=T...  14.2 us
  transfers between devices with their start and end apart: 8, of which 7 were waited for; matrix products, arithmetic and copies ran while one was open for 7% of the time, Pallas kernels for 0%

commit v1 on v0

v1 whole, which is shorter than its diff:
```python
import functools

import jax
import jax.numpy as jnp
from jax import lax
from jax.experimental import pallas as pl
from jax.experimental.pallas import tpu as pltpu
from jax.sharding import PartitionSpec as P

F32, BF16 = jnp.float32, jnp.bfloat16
EPSILON = 1e-06
NEG = -1e30
H, DH = 8, 128
T = 128
NY, NE, NZ = 4, 8, 4
RY = T // NY
PR = DH + 8
VMEM_LIMIT = 48 * 1024 * 1024

NN = ((1,), (0,))
NT = ((1,), (1,))
TN = ((0,), (0,))


def parts(x):
    if x.dtype == BF16:
        return [x]
    hi = x.astype(BF16)
    return [hi, (x - hi.astype(F32)).astype(BF16)]


def dot(a, b, dims):
    pa, pb = parts(a), parts(b)
    if len(pa) == 2 and len(pb) == 2:
        left, right = [pa[0], pa[0], pa[1]], [pb[0], pb[1], pb[0]]
    else:
        n = max(len(pa), len(pb))
        left = pa * (n // len(pa))
        right = pb * (n // len(pb))
    if len(left) > 1:
        left = jnp.concatenate(left, axis=dims[0][0])
        right = jnp.concatenate(right, axis=dims[1][0])
    else:
        left, right = left[0], right[0]
    return lax.dot_general(left, right, (dims, ((), ())), preferred_element_type=F32)


def sums(ld):
    r = lax.broadcasted_iota(jnp.int32, (T, T), 0)
    c = lax.broadcasted_iota(jnp.int32, (T, T), 1)
    upper = (r <= c).astype(F32)
    lower = (r >= c).astype(F32)
    row = lax.dot_general(
        ld, upper, (NN, ((), ())), precision=lax.Precision.HIGHEST, preferred_element_type=F32
    )
    col = lax.dot_general(
        lower, ld, (NT, ((), ())), precision=lax.Precision.HIGHEST, preferred_element_type=F32
    )
    return row, col, r >= c


def vmem_call(body, out_shape, n_smem, n_in, flops=1 << 28, name=None):
    return pl.pallas_call(
        body,
        out_shape=out_shape,
        in_specs=[pl.BlockSpec(memory_space=pltpu.SMEM)] * n_smem
        + [pl.BlockSpec(memory_space=pltpu.VMEM)] * n_in,
        out_specs=jax.tree.map(lambda _: pl.BlockSpec(memory_space=pltpu.VMEM), out_shape),
        compiler_params=pltpu.CompilerParams(vmem_limit_bytes=VMEM_LIMIT),
        name=name,
    )


def shape(*dims, dtype=F32):
    return jax.ShapeDtypeStruct(dims, dtype)


def cols(h):
    return slice(h * DH, (h + 1) * DH)


def block_state_kernel(valid, ld_ref, k_ref, v_ref, out_ref):
    for x in range(2):
        row, col, _ = sums(ld_ref[x])
        for h in range(H):
            p = x * H + h
            total = row[h : h + 1, T - 1 : T]
            scaled = v_ref[x, :, cols(h)].astype(F32) * jnp.exp(col[T - 1 : T, h : h + 1] - col[:, h : h + 1])
            state = dot(k_ref[x, :, cols(h)], scaled, TN)
            out_ref[p // 2, p % 2, 0:DH, :] = state * valid[x].astype(F32)
            out_ref[p // 2, p % 2, DH:PR, :] = jnp.broadcast_to(total, (PR - DH, DH))


def row_total_kernel(back, in_ref, out_ref):
    for p in range(2):
        order = range(NE - 1, -1, -1) if back else range(NE)
        state, total = None, None
        for e in order:
            ld = in_ref[e, p, DH : DH + 1, :]
            if state is None:
                state, total = in_ref[e, p, 0:DH, :], ld
            else:
                state = jnp.exp(ld) * state + in_ref[e, p, 0:DH, :]
                total = total + ld
        out_ref[p, 0:DH, :] = state
        out_ref[p, DH:PR, :] = jnp.broadcast_to(total, (PR - DH, DH))


def row_starts_kernel(back, at, *refs):
    if back:
        row_ref, far3, far2, far1, out_ref = refs
    else:
        init_ref, row_ref, far3, far2, far1, out_ref = refs
    for p in range(2):
        if back:
            state = jnp.zeros((DH, DH), F32)
        else:
            pair = at[0] * 2 + p
            state = init_ref[pair // H, pair % H].astype(F32)
        for far in (far3, far2, far1):
            state = jnp.exp(far[p, DH : DH + 1, :]) * state + far[p, 0:DH, :]
        for e in range(NE - 1, -1, -1) if back else range(NE):
            out_ref[e, p] = state
            state = jnp.exp(row_ref[e, p, DH : DH + 1, :]) * state + row_ref[e, p, 0:DH, :]


def outputs_kernel(valid, ld_ref, q_ref, k_ref, v_ref, s_ref, out_ref, normed_ref):
    for x in range(2):
        row, col, keep = sums(ld_ref[x])
        flag = valid[x].astype(F32)
        for h in range(H):
            p = x * H + h
            q, k, v = q_ref[x, :, cols(h)], k_ref[x, :, cols(h)], v_ref[x, :, cols(h)]
            decay = jnp.exp(jnp.where(keep, col[:, h : h + 1] - row[h : h + 1, :], -jnp.inf))
            scores = dot(q, k, NT) * (decay * flag)
            out = dot(scores, v, NN) + jnp.exp(col[:, h : h + 1]) * dot(q, s_ref[p // 2, p % 2], NN)
            inverse = 1.0 / jnp.sqrt(jnp.mean(out * out, axis=-1, keepdims=True) + EPSILON)
            out_ref[x, :, cols(h)] = out
            normed = (out * (inverse * flag)).astype(BF16)
            for y in range(NY):
                normed_ref[y, x, :, cols(h)] = normed[y * RY : (y + 1) * RY, :]


def same_time():
    t = lax.broadcasted_iota(jnp.int32, (16, 256), 0)
    lane = lax.broadcasted_iota(jnp.int32, (16, 256), 1)
    return (lane & 15) == t


def take(ref, g, h):
    part = ref[:, :, g * 16 : (g + 1) * 16, cols(h)]
    return part.reshape(128, DH)


def both(own_ref, other_ref, g, h):
    return jnp.concatenate([take(own_ref, g, h), take(other_ref, g, h)], axis=0)


def scaled_logits(key_valid, keys, queries):
    logits = (dot(keys, queries, NT) * (1.0 / float(DH) ** 0.5)).reshape(8, 16, 256)
    return [jnp.where(key_valid[j] > 0, logits[j], NEG) for j in range(8)]


def put(ref, g, h, value):
    value = value.astype(ref.dtype).reshape(NY, 2, 16, DH)
    ref[:, :, g * 16 : (g + 1) * 16, cols(h)] = value


def stats_kernel(key_valid, k_ref, q_ref, qx_ref, max_ref, sum_ref):
    mask = same_time()
    for h in range(H):
        for g in range(RY // 16):
            logits = scaled_logits(key_valid, take(k_ref, g, h), both(q_ref, qx_ref, g, h))
            top = functools.reduce(jnp.maximum, logits)
            total = functools.reduce(jnp.add, [jnp.exp(one - top) for one in logits])
            r = h * (RY // 16) + g
            max_ref[r : r + 1, :] = jnp.sum(jnp.where(mask, top, 0.0), axis=0, keepdims=True)
            sum_ref[r : r + 1, :] = jnp.sum(jnp.where(mask, total, 0.0), axis=0, keepdims=True)


def swap_halves(x):
    return jnp.concatenate([x[:, 128:], x[:, :128]], axis=1)


def weights_of(key_valid, k, q, r, max_ref, sum_ref, maxx_ref, sumx_ref, mask):
    logits = scaled_logits(key_valid, k, q)
    m, mx = max_ref[r : r + 1, :], swap_halves(maxx_ref[r : r + 1, :])
    top = jnp.maximum(m, mx)
    total = sum_ref[r : r + 1, :] * jnp.exp(m - top) + swap_halves(sumx_ref[r : r + 1, :]) * jnp.exp(mx - top)
    inverse = 1.0 / total
    return [jnp.where(mask, jnp.exp(one - top) * inverse, 0.0) for one in logits]


def mix_kernel(key_valid, k_ref, q_ref, qx_ref, n_ref, g_ref, gx_ref, max_ref, sum_ref, maxx_ref, sumx_ref, vi_ref, gn_ref, rd_ref):
    mask = same_time()
    vi = vi_ref[0:1, :]
    for h in range(H):
        for g in range(RY // 16):
            r = h * (RY // 16) + g
            weights = weights_of(
                key_valid, take(k_ref, g, h), both(q_ref, qx_ref, g, h), r, max_ref, sum_ref, maxx_ref, sumx_ref, mask
            )
            grads = both(g_ref, gx_ref, g, h)
            grad_weights = dot(take(n_ref, g, h), grads, NT).reshape(8, 16, 256)
            weights = [one * vi for one in weights]
            put(gn_ref, g, h, dot(jnp.concatenate(weights, axis=0), grads, NN))
            total = functools.reduce(jnp.add, [weights[j] * grad_weights[j] for j in range(8)])
            rd_ref[r : r + 1, :] = jnp.sum(total, axis=0, keepdims=True)


def cross_grads_kernel(
    key_valid, k_ref, q_ref, qx_ref, n_ref, g_ref, gx_ref, max_ref, sum_ref, maxx_ref, sumx_ref, vi_ref, rd_ref, rdx_ref,
    gk_ref, gq_ref, gqx_ref,
):
    mask = same_time()
    vi = vi_ref[0:1, :]
    for h in range(H):
        for g in range(RY // 16):
            r = h * (RY // 16) + g
            keys, queries = take(k_ref, g, h), both(q_ref, qx_ref, g, h)
            weights = weights_of(key_valid, keys, queries, r, max_ref, sum_ref, maxx_ref, sumx_ref, mask)
            grads = both(g_ref, gx_ref, g, h)
            grad_weights = dot(take(n_ref, g, h), grads, NT).reshape(8, 16, 256)
            along = rd_ref[r : r + 1, :] + swap_halves(rdx_ref[r : r + 1, :])
            scale = vi * (1.0 / float(DH) ** 0.5)
            grad_logits = jnp.concatenate(
                [weights[j] * (grad_weights[j] - along) * scale for j in range(8)], axis=0
            )
            put(gk_ref, g, h, dot(grad_logits, queries, NN))
            grad_queries = dot(grad_logits, keys, TN)
            put(gq_ref, g, h, grad_queries[:128])
            put(gqx_ref, g, h, grad_queries[128:])


def join_kernel(gq_ref, gqx_ref, gk_ref, out_ref):
    for y in range(NY):
        out_ref[y, 0] = (gq_ref[y] + gqx_ref[y].astype(F32)).astype(BF16)
        out_ref[y, 1] = gk_ref[y]


def grad_outputs_kernel(valid, ld_ref, q_ref, out_ref, gn_ref, go_ref, msg_ref):
    for x in range(2):
        row, col, _ = sums(ld_ref[x])
        flag = valid[x].astype(F32)
        for h in range(H):
            p = x * H + h
            out = out_ref[x, :, cols(h)]
            grad = jnp.concatenate([gn_ref[y, x, :, cols(h)] for y in range(NY)], axis=0).astype(F32)
            inverse = 1.0 / jnp.sqrt(jnp.mean(out * out, axis=-1, keepdims=True) + EPSILON)
            along = jnp.sum(grad * out, axis=-1, keepdims=True)
            go = flag * (inverse * grad - (inverse * inverse * inverse * (1.0 / DH) * along) * out)
            go_ref[x, :, cols(h)] = go
            scaled = go * jnp.exp(col[:, h : h + 1])
            msg_ref[p // 2, p % 2, 0:DH, :] = dot(q_ref[x, :, cols(h)], scaled, TN)
            msg_ref[p // 2, p % 2, DH:PR, :] = jnp.broadcast_to(row[h : h + 1, T - 1 : T], (PR - DH, DH))


def local_grads_kernel(valid, ld_ref, q_ref, k_ref, v_ref, s_ref, go_ref, gq_ref, gk_ref, gv_ref):
    for x in range(2):
        row, col, keep = sums(ld_ref[x])
        flag = valid[x].astype(F32)
        for h in range(H):
            p = x * H + h
            q, k, v = q_ref[x, :, cols(h)], k_ref[x, :, cols(h)], v_ref[x, :, cols(h)]
            go = go_ref[x, :, cols(h)]
            decay = jnp.exp(jnp.where(keep, col[:, h : h + 1] - row[h : h + 1, :], -jnp.inf)) * flag
            scores = dot(q, k, NT) * decay
            grad_scores = dot(go, v, NT) * decay
            gq = dot(grad_scores, k, NN) + jnp.exp(col[:, h : h + 1]) * dot(go, s_ref[p // 2, p % 2], NT)
            gq_ref[x, :, cols(h)] = gq.astype(BF16)
            gk_ref[x, :, cols(h)] = dot(grad_scores, q, TN)
            gv_ref[x, :, cols(h)] = dot(scores, go, TN)


def final_kernel(valid, ld_ref, k_ref, v_ref, gk_in, gv_in, s_ref, gk_ref, gv_ref):
    for x in range(2):
        row, col, _ = sums(ld_ref[x])
        flag = valid[x].astype(F32)
        for h in range(H):
            p = x * H + h
            k, v = k_ref[x, :, cols(h)], v_ref[x, :, cols(h)]
            to_end = jnp.exp(col[T - 1 : T, h : h + 1] - col[:, h : h + 1]) * flag
            state = s_ref[p // 2, p % 2]
            gk_ref[x, :, cols(h)] = (gk_in[x, :, cols(h)] * flag + to_end * dot(v, state, NT)).astype(BF16)
            gv_ref[x, :, cols(h)] = (gv_in[x, :, cols(h)] * flag + to_end * dot(k, state, NN)).astype(BF16)


ROWS = [[z * NE + e for e in range(NE)] for z in range(NZ)]
YS = [[half * NY + y for y in range(NY)] for half in range(2)]
SWAP = [(i, (i + NY) % (2 * NY)) for i in range(2 * NY)]


def to_rows(x):
    return lax.all_to_all(x, "tm", 0, 0, axis_index_groups=ROWS, tiled=True)


def over_y(x):
    return lax.all_to_all(x, "track", 0, 0, axis_index_groups=YS, tiled=True)


def swap(x):
    return lax.ppermute(x, "track", SWAP)


def z_shift(x, step):
    pairs = [
        (z * NE + e, (z + step) * NE + e) for z in range(NZ) for e in range(NE) if 0 <= z + step < NZ
    ]
    return lax.ppermute(x, "tm", pairs)


def scan_states(message, at, initial, back):
    row = to_rows(message)
    total = vmem_call(functools.partial(row_total_kernel, back), shape(2, PR, DH), 0, 1)(row)
    sign = -1 if back else 1
    far = [z_shift(total, sign * step) for step in (3, 2, 1)]
    starts = vmem_call(
        functools.partial(row_starts_kernel, back), shape(NE, 2, DH, DH), 1, 4 if back else 5
    )(at, *(() if back else (initial,)), row, *far)
    return to_rows(starts)


def per_device(q, k, v, log_decay, valid_length, initial, cross_q, cross_k, grad_out):
    tm, track = lax.axis_index("tm"), lax.axis_index("track")
    half, first = track // NY, tm * T
    alive = (first < valid_length).astype(jnp.int32)
    own_valid = lax.dynamic_slice(alive, (2 * track,), (2,))
    half_valid = lax.dynamic_slice(alive, (8 * half,), (8,))
    other_valid = lax.dynamic_slice(alive, (8 * (1 - half),), (8,))
    lanes = jnp.repeat(jnp.concatenate([half_valid, other_valid]).astype(F32), 16)
    vi = jnp.broadcast_to(lanes[None, :], (8, 256))
    at = jnp.stack([tm % NE, tm // NE]).astype(jnp.int32)

    def rows_of(x):
        return x.reshape(2, NY, RY, H * DH).transpose(1, 0, 2, 3)

    message = vmem_call(block_state_kernel, shape(NE, 2, PR, DH), 1, 3)(own_valid, log_decay, k, v)
    cq, go_in = over_y(rows_of(cross_q)), over_y(rows_of(grad_out))
    ck = over_y(rows_of(cross_k))
    cqx, gox = swap(cq), swap(go_in)

    state = scan_states(message, at, initial, False)
    out, normed = vmem_call(
        outputs_kernel, (shape(2, T, H * DH), shape(NY, 2, RY, H * DH, dtype=BF16)), 1, 5
    )(own_valid, log_decay, q, k, v, state)
    n_rows = RY // 16 * H
    tops, totals = vmem_call(stats_kernel, (shape(n_rows, 256), shape(n_rows, 256)), 1, 3)(half_valid, ck, cq, cqx)
    topsx, totalsx = swap(tops), swap(totals)
    nx = over_y(normed)
    quarter = shape(NY, 2, RY, H * DH, dtype=BF16)
    cross_in = (half_valid, ck, cq, cqx, nx, go_in, gox, tops, totals, topsx, totalsx, vi)
    gn, rd = vmem_call(mix_kernel, (quarter, shape(n_rows, 256)), 1, 11)(*cross_in)
    gn_t = over_y(gn)
    rdx = swap(rd)
    gk_x, gq_own, gq_other = vmem_call(
        cross_grads_kernel, (quarter, shape(NY, 2, RY, H * DH), quarter), 1, 13
    )(*cross_in, rd, rdx)
    gq_back = swap(gq_other)

    go, back_message = vmem_call(grad_outputs_kernel, (shape(2, T, H * DH), shape(NE, 2, PR, DH)), 1, 4)(
        own_valid, log_decay, q, out, gn_t
    )
    state_grad = scan_states(back_message, at, None, True)
    whole = shape(2, T, H * DH)
    half_whole = shape(2, T, H * DH, dtype=BF16)
    grad_q, gk_local, gv_local = vmem_call(local_grads_kernel, (half_whole, whole, whole), 1, 6)(
        own_valid, log_decay, q, k, v, state, go
    )
    grad_k, grad_v = vmem_call(final_kernel, (half_whole, half_whole), 1, 6)(
        own_valid, log_decay, k, v, gk_local, gv_local, state_grad
    )
    joined = vmem_call(join_kernel, shape(NY, 2, 2, RY, H * DH, dtype=BF16), 0, 3)(gq_own, gq_back, gk_x)
    joined = over_y(joined)
    grad_cross = joined.transpose(1, 2, 0, 3, 4).reshape(2, 2, T, H * DH)
    return grad_q, grad_k, grad_v, grad_cross[0], grad_cross[1]


def solution(mesh):
    rows = P("track", "tm", None)
    return jax.shard_map(
        per_device,
        mesh=mesh,
        in_specs=(rows, rows, rows, P("track", None, "tm"), P(), P("track", None, None, None), rows, rows, rows),
        out_specs=(rows,) * 5,
        check_vma=False,
    )
```

time: 611 us -> 252 us (0.41)
  waiting for transfers between devices: 277 us -> 97.9 us
  other arithmetic: 99.5 us -> 0.15 us
  blocking collectives: 90.3 us -> 11 us
  starting transfers between devices: 31.8 us -> 85.8 us
  matrix products: 38.3 us -> 0 us
  Pallas kernels: 0 us -> 30.1 us
  local copies, waits for them, and re-layouts: 52.8 us -> 24.6 us
  between operations: 14.4 us -> 0.94 us
    all_gather x2 -> x0, waiting for transfers between devices: 208 us -> none  [prefix_2(): pieces = jax.tree.map(lambda part: lax.all_gather(part, axis), value)]
    select_n x93 -> x0, other arithmetic: 90.9 us -> none  [lap(): jnp.where(position < mine, new, old)]
    all_gather x1 -> x0, blocking collectives: 63.4 us -> none  [prefix_2(): pieces = jax.tree.map(lambda part: lax.all_gather(part, axis), value)]
    ppermute x0 -> x12, waiting for transfers between devices: none -> 59.9 us  [the longest x6 30.7 us: z_shift(): return lax.ppermute(x, 'tm', pairs)]
    dot_general x17 -> x0, matrix products: 38.3 us -> none  [the longest x1 3.55 us: per_device(): jnp.einsum('xnthd,xhncd->xnthc', grad_outputs, start_states, precision=HI...]
    all_to_all x6 -> x9, waiting for transfers between devices: 69 us -> 38 us  [the longest x4 33.4 us: to_rows(): return lax.all_to_all(x, 'tm', 0, 0, axis_index_groups=ROWS, tiled=True)]
    pallas_call x0 -> x13, Pallas kernels: none -> 30.1 us  [the longest x1 6.06 us: per_device(): vmem_call(local_grads_kernel, (half_whole, whole, whole), 1, 6)]
    all_to_all x6 -> x9, starting transfers between devices: 31.8 us -> 60.8 us  [the longest x4 39 us: to_rows(): return lax.all_to_all(x, 'tm', 0, 0, axis_index_groups=ROWS, tiled=True)]
  transfers between devices with their start and end apart: 8 -> 21, of which waited for: 7 -> 15; matrix products, arithmetic and copies ran while one was open for 7% -> 2% of each run, Pallas kernels for 0% -> 8%
where the time goes in v1:
time: 252 us; the launch traced here: 250 us
  waiting for transfers between devices  97.9 us (39%)
  starting transfers between devices  85.8 us (34%)
  Pallas kernels  30.1 us (12%)
  local copies, waits for them, and re-layouts  24.6 us (10%)
  blocking collectives  11 us (4%)
    all_to_all x4, starting transfers between devices, to_rows(): return lax.all_to_all(x, 'tm', 0, 0, axis_index_groups=ROWS, tiled=True)  39 us
    all_to_all x4, waiting for transfers between devices, to_rows(): return lax.all_to_all(x, 'tm', 0, 0, axis_index_groups=ROWS, tiled=True)  33.4 us
    ppermute x6, waiting for transfers between devices, z_shift(): return lax.ppermute(x, 'tm', pairs)  30.7 us
    ppermute x6, waiting for transfers between devices, swap(): return lax.ppermute(x, 'track', SWAP)  29.1 us
    all_to_all x5, starting transfers between devices, over_y(): return lax.all_to_all(x, 'track', 0, 0, axis_index_groups=YS, tiled=True)  21.8 us
    unnamed x62, local copies, waits for them, and re-layouts  16.9 us
    ppermute x6, starting transfers between devices, z_shift(): return lax.ppermute(x, 'tm', pairs)  13.6 us
    ppermute x6, starting transfers between devices, swap(): return lax.ppermute(x, 'track', SWAP)  11.4 us
  transfers between devices with their start and end apart: 21, of which 15 were waited for; matrix products, arithmetic and copies ran while one was open for 2% of the time, Pallas kernels for 8%

profile of v1, /device:TPU:1, one launch (start us, length us, event | category | flops | bytes accessed | tf_op | source)
XLA Modules:
  0.0 250.4 jit_solution(946523887934708583)
XLA Ops:
  2.6 5.0 %all-to-all-start.3 = ((bf16[4,2,32,1024]{3,2,1,0:T(8,128)(2,1)}), bf16[4,2,32,1024]{3,2,1,0:T(8,128)(2,1)S(1)}, u32[]{:S(2)}, u32[]{:S(2)}) async-start(bf16[4,2,32,1024]{3,2,1,0:T(8,128)(2,1)} %bitcast.15), calls=%async_computation.3 | async-start | bytes 1048576 | tf_op jit(solution)/shard_map/all_to_all | solution.py:298
  10.5 4.6 %all-to-all-done.3.q_ref = bf16[4,2,32,1024]{3,2,1,0:T(8,128)(2,1)S(1)} async-done(((bf16[4,2,32,1024]{3,2,1,0:T(8,128)(2,1)}), bf16[4,2,32,1024]{3,2,1,0:T(8,128)(2,1)S(1)}, u32[]{:S(2)}, u32[]{:S(2)}) %all-to-all-start.3) | async-done | bytes 524320 | tf_op jit(solution)/shard_map/all_to_all | solution.py:298
  16.0 7.2 %all-to-all-start = ((f32[8,2,136,128]{3,2,1,0:T(8,128)}), f32[8,2,136,128]{3,2,1,0:T(8,128)S(1)}, u32[]{:S(2)}, u32[]{:S(2)}) async-start(f32[8,2,136,128]{3,2,1,0:T(8,128)} %copy-done.10), calls=%async_computation | async-start | bytes 2228224 | tf_op jit(solution)/shard_map/all_to_all | solution.py:294
  24.0 15.0 %all-to-all-done.in_ref.refs_1_ = f32[8,2,136,128]{3,2,1,0:T(8,128)S(1)} async-done(((f32[8,2,136,128]{3,2,1,0:T(8,128)}), f32[8,2,136,128]{3,2,1,0:T(8,128)S(1)}, u32[]{:S(2)}, u32[]{:S(2)}) %all-to-all-start) | async-done | bytes 1114144 | tf_op jit(solution)/shard_map/all_to_all | solution.py:294
  39.0 4.1 %all-to-all-start.5 = ((bf16[4,2,32,1024]{3,2,1,0:T(8,128)(2,1)}), bf16[4,2,32,1024]{3,2,1,0:T(8,128)(2,1)}, u32[]{:S(2)}, u32[]{:S(2)}) async-start(bf16[4,2,32,1024]{3,2,1,0:T(8,128)(2,1)} %bitcast.14), calls=%async_computation.5 | async-start | bytes 1048576 | tf_op jit(solution)/shard_map/all_to_all | solution.py:298
  43.2 3.5 %collective-permute-start.2 = (f32[2,136,128]{2,1,0:T(8,128)S(1)}, f32[2,136,128]{2,1,0:T(8,128)S(1)}, u32[]{:S(2)}, u32[]{:S(2)}) collective-permute-start(f32[2,136,128]{2,1,0:T(8,128)S(1)} %shard_map.129), channel_id=1, source_target_pairs={{0,8},{1,9},{2,10},{3,11},{4,12},{5,13},{6,14},{7,15},{8,16},{9,17... | collective-permute-start | bytes 417800 | tf_op jit(solution)/shard_map/ppermute | solution.py:309
  46.8 4.9 %collective-permute-start.1 = (f32[2,136,128]{2,1,0:T(8,128)S(1)}, f32[2,136,128]{2,1,0:T(8,128)S(1)}, u32[]{:S(2)}, u32[]{:S(2)}) collective-permute-start(f32[2,136,128]{2,1,0:T(8,128)S(1)} %shard_map.129), channel_id=1, source_target_pairs={{0,16},{1,17},{2,18},{3,19},{4,20},{5,21},{6,22},{7,23},{8,24},{9,... | collective-permute-start | bytes 417800 | tf_op jit(solution)/shard_map/ppermute | solution.py:309
  53.7 2.8 %collective-permute-done.refs_2_ = f32[2,136,128]{2,1,0:T(8,128)S(1)} collective-permute-done((f32[2,136,128]{2,1,0:T(8,128)S(1)}, f32[2,136,128]{2,1,0:T(8,128)S(1)}, u32[]{:S(2)}, u32[]{:S(2)}) %collective-permute-start) | collective-permute-done | bytes 139296 | tf_op jit(solution)/shard_map/ppermute | solution.py:309
  60.8 5.6 %all-to-all-start.1 = ((f32[8,2,128,128]{3,2,1,0:T(8,128)}), f32[8,2,128,128]{3,2,1,0:T(8,128)S(1)}, u32[]{:S(2)}, u32[]{:S(2)}) async-start(f32[8,2,128,128]{3,2,1,0:T(8,128)} %copy-done.12), calls=%async_computation.1 | async-start | bytes 2097152 | tf_op jit(solution)/shard_map/all_to_all | solution.py:294
  67.3 14.3 %all-to-all-done.1.s_ref = f32[8,2,128,128]{3,2,1,0:T(8,128)S(1)} async-done(((f32[8,2,128,128]{3,2,1,0:T(8,128)}), f32[8,2,128,128]{3,2,1,0:T(8,128)S(1)}, u32[]{:S(2)}, u32[]{:S(2)}) %all-to-all-start.1) | async-done | bytes 1048608 | tf_op jit(solution)/shard_map/all_to_all | solution.py:294
  81.6 4.2 %all-to-all-start.2 = ((bf16[4,2,32,1024]{3,2,1,0:T(8,128)(2,1)}), bf16[4,2,32,1024]{3,2,1,0:T(8,128)(2,1)S(1)}, u32[]{:S(2)}, u32[]{:S(2)}) async-start(bf16[4,2,32,1024]{3,2,1,0:T(8,128)(2,1)} %bitcast.17), calls=%async_computation.2 | async-start | bytes 1048576 | tf_op jit(solution)/shard_map/all_to_all | solution.py:298
  85.8 4.2 %collective-permute-start.3 = (bf16[4,2,32,1024]{3,2,1,0:T(8,128)(2,1)S(1)}, bf16[4,2,32,1024]{3,2,1,0:T(8,128)(2,1)}, u32[]{:S(2)}, u32[]{:S(2)}) collective-permute-start(bf16[4,2,32,1024]{3,2,1,0:T(8,128)(2,1)S(1)} %copy-done.3), channel_id=1, source_target_pairs={{0,128},{32,160},{64,192},{96,224},{128,0},{160,32},{192,64},{224,... | collective-permute-start | bytes 1572872 | tf_op jit(solution)/shard_map/ppermute | solution.py:302
  92.2 2.8 %shard_map.131 = (f32[2,128,1024]{2,1,0:T(8,128)S(1)}, bf16[4,2,32,1024]{3,2,1,0:T(8,128)(2,1)S(1)}) custom-call(s32[2]{0:T(128)S(1)} %dynamic_slice.9.valid, f32[2,8,128]{2,1,0:T(8,128)S(1)} %copy-done.25, bf16[2,128,1024]{2,1,0:T(8,128)(2,1)S(1)} %copy-done.7, bf16[2,128,1024]{2,1,0:T(8,128)(2,1)S(1)} %copy-done, bf16[2,128,1024]{2,1,0:T(8,128)(2,1)S(1)} %copy-done.1, ...), custom_call_target="tpu_custom_call" | custom-call | tf_op jit(solution)/shard_map/pallas_call | solution.py:343
  96.8 4.2 %all-to-all-start.4 = ((bf16[4,2,32,1024]{3,2,1,0:T(8,128)(2,1)}), bf16[4,2,32,1024]{3,2,1,0:T(8,128)(2,1)}, u32[]{:S(2)}, u32[]{:S(2)}) async-start(bf16[4,2,32,1024]{3,2,1,0:T(8,128)(2,1)} %copy-done.24), calls=%async_computation.4 | async-start | bytes 1048576 | tf_op jit(solution)/shard_map/all_to_all | solution.py:298
  104.1 4.3 %collective-permute-start.5 = (f32[16,256]{1,0:T(8,128)S(1)}, f32[16,256]{1,0:T(8,128)S(1)}, u32[]{:S(2)}, u32[]{:S(2)}) collective-permute-start(f32[16,256]{1,0:T(8,128)S(1)} %get-tuple-element.23.max_ref), channel_id=1, source_target_pairs={{0,128},{32,160},{64,192},{96,224},{128,0},{160,32},{192,64},{224,... | collective-permute-start | bytes 49160 | tf_op jit(solution)/shard_map/ppermute | solution.py:302
  109.8 3.7 %collective-permute-done.4.gx_ref = bf16[4,2,32,1024]{3,2,1,0:T(8,128)(2,1)} collective-permute-done((bf16[4,2,32,1024]{3,2,1,0:T(8,128)(2,1)}, bf16[4,2,32,1024]{3,2,1,0:T(8,128)(2,1)}, u32[]{:S(2)}, u32[]{:S(2)}) %collective-permute-start.4) | collective-permute-done | bytes 524320 | tf_op jit(solution)/shard_map/ppermute | solution.py:302
  115.5 4.8 %shard_map.133 = (bf16[4,2,32,1024]{3,2,1,0:T(8,128)(2,1)S(1)}, f32[16,256]{1,0:T(8,128)S(1)}) custom-call(s32[8]{0:T(128)S(1)} %get-tuple-element.40.key_valid, bf16[4,2,32,1024]{3,2,1,0:T(8,128)(2,1)S(1)} %all-to-all-done.2.k_ref, bf16[4,2,32,1024]{3,2,1,0:T(8,128)(2,1)S(1)} %copy-done.3, bf16[4,2,32,1024]{3,2,1,0:T(8,128)(2,1)} %collective-permute-done.3.qx_ref, ...), custom_call_target="tpu_custom_call" | custom-call | tf_op jit(solution)/shard_map/pallas_call | solution.py:352
  120.3 11.0 %all_to_all.50.gn_ref = bf16[4,2,32,1024]{3,2,1,0:T(8,128)(2,1)S(1)} all-to-all(bf16[4,2,32,1024]{3,2,1,0:T(8,128)(2,1)S(1)} %get-tuple-element.25), channel_id=1, replica_groups={{0,32,64,96},{128,160,192,224},{1,33,65,97},{129,161,193,225},{2,34,66,..., dimensions={0} | all-to-all | bytes 1048576 | tf_op jit(solution)/shard_map/all_to_all | solution.py:298
  131.3 2.8 %shard_map.134 = (f32[2,128,1024]{2,1,0:T(8,128)S(1)}, f32[8,2,136,128]{3,2,1,0:T(8,128)S(1)}) custom-call(s32[2]{0:T(128)S(1)} %dynamic_slice.9.valid, f32[2,8,128]{2,1,0:T(8,128)S(1)} %copy-done.25, bf16[2,128,1024]{2,1,0:T(8,128)(2,1)S(1)} %copy-done.8, f32[2,128,1024]{2,1,0:T(8,128)S(1)} %copy-done.20, bf16[4,2,32,1024]{3,2,1,0:T(8,128)(2,1)S(1)} %all_to_all.50.gn_ref), custom_call_target="tpu_custom_call" | custom-call | tf_op jit(solution)/shard_map/pallas_call | solution.py:360
  136.2 20.4 %all-to-all-start.7 = ((f32[8,2,136,128]{3,2,1,0:T(8,128)}), f32[8,2,136,128]{3,2,1,0:T(8,128)S(1)}, u32[]{:S(2)}, u32[]{:S(2)}) async-start(f32[8,2,136,128]{3,2,1,0:T(8,128)} %copy-done.14), calls=%async_computation.7 | async-start | bytes 2228224 | tf_op jit(solution)/shard_map/all_to_all | solution.py:294
  156.9 6.3 %collective-permute-done.10.rdx_ref = f32[16,256]{1,0:T(8,128)S(1)} collective-permute-done((f32[16,256]{1,0:T(8,128)S(1)}, f32[16,256]{1,0:T(8,128)S(1)}, u32[]{:S(2)}, u32[]{:S(2)}) %collective-permute-start.10) | collective-permute-done | bytes 16416 | tf_op jit(solution)/shard_map/ppermute | solution.py:302
  165.2 5.2 %shard_map.139 = (bf16[4,2,32,1024]{3,2,1,0:T(8,128)(2,1)S(1)}, f32[4,2,32,1024]{3,2,1,0:T(8,128)S(1)}, bf16[4,2,32,1024]{3,2,1,0:T(8,128)(2,1)S(1)}) custom-call(s32[8]{0:T(128)S(1)} %get-tuple-element.40.key_valid, bf16[4,2,32,1024]{3,2,1,0:T(8,128)(2,1)S(1)} %copy-done.6, bf16[4,2,32,1024]{3,2,1,0:T(8,128)(2,1)S(1)} %copy-done.4, ...), custom_call_target="tpu_custom_call" | custom-call | tf_op jit(solution)/shard_map/pallas_call | solution.py:355
  170.7 16.1 %collective-permute-done.11.gqx_ref = bf16[4,2,32,1024]{3,2,1,0:T(8,128)(2,1)S(1)} collective-permute-done((bf16[4,2,32,1024]{3,2,1,0:T(8,128)(2,1)S(1)}, bf16[4,2,32,1024]{3,2,1,0:T(8,128)(2,1)S(1)}, u32[]{:S(2)}, u32[]{:S(2)}) %collective-permute-start.11) | collective-permute-done | bytes 524320 | tf_op jit(solution)/shard_map/ppermute | solution.py:302
  187.9 4.2 %all-to-all-start.9 = ((bf16[4,2,2,32,1024]{4,3,2,1,0:T(8,128)(2,1)}), bf16[4,2,2,32,1024]{4,3,2,1,0:T(8,128)(2,1)}, u32[]{:S(2)}, u32[]{:S(2)}) async-start(bf16[4,2,2,32,1024]{4,3,2,1,0:T(8,128)(2,1)} %copy-done.11), calls=%async_computation.9 | async-start | bytes 2097152 | tf_op jit(solution)/shard_map/all_to_all | solution.py:298
  196.2 9.1 %collective-permute-done.9.refs_3_ = f32[2,136,128]{2,1,0:T(8,128)S(1)} collective-permute-done((f32[2,136,128]{2,1,0:T(8,128)S(1)}, f32[2,136,128]{2,1,0:T(8,128)S(1)}, u32[]{:S(2)}, u32[]{:S(2)}) %collective-permute-start.9) | collective-permute-done | bytes 139296 | tf_op jit(solution)/shard_map/ppermute | solution.py:309
  205.3 8.1 %collective-permute-done.8.refs_2_ = f32[2,136,128]{2,1,0:T(8,128)S(1)} collective-permute-done((f32[2,136,128]{2,1,0:T(8,128)S(1)}, f32[2,136,128]{2,1,0:T(8,128)S(1)}, u32[]{:S(2)}, u32[]{:S(2)}) %collective-permute-start.8) | collective-permute-done | bytes 139296 | tf_op jit(solution)/shard_map/ppermute | solution.py:309
  213.3 10.1 %collective-permute-done.7.refs_1_ = f32[2,136,128]{2,1,0:T(8,128)S(1)} collective-permute-done((f32[2,136,128]{2,1,0:T(8,128)S(1)}, f32[2,136,128]{2,1,0:T(8,128)S(1)}, u32[]{:S(2)}, u32[]{:S(2)}) %collective-permute-start.7) | collective-permute-done | bytes 139296 | tf_op jit(solution)/shard_map/ppermute | solution.py:309
  225.1 5.7 %all-to-all-start.8 = ((f32[8,2,128,128]{3,2,1,0:T(8,128)}), f32[8,2,128,128]{3,2,1,0:T(8,128)}, u32[]{:S(2)}, u32[]{:S(2)}) async-start(f32[8,2,128,128]{3,2,1,0:T(8,128)} %copy-done.13), calls=%async_computation.8 | async-start | bytes 2097152 | tf_op jit(solution)/shard_map/all_to_all | solution.py:294
  232.1 6.1 %shard_map.135 = (bf16[2,128,1024]{2,1,0:T(8,128)(2,1)}, f32[2,128,1024]{2,1,0:T(8,128)S(1)}, f32[2,128,1024]{2,1,0:T(8,128)S(1)}) custom-call(s32[2]{0:T(128)S(1)} %dynamic_slice.9.valid, f32[2,8,128]{2,1,0:T(8,128)S(1)} %copy-done.25, bf16[2,128,1024]{2,1,0:T(8,128)(2,1)S(1)} %copy-done.9, bf16[2,128,1024]{2,1,0:T(8,128)(2,1)S(1)} %copy-done, ...), custom_call_target="tpu_custom_call" | custom-call | tf_op jit(solution)/shard_map/pallas_call | solution.py:366
  238.1 2.0 fusion
  241.9 4.2 %all-to-all-done.8.s_ref = f32[8,2,128,128]{3,2,1,0:T(8,128)} async-done(((f32[8,2,128,128]{3,2,1,0:T(8,128)}), f32[8,2,128,128]{3,2,1,0:T(8,128)}, u32[]{:S(2)}, u32[]{:S(2)}) %all-to-all-start.8) | async-done | bytes 1048608 | tf_op jit(solution)/shard_map/all_to_all | solution.py:294
  247.3 3.1 %shard_map.138 = (bf16[2,128,1024]{2,1,0:T(8,128)(2,1)}, bf16[2,128,1024]{2,1,0:T(8,128)(2,1)}) custom-call(s32[2]{0:T(128)S(1)} %dynamic_slice.9.valid, f32[2,8,128]{2,1,0:T(8,128)S(1)} %copy-done.25, bf16[2,128,1024]{2,1,0:T(8,128)(2,1)S(1)} %copy-done, bf16[2,128,1024]{2,1,0:T(8,128)(2,1)S(1)} %copy-done.1, f32[2,128,1024]{2,1,0:T(8,128)S(1)} %copy-done.16, ...), custom_call_target="tpu_custom_call" | custom-call | tf_op jit(solution)/shard_map/pallas_call | solution.py:369
  (100 shorter events, 39.7 us)
Async XLA Ops:
  0.6 7.0 %copy-start.30 = (s32[16]{0:T(128)S(1)}, s32[16]{0:T(128)}, u32[]{:S(2)}) copy-start(s32[16]{0:T(128)} %param.13) | copy-start | bytes 196
  0.6 7.1 %copy-start.25 = (f32[2,8,128]{2,1,0:T(8,128)S(1)}, f32[2,8,128]{2,1,0:T(8,128)}, u32[]{:S(2)}) copy-start(f32[2,8,128]{2,1,0:T(8,128)} %ld_ref.9) | copy-start | bytes 24580
  0.7 7.1 %copy-start.1 = (bf16[2,128,1024]{2,1,0:T(8,128)(2,1)S(1)}, bf16[2,128,1024]{2,1,0:T(8,128)(2,1)}, u32[]{:S(2)}) copy-start(bf16[2,128,1024]{2,1,0:T(8,128)(2,1)} %v_ref.7) | copy-start | bytes 1572868
  0.7 7.1 %copy-start = (bf16[2,128,1024]{2,1,0:T(8,128)(2,1)S(1)}, bf16[2,128,1024]{2,1,0:T(8,128)(2,1)}, u32[]{:S(2)}) copy-start(bf16[2,128,1024]{2,1,0:T(8,128)(2,1)} %k_ref.7) | copy-start | bytes 1572868
  2.6 12.6 %all-to-all-start.3 = ((bf16[4,2,32,1024]{3,2,1,0:T(8,128)(2,1)}), bf16[4,2,32,1024]{3,2,1,0:T(8,128)(2,1)S(1)}, u32[]{:S(2)}, u32[]{:S(2)}) async-start(bf16[4,2,32,1024]{3,2,1,0:T(8,128)(2,1)} %bitcast.15), calls=%async_computation.3 | async-start | bytes 1048576 | tf_op jit(solution)/shard_map/all_to_all | solution.py:298
  10.5 12.6 %copy-start.28 = (bf16[2,128,1024]{2,1,0:T(8,128)(2,1)S(1)}, bf16[2,128,1024]{2,1,0:T(8,128)(2,1)}, u32[]{:S(2)}) copy-start(bf16[2,128,1024]{2,1,0:T(8,128)(2,1)} %param.17) | copy-start | bytes 1572868
  16.0 23.0 %all-to-all-start = ((f32[8,2,136,128]{3,2,1,0:T(8,128)}), f32[8,2,136,128]{3,2,1,0:T(8,128)S(1)}, u32[]{:S(2)}, u32[]{:S(2)}) async-start(f32[8,2,136,128]{3,2,1,0:T(8,128)} %copy-done.10), calls=%async_computation | async-start | bytes 2228224 | tf_op jit(solution)/shard_map/all_to_all | solution.py:294
  39.0 21.9 %all-to-all-start.5 = ((bf16[4,2,32,1024]{3,2,1,0:T(8,128)(2,1)}), bf16[4,2,32,1024]{3,2,1,0:T(8,128)(2,1)}, u32[]{:S(2)}, u32[]{:S(2)}) async-start(bf16[4,2,32,1024]{3,2,1,0:T(8,128)(2,1)} %bitcast.14), calls=%async_computation.5 | async-start | bytes 1048576 | tf_op jit(solution)/shard_map/all_to_all | solution.py:298
  43.2 9.9 %collective-permute-start.2 = (f32[2,136,128]{2,1,0:T(8,128)S(1)}, f32[2,136,128]{2,1,0:T(8,128)S(1)}, u32[]{:S(2)}, u32[]{:S(2)}) collective-permute-start(f32[2,136,128]{2,1,0:T(8,128)S(1)} %shard_map.129), channel_id=1, source_target_pairs={{0,8},{1,9},{2,10},{3,11},{4,12},{5,13},{6,14},{7,15},{8,16},{9,17... | collective-permute-start | bytes 417800 | tf_op jit(solution)/shard_map/ppermute | solution.py:309
  46.8 6.9 %collective-permute-start.1 = (f32[2,136,128]{2,1,0:T(8,128)S(1)}, f32[2,136,128]{2,1,0:T(8,128)S(1)}, u32[]{:S(2)}, u32[]{:S(2)}) collective-permute-start(f32[2,136,128]{2,1,0:T(8,128)S(1)} %shard_map.129), channel_id=1, source_target_pairs={{0,16},{1,17},{2,18},{3,19},{4,20},{5,21},{6,22},{7,23},{8,24},{9,... | collective-permute-start | bytes 417800 | tf_op jit(solution)/shard_map/ppermute | solution.py:309
  51.7 4.9 %collective-permute-start = (f32[2,136,128]{2,1,0:T(8,128)S(1)}, f32[2,136,128]{2,1,0:T(8,128)S(1)}, u32[]{:S(2)}, u32[]{:S(2)}) collective-permute-start(f32[2,136,128]{2,1,0:T(8,128)S(1)} %shard_map.129), channel_id=1, source_target_pairs={{0,24},{1,25},{2,26},{3,27},{4,28},{5,29},{6,30},{7,31},{32,56},{3... | collective-permute-start | bytes 417800 | tf_op jit(solution)/shard_map/ppermute | solution.py:309
  60.8 5.6 %copy-start.29 = (bf16[2,128,1024]{2,1,0:T(8,128)(2,1)S(1)}, bf16[2,128,1024]{2,1,0:T(8,128)(2,1)}, u32[]{:S(2)}) copy-start(bf16[2,128,1024]{2,1,0:T(8,128)(2,1)} %param.16) | copy-start | bytes 1572868
  60.8 20.7 %all-to-all-start.1 = ((f32[8,2,128,128]{3,2,1,0:T(8,128)}), f32[8,2,128,128]{3,2,1,0:T(8,128)S(1)}, u32[]{:S(2)}, u32[]{:S(2)}) async-start(f32[8,2,128,128]{3,2,1,0:T(8,128)} %copy-done.12), calls=%async_computation.1 | async-start | bytes 2097152 | tf_op jit(solution)/shard_map/all_to_all | solution.py:294
  66.5 19.3 %copy-start.3 = (bf16[4,2,32,1024]{3,2,1,0:T(8,128)(2,1)S(1)}, bf16[4,2,32,1024]{3,2,1,0:T(8,128)(2,1)}, u32[]{:S(2)}) copy-start(bf16[4,2,32,1024]{3,2,1,0:T(8,128)(2,1)} %copy-done.2) | copy-start | bytes 1572868
  81.6 15.2 %all-to-all-start.2 = ((bf16[4,2,32,1024]{3,2,1,0:T(8,128)(2,1)}), bf16[4,2,32,1024]{3,2,1,0:T(8,128)(2,1)S(1)}, u32[]{:S(2)}, u32[]{:S(2)}) async-start(bf16[4,2,32,1024]{3,2,1,0:T(8,128)(2,1)} %bitcast.17), calls=%async_computation.2 | async-start | bytes 1048576 | tf_op jit(solution)/shard_map/all_to_all | solution.py:298
  85.8 16.4 %collective-permute-start.3 = (bf16[4,2,32,1024]{3,2,1,0:T(8,128)(2,1)S(1)}, bf16[4,2,32,1024]{3,2,1,0:T(8,128)(2,1)}, u32[]{:S(2)}, u32[]{:S(2)}) collective-permute-start(bf16[4,2,32,1024]{3,2,1,0:T(8,128)(2,1)S(1)} %copy-done.3), channel_id=1, source_target_pairs={{0,128},{32,160},{64,192},{96,224},{128,0},{160,32},{192,64},{224,... | collective-permute-start | bytes 1572872 | tf_op jit(solution)/shard_map/ppermute | solution.py:302
  90.0 23.5 %collective-permute-start.4 = (bf16[4,2,32,1024]{3,2,1,0:T(8,128)(2,1)}, bf16[4,2,32,1024]{3,2,1,0:T(8,128)(2,1)}, u32[]{:S(2)}, u32[]{:S(2)}) collective-permute-start(bf16[4,2,32,1024]{3,2,1,0:T(8,128)(2,1)} %all-to-all-done.5.g_ref), channel_id=1, source_target_pairs={{0,128},{32,160},{64,192},{96,224},{128,0},{160,32},{192,64},{224,... | collective-permute-start | bytes 1572872 | tf_op jit(solution)/shard_map/ppermute | solution.py:302
  96.8 18.7 %copy-start.5 = (bf16[4,2,32,1024]{3,2,1,0:T(8,128)(2,1)}, bf16[4,2,32,1024]{3,2,1,0:T(8,128)(2,1)S(1)}, u32[]{:S(2)}) copy-start(bf16[4,2,32,1024]{3,2,1,0:T(8,128)(2,1)S(1)} %all-to-all-done.2.k_ref) | copy-start | bytes 1572868
  96.8 18.7 %all-to-all-start.4 = ((bf16[4,2,32,1024]{3,2,1,0:T(8,128)(2,1)}), bf16[4,2,32,1024]{3,2,1,0:T(8,128)(2,1)}, u32[]{:S(2)}, u32[]{:S(2)}) async-start(bf16[4,2,32,1024]{3,2,1,0:T(8,128)(2,1)} %copy-done.24), calls=%async_computation.4 | async-start | bytes 1048576 | tf_op jit(solution)/shard_map/all_to_all | solution.py:298
  104.1 9.7 %collective-permute-start.5 = (f32[16,256]{1,0:T(8,128)S(1)}, f32[16,256]{1,0:T(8,128)S(1)}, u32[]{:S(2)}, u32[]{:S(2)}) collective-permute-start(f32[16,256]{1,0:T(8,128)S(1)} %get-tuple-element.23.max_ref), channel_id=1, source_target_pairs={{0,128},{32,160},{64,192},{96,224},{128,0},{160,32},{192,64},{224,... | collective-permute-start | bytes 49160 | tf_op jit(solution)/shard_map/ppermute | solution.py:302
  108.4 7.0 %collective-permute-start.6 = (f32[16,256]{1,0:T(8,128)S(1)}, f32[16,256]{1,0:T(8,128)S(1)}, u32[]{:S(2)}, u32[]{:S(2)}) collective-permute-start(f32[16,256]{1,0:T(8,128)S(1)} %get-tuple-element.24.sum_ref), channel_id=1, source_target_pairs={{0,128},{32,160},{64,192},{96,224},{128,0},{160,32},{192,64},{224,... | collective-permute-start | bytes 49160 | tf_op jit(solution)/shard_map/ppermute | solution.py:302
  115.5 15.8 %copy-start.20 = (f32[2,128,1024]{2,1,0:T(8,128)S(1)}, f32[2,128,1024]{2,1,0:T(8,128)}, u32[]{:S(2)}) copy-start(f32[2,128,1024]{2,1,0:T(8,128)} %copy-done.19) | copy-start | bytes 3145732
  120.3 11.0 %copy-start.8 = (bf16[2,128,1024]{2,1,0:T(8,128)(2,1)S(1)}, bf16[2,128,1024]{2,1,0:T(8,128)(2,1)}, u32[]{:S(2)}) copy-start(bf16[2,128,1024]{2,1,0:T(8,128)(2,1)} %q_ref.5) | copy-start | bytes 1572868
  136.2 51.7 %all-to-all-start.7 = ((f32[8,2,136,128]{3,2,1,0:T(8,128)}), f32[8,2,136,128]{3,2,1,0:T(8,128)S(1)}, u32[]{:S(2)}, u32[]{:S(2)}) async-start(f32[8,2,136,128]{3,2,1,0:T(8,128)} %copy-done.14), calls=%async_computation.7 | async-start | bytes 2228224 | tf_op jit(solution)/shard_map/all_to_all | solution.py:294
  156.6 6.5 %collective-permute-start.10 = (f32[16,256]{1,0:T(8,128)S(1)}, f32[16,256]{1,0:T(8,128)S(1)}, u32[]{:S(2)}, u32[]{:S(2)}) collective-permute-start(f32[16,256]{1,0:T(8,128)S(1)} %get-tuple-element.33.rd_ref), channel_id=1, source_target_pairs={{0,128},{32,160},{64,192},{96,224},{128,0},{160,32},{192,64},{224,... | collective-permute-start | bytes 49160 | tf_op jit(solution)/shard_map/ppermute | solution.py:302
  170.4 16.4 %collective-permute-start.11 = (bf16[4,2,32,1024]{3,2,1,0:T(8,128)(2,1)S(1)}, bf16[4,2,32,1024]{3,2,1,0:T(8,128)(2,1)S(1)}, u32[]{:S(2)}, u32[]{:S(2)}) collective-permute-start(bf16[4,2,32,1024]{3,2,1,0:T(8,128)(2,1)S(1)} %get-tuple-element.35), channel_id=1, source_target_pairs={{0,128},{32,160},{64,192},{96,224},{128,0},{160,32},{192,64},{224,... | collective-permute-start | bytes 1572872 | tf_op jit(solution)/shard_map/ppermute | solution.py:302
  187.9 37.2 %all-to-all-start.9 = ((bf16[4,2,2,32,1024]{4,3,2,1,0:T(8,128)(2,1)}), bf16[4,2,2,32,1024]{4,3,2,1,0:T(8,128)(2,1)}, u32[]{:S(2)}, u32[]{:S(2)}) async-start(bf16[4,2,2,32,1024]{4,3,2,1,0:T(8,128)(2,1)} %copy-done.11), calls=%async_computation.9 | async-start | bytes 2097152 | tf_op jit(solution)/shard_map/all_to_all | solution.py:298
  192.3 13.0 %collective-permute-start.9 = (f32[2,136,128]{2,1,0:T(8,128)S(1)}, f32[2,136,128]{2,1,0:T(8,128)S(1)}, u32[]{:S(2)}, u32[]{:S(2)}) collective-permute-start(f32[2,136,128]{2,1,0:T(8,128)S(1)} %shard_map.136), channel_id=1, source_target_pairs={{8,0},{9,1},{10,2},{11,3},{12,4},{13,5},{14,6},{15,7},{16,8},{17,9... | collective-permute-start | bytes 417800 | tf_op jit(solution)/shard_map/ppermute | solution.py:309
  193.6 19.8 %collective-permute-start.8 = (f32[2,136,128]{2,1,0:T(8,128)S(1)}, f32[2,136,128]{2,1,0:T(8,128)S(1)}, u32[]{:S(2)}, u32[]{:S(2)}) collective-permute-start(f32[2,136,128]{2,1,0:T(8,128)S(1)} %shard_map.136), channel_id=1, source_target_pairs={{16,0},{17,1},{18,2},{19,3},{20,4},{21,5},{22,6},{23,7},{24,8},{25... | collective-permute-start | bytes 417800 | tf_op jit(solution)/shard_map/ppermute | solution.py:309
  194.9 28.6 %collective-permute-start.7 = (f32[2,136,128]{2,1,0:T(8,128)S(1)}, f32[2,136,128]{2,1,0:T(8,128)S(1)}, u32[]{:S(2)}, u32[]{:S(2)}) collective-permute-start(f32[2,136,128]{2,1,0:T(8,128)S(1)} %shard_map.136), channel_id=1, source_target_pairs={{24,0},{25,1},{26,2},{27,3},{28,4},{29,5},{30,6},{31,7},{56,32},{5... | collective-permute-start | bytes 417800 | tf_op jit(solution)/shard_map/ppermute | solution.py:309
  225.1 5.7 %copy-start.9 = (bf16[2,128,1024]{2,1,0:T(8,128)(2,1)S(1)}, bf16[2,128,1024]{2,1,0:T(8,128)(2,1)}, u32[]{:S(2)}) copy-start(bf16[2,128,1024]{2,1,0:T(8,128)(2,1)} %q_ref.5) | copy-start | bytes 1572868
  225.1 20.9 %all-to-all-start.8 = ((f32[8,2,128,128]{3,2,1,0:T(8,128)}), f32[8,2,128,128]{3,2,1,0:T(8,128)}, u32[]{:S(2)}, u32[]{:S(2)}) async-start(f32[8,2,128,128]{3,2,1,0:T(8,128)} %copy-done.13), calls=%async_computation.8 | async-start | bytes 2097152 | tf_op jit(solution)/shard_map/all_to_all | solution.py:294
  (20 other events, 27.7 us)

commit v2 on v1

v2 whole, which is shorter than its diff:
```python
import functools

import jax
import jax.numpy as jnp
from jax import lax
from jax.experimental import pallas as pl
from jax.experimental.pallas import tpu as pltpu
from jax.sharding import PartitionSpec as P

F32, BF16 = jnp.float32, jnp.bfloat16
EPSILON = 1e-06
NEG = -1e30
H, DH = 8, 128
T = 128
NY, NX, NZ = 4, 4, 4
RY = T // NY
PR = DH + 8
PZ = DH + 16
VMEM_LIMIT = 48 * 1024 * 1024

NN = ((1,), (0,))
NT = ((1,), (1,))
TN = ((0,), (0,))


def parts(x):
    if x.dtype == BF16:
        return [x]
    hi = x.astype(BF16)
    return [hi, (x - hi.astype(F32)).astype(BF16)]


def dot(a, b, dims):
    pa, pb = parts(a), parts(b)
    if len(pa) == 2 and len(pb) == 2:
        left, right = [pa[0], pa[0], pa[1]], [pb[0], pb[1], pb[0]]
    else:
        n = max(len(pa), len(pb))
        left = pa * (n // len(pa))
        right = pb * (n // len(pb))
    if len(left) > 1:
        left = jnp.concatenate(left, axis=dims[0][0])
        right = jnp.concatenate(right, axis=dims[1][0])
    else:
        left, right = left[0], right[0]
    return lax.dot_general(left, right, (dims, ((), ())), preferred_element_type=F32)


def sums(ld):
    r = lax.broadcasted_iota(jnp.int32, (T, T), 0)
    c = lax.broadcasted_iota(jnp.int32, (T, T), 1)
    upper = (r <= c).astype(F32)
    lower = (r >= c).astype(F32)
    row = lax.dot_general(
        ld, upper, (NN, ((), ())), precision=lax.Precision.HIGHEST, preferred_element_type=F32
    )
    col = lax.dot_general(
        lower, ld, (NT, ((), ())), precision=lax.Precision.HIGHEST, preferred_element_type=F32
    )
    return row, col, r >= c


def vmem_call(body, out_shape, n_smem, n_in, scratch=(), after=()):
    n = n_smem + n_in

    def ordered(*refs):
        body(*refs[:n], *refs[n + len(after) :])

    call = pl.pallas_call(
        ordered,
        out_shape=out_shape,
        in_specs=[pl.BlockSpec(memory_space=pltpu.SMEM)] * n_smem
        + [pl.BlockSpec(memory_space=pltpu.VMEM)] * n_in
        + [pl.BlockSpec(memory_space=pl.ANY)] * len(after),
        out_specs=jax.tree.map(lambda _: pl.BlockSpec(memory_space=pltpu.VMEM), out_shape),
        scratch_shapes=scratch,
        compiler_params=pltpu.CompilerParams(vmem_limit_bytes=VMEM_LIMIT),
    )
    return lambda *args: call(*args, *after)


def shape(*dims, dtype=F32):
    return jax.ShapeDtypeStruct(dims, dtype)


def cols(h):
    return slice(h * DH, (h + 1) * DH)


def store_message(ref, h, state, total):
    ref[h, 0:DH, :] = state
    ref[h, DH:PR, :] = jnp.broadcast_to(total, (PR - DH, DH))


def pack_kernel(*refs):
    *ins, out_ref = refs
    for i, one in enumerate(ins):
        for y in range(NY):
            out_ref[y, i] = one[:, y * RY : (y + 1) * RY, :]


def pack(*arrays, after=()):
    n = len(arrays)
    return vmem_call(pack_kernel, shape(NY, n, 2, RY, H * DH, dtype=BF16), 0, n, after=after)(*arrays)


def block_state_kernel(at, valid, ld_ref, k_ref, v_ref, keep_ref, send_ref):
    for i, out_ref in enumerate((keep_ref, send_ref)):
        x = at[0] if i == 0 else 1 - at[0]
        row, col, _ = sums(ld_ref[x])
        for h in range(H):
            scaled = v_ref[x, :, cols(h)].astype(F32) * jnp.exp(col[T - 1 : T, h : h + 1] - col[:, h : h + 1])
            state = dot(k_ref[x, :, cols(h)], scaled, TN)
            store_message(out_ref, h, state * valid[x].astype(F32), row[h : h + 1, T - 1 : T])


def chip_total_kernel(back, at, mine_ref, theirs_ref, *out_refs):
    first = at[0] == (1 if back else 0)
    for q, out_ref in enumerate(out_refs):
        for i in range(2):
            h = 2 * lax.rem(at[1] + q, NX) + i
            mine, theirs = mine_ref[h, DH : DH + 1, :], theirs_ref[h, DH : DH + 1, :]
            a = jnp.where(first, jnp.exp(theirs), 1.0)
            b = jnp.where(first, 1.0, jnp.exp(mine))
            store_message(out_ref, i, a * mine_ref[h, 0:DH, :] + b * theirs_ref[h, 0:DH, :], mine + theirs)


def row_total_kernel(back, at, *refs):
    *in_refs, row_ref, out_ref = refs
    for q, one in enumerate(in_refs):
        row_ref[lax.rem(at[1] - q + NX, NX)] = one[...]
    for p in range(2):
        state, total = None, None
        for j in range(NX - 1, -1, -1) if back else range(NX):
            ld = row_ref[j, p, DH : DH + 1, :]
            if state is None:
                state, total = row_ref[j, p, 0:DH, :], ld
            else:
                state = jnp.exp(ld) * state + row_ref[j, p, 0:DH, :]
                total = total + ld
        high = total.astype(BF16).astype(F32)
        middle = (total - high).astype(BF16).astype(F32)
        r = lax.broadcasted_iota(jnp.int32, (PZ - DH, DH), 0)
        pieces = jnp.where(r == 0, high, jnp.where(r == 1, middle, jnp.where(r == 2, total - high - middle, 0.0)))
        out_ref[p] = jnp.concatenate([state, pieces], axis=0).astype(BF16)


def row_starts_kernel(back, at, *refs):
    if back:
        row_ref, far3, far2, far1, *out_refs, starts = refs
    else:
        init_ref, row_ref, far3, far2, far1, *out_refs, starts = refs
    for p in range(2):
        if back:
            state = jnp.zeros((DH, DH), F32)
        else:
            state = init_ref[at[0], 2 * at[1] + p].astype(F32)
        for far in (far3, far2, far1):
            one = far[p].astype(F32)
            state = jnp.exp(jnp.sum(one[DH:PZ], axis=0, keepdims=True)) * state + one[0:DH]
        for j in range(NX - 1, -1, -1) if back else range(NX):
            starts[j, p] = state
            state = jnp.exp(row_ref[j, p, DH : DH + 1, :]) * state + row_ref[j, p, 0:DH, :]
    for q, out_ref in enumerate(out_refs):
        out_ref[...] = starts[lax.rem(at[1] + q, NX)]


def core_starts_kernel(back, at, *refs):
    *in_refs, mine_ref, theirs_ref, keep_ref, send_ref = refs
    first = at[0] == (1 if back else 0)
    on, off = jnp.where(first, 1.0, 0.0), jnp.where(first, 0.0, 1.0)
    for q, one in enumerate(in_refs):
        for i in range(2):
            h = 2 * lax.rem(at[1] - q + NX, NX) + i
            state = one[i]
            mine, theirs = mine_ref[h, DH : DH + 1, :], theirs_ref[h, DH : DH + 1, :]
            keep_ref[h] = jnp.where(first, 1.0, jnp.exp(theirs)) * state + off * theirs_ref[h, 0:DH, :]
            send_ref[h] = jnp.where(first, jnp.exp(mine), 1.0) * state + on * mine_ref[h, 0:DH, :]


def outputs_kernel(at, valid, ld_ref, q_ref, k_ref, v_ref, *refs):
    *s_refs, out_ref, normed_ref = refs
    for i, s_ref in enumerate(s_refs):
        x = at[0] if i == 0 else 1 - at[0]
        row, col, keep = sums(ld_ref[x])
        flag = valid[x].astype(F32)
        for h in range(H):
            q, k, v = q_ref[x, :, cols(h)], k_ref[x, :, cols(h)], v_ref[x, :, cols(h)]
            decay = jnp.exp(jnp.where(keep, col[:, h : h + 1] - row[h : h + 1, :], -jnp.inf))
            scores = dot(q, k, NT) * (decay * flag)
            out = dot(scores, v, NN) + jnp.exp(col[:, h : h + 1]) * dot(q, s_ref[h], NN)
            inverse = 1.0 / jnp.sqrt(jnp.mean(out * out, axis=-1, keepdims=True) + EPSILON)
            out_ref[x, :, cols(h)] = out
            normed = (out * (inverse * flag)).astype(BF16)
            for y in range(NY):
                normed_ref[y, 0, x, :, cols(h)] = normed[y * RY : (y + 1) * RY, :]


def same_time():
    t = lax.broadcasted_iota(jnp.int32, (16, 256), 0)
    lane = lax.broadcasted_iota(jnp.int32, (16, 256), 1)
    return (lane & 15) == t


def take(ref, g, h, i=0):
    part = ref[:, i, :, g * 16 : (g + 1) * 16, cols(h)]
    return part.reshape(128, DH)


def queries_of(qqk_ref, g, h):
    return jnp.concatenate([take(qqk_ref, g, h, 0), take(qqk_ref, g, h, 1)], axis=0)


def grads_of(g_ref, gx_ref, g, h):
    return jnp.concatenate([take(g_ref, g, h), take(gx_ref, g, h)], axis=0)


def scaled_logits(key_valid, keys, queries):
    logits = (dot(keys, queries, NT) * (1.0 / float(DH) ** 0.5)).reshape(8, 16, 256)
    return [jnp.where(key_valid[j] > 0, logits[j], NEG) for j in range(8)]


def put(ref, g, h, value):
    value = value.astype(ref.dtype).reshape(NY, 2, 16, DH)
    ref[:, 0, :, g * 16 : (g + 1) * 16, cols(h)] = value


def stats_kernel(key_valid, qqk_ref, max_ref, sum_ref):
    mask = same_time()
    for h in range(H):
        for g in range(RY // 16):
            logits = scaled_logits(key_valid, take(qqk_ref, g, h, 2), queries_of(qqk_ref, g, h))
            top = functools.reduce(jnp.maximum, logits)
            total = functools.reduce(jnp.add, [jnp.exp(one - top) for one in logits])
            r = h * (RY // 16) + g
            max_ref[r : r + 1, :] = jnp.sum(jnp.where(mask, top, 0.0), axis=0, keepdims=True)
            sum_ref[r : r + 1, :] = jnp.sum(jnp.where(mask, total, 0.0), axis=0, keepdims=True)


def swap_halves(x):
    return jnp.concatenate([x[:, 128:], x[:, :128]], axis=1)


def weights_of(key_valid, k, q, r, max_ref, sum_ref, maxx_ref, sumx_ref, mask):
    logits = scaled_logits(key_valid, k, q)
    m, mx = max_ref[r : r + 1, :], swap_halves(maxx_ref[r : r + 1, :])
    top = jnp.maximum(m, mx)
    total = sum_ref[r : r + 1, :] * jnp.exp(m - top) + swap_halves(sumx_ref[r : r + 1, :]) * jnp.exp(mx - top)
    inverse = 1.0 / total
    return [jnp.where(mask, jnp.exp(one - top) * inverse, 0.0) for one in logits]


def mix_kernel(key_valid, qqk_ref, g_ref, gx_ref, n_ref, max_ref, sum_ref, maxx_ref, sumx_ref, vi_ref, gn_ref, rd_ref):
    mask = same_time()
    vi = vi_ref[0:1, :]
    for h in range(H):
        for g in range(RY // 16):
            r = h * (RY // 16) + g
            weights = weights_of(
                key_valid, take(qqk_ref, g, h, 2), queries_of(qqk_ref, g, h), r, max_ref, sum_ref, maxx_ref, sumx_ref, mask
            )
            grads = grads_of(g_ref, gx_ref, g, h)
            grad_weights = dot(take(n_ref, g, h), grads, NT).reshape(8, 16, 256)
            weights = [one * vi for one in weights]
            put(gn_ref, g, h, dot(jnp.concatenate(weights, axis=0), grads, NN))
            total = functools.reduce(jnp.add, [weights[j] * grad_weights[j] for j in range(8)])
            rd_ref[r : r + 1, :] = jnp.sum(total, axis=0, keepdims=True)


def cross_grads_kernel(
    key_valid, qqk_ref, g_ref, gx_ref, n_ref, max_ref, sum_ref, maxx_ref, sumx_ref, vi_ref, rd_ref, rdx_ref,
    gk_ref, gq_ref, gqx_ref,
):
    mask = same_time()
    vi = vi_ref[0:1, :]
    for h in range(H):
        for g in range(RY // 16):
            r = h * (RY // 16) + g
            keys, queries = take(qqk_ref, g, h, 2), queries_of(qqk_ref, g, h)
            weights = weights_of(key_valid, keys, queries, r, max_ref, sum_ref, maxx_ref, sumx_ref, mask)
            grads = grads_of(g_ref, gx_ref, g, h)
            grad_weights = dot(take(n_ref, g, h), grads, NT).reshape(8, 16, 256)
            along = rd_ref[r : r + 1, :] + swap_halves(rdx_ref[r : r + 1, :])
            scale = vi * (1.0 / float(DH) ** 0.5)
            grad_logits = jnp.concatenate(
                [weights[j] * (grad_weights[j] - along) * scale for j in range(8)], axis=0
            )
            put(gk_ref, g, h, dot(grad_logits, queries, NN))
            grad_queries = dot(grad_logits, keys, TN)
            put(gq_ref, g, h, grad_queries[:128])
            put(gqx_ref, g, h, grad_queries[128:])


def join_kernel(gq_ref, gqx_ref, gk_ref, out_ref):
    for y in range(NY):
        out_ref[y, 0] = (gq_ref[y, 0] + gqx_ref[y, 0].astype(F32)).astype(BF16)
        out_ref[y, 1] = gk_ref[y, 0]


def grad_outputs_kernel(at, valid, ld_ref, q_ref, out_ref, gn_ref, go_ref, keep_ref, send_ref):
    for i, msg_ref in enumerate((keep_ref, send_ref)):
        x = at[0] if i == 0 else 1 - at[0]
        row, col, _ = sums(ld_ref[x])
        flag = valid[x].astype(F32)
        for h in range(H):
            out = out_ref[x, :, cols(h)]
            grad = jnp.concatenate([gn_ref[y, 0, x, :, cols(h)] for y in range(NY)], axis=0).astype(F32)
            inverse = 1.0 / jnp.sqrt(jnp.mean(out * out, axis=-1, keepdims=True) + EPSILON)
            along = jnp.sum(grad * out, axis=-1, keepdims=True)
            go = flag * (inverse * grad - (inverse * inverse * inverse * (1.0 / DH) * along) * out)
            go_ref[x, :, cols(h)] = go
            scaled = go * jnp.exp(col[:, h : h + 1])
            store_message(msg_ref, h, dot(q_ref[x, :, cols(h)], scaled, TN), row[h : h + 1, T - 1 : T])


def local_grads_kernel(at, valid, ld_ref, q_ref, k_ref, v_ref, go_ref, *refs):
    *s_refs, gq_ref, gk_ref, gv_ref = refs
    for i, s_ref in enumerate(s_refs):
        x = at[0] if i == 0 else 1 - at[0]
        row, col, keep = sums(ld_ref[x])
        flag = valid[x].astype(F32)
        for h in range(H):
            q, k, v = q_ref[x, :, cols(h)], k_ref[x, :, cols(h)], v_ref[x, :, cols(h)]
            go = go_ref[x, :, cols(h)]
            decay = jnp.exp(jnp.where(keep, col[:, h : h + 1] - row[h : h + 1, :], -jnp.inf)) * flag
            scores = dot(q, k, NT) * decay
            grad_scores = dot(go, v, NT) * decay
            gq = dot(grad_scores, k, NN) + jnp.exp(col[:, h : h + 1]) * dot(go, s_ref[h], NT)
            gq_ref[x, :, cols(h)] = gq.astype(BF16)
            gk_ref[x, :, cols(h)] = dot(grad_scores, q, TN)
            gv_ref[x, :, cols(h)] = dot(scores, go, TN)


def final_kernel(at, valid, ld_ref, k_ref, v_ref, gk_in, gv_in, *refs):
    *s_refs, gk_ref, gv_ref = refs
    for i, s_ref in enumerate(s_refs):
        x = at[0] if i == 0 else 1 - at[0]
        row, col, _ = sums(ld_ref[x])
        flag = valid[x].astype(F32)
        for h in range(H):
            k, v = k_ref[x, :, cols(h)], v_ref[x, :, cols(h)]
            to_end = jnp.exp(col[T - 1 : T, h : h + 1] - col[:, h : h + 1]) * flag
            state = s_ref[h]
            gk_ref[x, :, cols(h)] = (gk_in[x, :, cols(h)] * flag + to_end * dot(v, state, NT)).astype(BF16)
            gv_ref[x, :, cols(h)] = (gv_in[x, :, cols(h)] * flag + to_end * dot(k, state, NN)).astype(BF16)


YS = [[half * NY + y for y in range(NY)] for half in range(2)]
SWAP = [(i, (i + NY) % (2 * NY)) for i in range(2 * NY)]


def over_y(x):
    return lax.all_to_all(x, "track", 0, 0, axis_index_groups=YS, tiled=True)


def swap(x):
    return lax.ppermute(x, "track", SWAP)


def over_tm(x, to):
    pairs = []
    for i in range(NZ * NX * 2):
        place = to(i // (2 * NX), i // 2 % NX, i % 2)
        if place is not None:
            pairs.append((i, (place[0] * NX + place[1]) * 2 + place[2]))
    return lax.ppermute(x, "tm", pairs)


def core_swap(x):
    return over_tm(x, lambda z, x, c: (z, x, 1 - c))


def x_shift(x, step):
    return over_tm(x, lambda z, x, c: (z, (x + step) % NX, c)) if step else x


def z_shift(x, step):
    return over_tm(x, lambda z, x, c: (z + step, x, c) if 0 <= z + step < NZ else None)


def chip_totals(mine, send, at, back):
    theirs = core_swap(send)
    totals = vmem_call(functools.partial(chip_total_kernel, back), (shape(2, PR, DH),) * NX, 1, 2)(at, mine, theirs)
    return theirs, [x_shift(one, q) for q, one in enumerate(totals)]


def earlier_rows(totals, at, back, after):
    row, total = vmem_call(
        functools.partial(row_total_kernel, back),
        (shape(NX, 2, PR, DH), shape(2, PZ, DH, dtype=BF16)),
        1,
        NX,
        after=after,
    )(at, *totals)
    sign = -1 if back else 1
    return row, [z_shift(total, sign * step) for step in (3, 2, 1)]


def chip_starts(row, far, at, initial, back, after):
    own = () if back else (initial,)
    starts = vmem_call(
        functools.partial(row_starts_kernel, back),
        (shape(2, DH, DH),) * NX,
        1,
        len(own) + 4,
        scratch=[pltpu.VMEM((NX, 2, DH, DH), F32)],
        after=after,
    )(at, *own, row, *far)
    return [x_shift(one, q) for q, one in enumerate(starts)]


def core_starts(starts, mine, theirs, at, back, after=()):
    keep, give = vmem_call(
        functools.partial(core_starts_kernel, back), (shape(H, DH, DH),) * 2, 1, NX + 2, after=after
    )(at, *starts, mine, theirs)
    return keep, core_swap(give)


def per_device(q, k, v, log_decay, valid_length, initial, cross_q, cross_k, grad_out):
    tm, track = lax.axis_index("tm"), lax.axis_index("track")
    half, first = track // NY, tm * T
    alive = (first < valid_length).astype(jnp.int32)
    own_valid = lax.dynamic_slice(alive, (2 * track,), (2,))
    half_valid = lax.dynamic_slice(alive, (8 * half,), (8,))
    other_valid = lax.dynamic_slice(alive, (8 * (1 - half),), (8,))
    lanes = jnp.repeat(jnp.concatenate([half_valid, other_valid]).astype(F32), 16)
    vi = jnp.broadcast_to(lanes[None, :], (8, 256))
    at = jnp.stack([tm % 2, tm // 2 % NX, tm // (2 * NX)]).astype(jnp.int32)

    message = (shape(H, PR, DH),) * 2
    whole = shape(2, T, H * DH)
    half_whole = shape(2, T, H * DH, dtype=BF16)
    quarter = shape(NY, 1, 2, RY, H * DH, dtype=BF16)
    row_stats = shape(RY // 16 * H, 256)

    raw_qx = swap(cross_q)
    packed_g = pack(grad_out)
    gy = over_y(packed_g)
    mine, send = vmem_call(block_state_kernel, message, 2, 3, after=(packed_g,))(at, own_valid, log_decay, k, v)
    theirs, totals = chip_totals(mine, send, at, False)
    row, far = earlier_rows(totals, at, False, (raw_qx,))
    packed_q = pack(cross_q, raw_qx, cross_k)
    qqk = over_y(packed_q)
    starts = chip_starts(row, far, at, initial, False, (packed_q,))
    gy, _ = lax.optimization_barrier((gy, far[0]))
    gx = swap(gy)
    states = core_starts(starts, mine, theirs, at, False)
    tops, sums_ = vmem_call(stats_kernel, (row_stats, row_stats), 1, 1)(half_valid, qqk)
    topsx, sumsx = swap(tops), swap(sums_)
    out, normed = vmem_call(outputs_kernel, (whole, quarter), 2, 6, after=(tops,))(
        at, own_valid, log_decay, q, k, v, *states
    )
    nx = over_y(normed)
    cross_in = (half_valid, qqk, gy, gx, nx, tops, sums_, topsx, sumsx, vi)
    gn, rd = vmem_call(mix_kernel, (quarter, row_stats), 1, 9)(*cross_in)
    gn_t = over_y(gn)
    rdx = swap(rd)
    gk_x, gq_own, gq_other = vmem_call(cross_grads_kernel, (quarter, shape(NY, 1, 2, RY, H * DH), quarter), 1, 11)(
        *cross_in, rd, rdx
    )
    gq_back = swap(gq_other)
    go, mine, send = vmem_call(grad_outputs_kernel, (whole, *message), 2, 4, after=(gq_other,))(
        at, own_valid, log_decay, q, out, gn_t
    )
    theirs, totals = chip_totals(mine, send, at, True)
    row, far = earlier_rows(totals, at, True, (gq_back,))
    joined = vmem_call(join_kernel, shape(NY, 2, 2, RY, H * DH, dtype=BF16), 0, 3)(gq_own, gq_back, gk_x)
    starts = chip_starts(row, far, at, None, True, (joined,))
    joined = over_y(joined)
    grad_q, gk_local, gv_local = vmem_call(local_grads_kernel, (half_whole, whole, whole), 2, 7)(
        at, own_valid, log_decay, q, k, v, go, *states
    )
    state_grads = core_starts(starts, mine, theirs, at, True, (grad_q,))
    grad_k, grad_v = vmem_call(final_kernel, (half_whole, half_whole), 2, 7)(
        at, own_valid, log_decay, k, v, gk_local, gv_local, *state_grads
    )
    grad_cross = joined.transpose(1, 2, 0, 3, 4).reshape(2, 2, T, H * DH)
    return grad_q, grad_k, grad_v, grad_cross[0], grad_cross[1]


def solution(mesh):
    rows = P("track", "tm", None)
    return jax.shard_map(
        per_device,
        mesh=mesh,
        in_specs=(rows, rows, rows, P("track", None, "tm"), P(), P("track", None, None, None), rows, rows, rows),
        out_specs=(rows,) * 5,
        check_vma=False,
    )
```

time: 252 us -> 202 us (0.80)
  waiting for transfers between devices: 97.9 us -> 53.6 us
  Pallas kernels: 30.1 us -> 43.1 us
  blocking collectives: 11 us -> 0 us
  local copies, waits for them, and re-layouts: 24.6 us -> 14.2 us
  starting transfers between devices: 85.8 us -> 89.2 us
    all_to_all x4 -> x0, starting transfers between devices: 39 us -> none  [to_rows(): return lax.all_to_all(x, 'tm', 0, 0, axis_index_groups=ROWS, tiled=True)]
    ppermute x6 -> x22, starting transfers between devices: 13.6 us -> 48.6 us  [over_tm(): return lax.ppermute(x, 'tm', pairs)]
    all_to_all x4 -> x0, waiting for transfers between devices: 33.4 us -> none  [to_rows(): return lax.all_to_all(x, 'tm', 0, 0, axis_index_groups=ROWS, tiled=True)]
    pallas_call x13 -> x19, Pallas kernels: 30.1 us -> 43.1 us  [vmem_call(): return lambda *args: call(*args, *after)]
    all_to_all x1 -> x0, blocking collectives: 11 us -> none  [over_y(): return lax.all_to_all(x, 'track', 0, 0, axis_index_groups=YS, tiled=True)]
    ppermute x6, starting transfers between devices: 11.4 us -> 18.9 us  [swap(): return lax.ppermute(x, 'track', SWAP)]
    ppermute x6 -> x22, waiting for transfers between devices: 30.7 us -> 24.3 us  [over_tm(): return lax.ppermute(x, 'tm', pairs)]
    unnamed x62, local copies, waits for them, and re-layouts: 16.9 us -> 10.9 us
  transfers between devices with their start and end apart: 21 -> 33, of which waited for: 15 -> 19; matrix products, arithmetic and copies ran while one was open for 2% -> 2% of each run, Pallas kernels for 8% -> 18%
where the time goes in v2:
time: 202 us; the launch traced here: 201 us
  starting transfers between devices  89.2 us (44%)
  waiting for transfers between devices  53.6 us (27%)
  Pallas kernels  43.1 us (21%)
  local copies, waits for them, and re-layouts  14.2 us (7%)
    ppermute x22, starting transfers between devices, over_tm(): return lax.ppermute(x, 'tm', pairs)  48.6 us
    pallas_call x19, Pallas kernels, vmem_call(): return lambda *args: call(*args, *after)  43.1 us
    ppermute x6, waiting for transfers between devices, swap(): return lax.ppermute(x, 'track', SWAP)  29.3 us
    ppermute x22, waiting for transfers between devices, over_tm(): return lax.ppermute(x, 'tm', pairs)  24.3 us
    all_to_all x5, starting transfers between devices, over_y(): return lax.all_to_all(x, 'track', 0, 0, axis_index_groups=YS, tiled=True)  21.7 us
    ppermute x6, starting transfers between devices, swap(): return lax.ppermute(x, 'track', SWAP)  18.9 us
    unnamed x62, local copies, waits for them, and re-layouts  10.9 us
  transfers between devices with their start and end apart: 33, of which 19 were waited for; matrix products, arithmetic and copies ran while one was open for 2% of the time, Pallas kernels for 18%

profile of v2, /device:TPU:1, one launch (start us, length us, event | category | flops | bytes accessed | tf_op | source)
XLA Modules:
  0.0 201.2 jit_solution(1733620119077064358)
XLA Ops:
  0.7 7.8 %collective-permute-start.4 = (bf16[2,128,1024]{2,1,0:T(8,128)(2,1)}, bf16[2,128,1024]{2,1,0:T(8,128)(2,1)S(1)}, u32[]{:S(2)}, u32[]{:S(2)}) collective-permute-start(bf16[2,128,1024]{2,1,0:T(8,128)(2,1)} %refs_0_.3), channel_id=1, source_target_pairs={{0,128},{32,160},{64,192},{96,224},{128,0},{160,32},{192,64},{224,... | collective-permute-start | bytes 1572872 | tf_op jit(solution)/shard_map/ppermute | solution.py:357
  10.4 4.3 %all-to-all-start.1 = ((bf16[4,1,2,32,1024]{4,3,2,1,0:T(8,128)(2,1)}), bf16[4,1,2,32,1024]{4,3,2,1,0:T(8,128)(2,1)}, u32[]{:S(2)}, u32[]{:S(2)}) async-start(bf16[4,1,2,32,1024]{4,3,2,1,0:T(8,128)(2,1)} %shard_map.128.refs_5_), calls=%async_computation.1 | async-start | bytes 1048576 | tf_op jit(solution)/shard_map/all_to_all | solution.py:353
  14.9 2.6 %shard_map.129 = (f32[8,136,128]{2,1,0:T(8,128)S(1)}, f32[8,136,128]{2,1,0:T(8,128)}) custom-call(s32[3]{0:T(128)S(1)} %pad_add_fusion.refs_0_, s32[2]{0:T(128)S(1)} %dynamic_slice.9.refs_1_, f32[2,8,128]{2,1,0:T(8,128)S(1)} %copy-done.29, bf16[2,128,1024]{2,1,0:T(8,128)(2,1)S(1)} %copy-done, bf16[2,128,1024]{2,1,0:T(8,128)(2,1)S(1)} %copy-done.1, ...), custom_call_target="tpu_custom_call" | custom-call | tf_op jit(solution)/shard_map/pallas_call | solution.py:79
  18.7 3.2 %collective-permute-done.4.refs_5_.refs_1_ = bf16[2,128,1024]{2,1,0:T(8,128)(2,1)S(1)} collective-permute-done((bf16[2,128,1024]{2,1,0:T(8,128)(2,1)}, bf16[2,128,1024]{2,1,0:T(8,128)(2,1)S(1)}, u32[]{:S(2)}, u32[]{:S(2)}) %collective-permute-start.4) | collective-permute-done | bytes 524320 | tf_op jit(solution)/shard_map/ppermute | solution.py:357
  23.2 4.7 %all-to-all-start = ((bf16[4,3,2,32,1024]{4,3,2,1,0:T(8,128)(2,1)}), bf16[4,3,2,32,1024]{4,3,2,1,0:T(8,128)(2,1)S(1)}, u32[]{:S(2)}, u32[]{:S(2)}) async-start(bf16[4,3,2,32,1024]{4,3,2,1,0:T(8,128)(2,1)} %shard_map.132.refs_6_), calls=%async_computation | async-start | bytes 3145728 | tf_op jit(solution)/shard_map/all_to_all | solution.py:353
  30.5 2.5 %collective-permute-start.2 = (f32[2,136,128]{2,1,0:T(8,128)S(1)}, f32[2,136,128]{2,1,0:T(8,128)S(1)}, u32[]{:S(2)}, u32[]{:S(2)}) collective-permute-start(f32[2,136,128]{2,1,0:T(8,128)S(1)} %get-tuple-element.53), channel_id=1, source_target_pairs={{0,4},{1,5},{2,6},{3,7},{4,0},{5,1},{6,2},{7,3},{8,12},{9,13},{10,... | collective-permute-start | bytes 417800 | tf_op jit(solution)/shard_map/ppermute | solution.py:366
  34.7 3.0 %collective-permute-done.2.refs_3_ = f32[2,136,128]{2,1,0:T(8,128)S(1)} collective-permute-done((f32[2,136,128]{2,1,0:T(8,128)S(1)}, f32[2,136,128]{2,1,0:T(8,128)S(1)}, u32[]{:S(2)}, u32[]{:S(2)}) %collective-permute-start.2) | collective-permute-done | bytes 139296 | tf_op jit(solution)/shard_map/ppermute | solution.py:366
  39.8 8.7 %collective-permute-start.5 = (bf16[2,144,128]{2,1,0:T(8,128)(2,1)S(1)}, bf16[2,144,128]{2,1,0:T(8,128)(2,1)S(1)}, u32[]{:S(2)}, u32[]{:S(2)}) collective-permute-start(bf16[2,144,128]{2,1,0:T(8,128)(2,1)S(1)} %get-tuple-element.56), channel_id=1, source_target_pairs={{0,24},{1,25},{2,26},{3,27},{4,28},{5,29},{6,30},{7,31},{32,56},{3... | collective-permute-start | bytes 221192 | tf_op jit(solution)/shard_map/ppermute | solution.py:366
  48.5 4.8 %collective-permute-start.6 = (bf16[2,144,128]{2,1,0:T(8,128)(2,1)S(1)}, bf16[2,144,128]{2,1,0:T(8,128)(2,1)S(1)}, u32[]{:S(2)}, u32[]{:S(2)}) collective-permute-start(bf16[2,144,128]{2,1,0:T(8,128)(2,1)S(1)} %get-tuple-element.56), channel_id=1, source_target_pairs={{0,16},{1,17},{2,18},{3,19},{4,20},{5,21},{6,22},{7,23},{8,24},{9,... | collective-permute-start | bytes 221192 | tf_op jit(solution)/shard_map/ppermute | solution.py:366
  57.3 3.0 %collective-permute-start.9 = (f32[2,128,128]{2,1,0:T(8,128)S(1)}, f32[2,128,128]{2,1,0:T(8,128)S(1)}, u32[]{:S(2)}, u32[]{:S(2)}) collective-permute-start(f32[2,128,128]{2,1,0:T(8,128)S(1)} %get-tuple-element.59), channel_id=1, source_target_pairs={{0,4},{1,5},{2,6},{3,7},{4,0},{5,1},{6,2},{7,3},{8,12},{9,13},{10,... | collective-permute-start | bytes 393224 | tf_op jit(solution)/shard_map/ppermute | solution.py:366
  61.8 2.2 %collective-permute-done.9.refs_3_ = f32[2,128,128]{2,1,0:T(8,128)S(1)} collective-permute-done((f32[2,128,128]{2,1,0:T(8,128)S(1)}, f32[2,128,128]{2,1,0:T(8,128)S(1)}, u32[]{:S(2)}, u32[]{:S(2)}) %collective-permute-start.9) | collective-permute-done | bytes 131104 | tf_op jit(solution)/shard_map/ppermute | solution.py:366
  67.2 4.6 %collective-permute-start.11 = (f32[8,128,128]{2,1,0:T(8,128)}, f32[8,128,128]{2,1,0:T(8,128)}, u32[]{:S(2)}, u32[]{:S(2)}) collective-permute-start(f32[8,128,128]{2,1,0:T(8,128)} %get-tuple-element.62), channel_id=1, source_target_pairs={{0,1},{1,0},{2,3},{3,2},{4,5},{5,4},{6,7},{7,6},{8,9},{9,8},{10,11... | collective-permute-start | bytes 1572872 | tf_op jit(solution)/shard_map/ppermute | solution.py:366
  71.8 4.7 %collective-permute-start.12 = (bf16[4,1,2,32,1024]{4,3,2,1,0:T(8,128)(2,1)}, bf16[4,1,2,32,1024]{4,3,2,1,0:T(8,128)(2,1)}, u32[]{:S(2)}, u32[]{:S(2)}) collective-permute-start(bf16[4,1,2,32,1024]{4,3,2,1,0:T(8,128)(2,1)} %all-to-all-done.1.refs_2_), channel_id=1, source_target_pairs={{0,128},{32,160},{64,192},{96,224},{128,0},{160,32},{192,64},{224,... | collective-permute-start | bytes 1572872 | tf_op jit(solution)/shard_map/ppermute | solution.py:357
  78.1 3.3 %shard_map.136 = (f32[2,128,1024]{2,1,0:T(8,128)S(1)}, bf16[4,1,2,32,1024]{4,3,2,1,0:T(8,128)(2,1)S(1)}) custom-call(s32[3]{0:T(128)S(1)} %pad_add_fusion.refs_0_, s32[2]{0:T(128)S(1)} %dynamic_slice.9.refs_1_, f32[2,8,128]{2,1,0:T(8,128)S(1)} %copy-done.29, bf16[2,128,1024]{2,1,0:T(8,128)(2,1)S(1)} %copy-done.2, bf16[2,128,1024]{2,1,0:T(8,128)(2,1)S(1)} %copy-done, ...), custom_call_target="tpu_custom_call" | custom-call | tf_op jit(solution)/shard_map/pallas_call | solution.py:79
  83.1 4.2 %all-to-all-start.2 = ((bf16[4,1,2,32,1024]{4,3,2,1,0:T(8,128)(2,1)}), bf16[4,1,2,32,1024]{4,3,2,1,0:T(8,128)(2,1)}, u32[]{:S(2)}, u32[]{:S(2)}) async-start(bf16[4,1,2,32,1024]{4,3,2,1,0:T(8,128)(2,1)} %copy-done.23), calls=%async_computation.2 | async-start | bytes 1048576 | tf_op jit(solution)/shard_map/all_to_all | solution.py:353
  88.2 4.7 %collective-permute-start.14 = (f32[16,256]{1,0:T(8,128)S(1)}, f32[16,256]{1,0:T(8,128)S(1)}, u32[]{:S(2)}, u32[]{:S(2)}) collective-permute-start(f32[16,256]{1,0:T(8,128)S(1)} %get-tuple-element.67.refs_6_), channel_id=1, source_target_pairs={{0,128},{32,160},{64,192},{96,224},{128,0},{160,32},{192,64},{224,... | collective-permute-start | bytes 49160 | tf_op jit(solution)/shard_map/ppermute | solution.py:357
  94.2 10.0 %collective-permute-done.14.refs_8_ = f32[16,256]{1,0:T(8,128)S(1)} collective-permute-done((f32[16,256]{1,0:T(8,128)S(1)}, f32[16,256]{1,0:T(8,128)S(1)}, u32[]{:S(2)}, u32[]{:S(2)}) %collective-permute-start.14) | collective-permute-done | bytes 16416 | tf_op jit(solution)/shard_map/ppermute | solution.py:357
  104.2 4.6 %shard_map.137 = (bf16[4,1,2,32,1024]{4,3,2,1,0:T(8,128)(2,1)S(1)}, f32[16,256]{1,0:T(8,128)S(1)}) custom-call(s32[8]{0:T(128)S(1)} %get-tuple-element.96.refs_0_, bf16[4,3,2,32,1024]{4,3,2,1,0:T(8,128)(2,1)S(1)} %all-to-all-done.refs_1_, bf16[4,1,2,32,1024]{4,3,2,1,0:T(8,128)(2,1)} %all-to-all-done.1.refs_2_, ...), custom_call_target="tpu_custom_call" | custom-call | tf_op jit(solution)/shard_map/pallas_call | solution.py:79
  109.5 4.1 %all-to-all-start.3 = ((bf16[4,1,2,32,1024]{4,3,2,1,0:T(8,128)(2,1)}), bf16[4,1,2,32,1024]{4,3,2,1,0:T(8,128)(2,1)}, u32[]{:S(2)}, u32[]{:S(2)}) async-start(bf16[4,1,2,32,1024]{4,3,2,1,0:T(8,128)(2,1)} %copy-done.22), calls=%async_computation.3 | async-start | bytes 1048576 | tf_op jit(solution)/shard_map/all_to_all | solution.py:353
  114.1 6.1 %collective-permute-done.15.refs_11_ = f32[16,256]{1,0:T(8,128)S(1)} collective-permute-done((f32[16,256]{1,0:T(8,128)S(1)}, f32[16,256]{1,0:T(8,128)S(1)}, u32[]{:S(2)}, u32[]{:S(2)}) %collective-permute-start.15) | collective-permute-done | bytes 16416 | tf_op jit(solution)/shard_map/ppermute | solution.py:357
  120.3 5.8 %shard_map.138 = (bf16[4,1,2,32,1024]{4,3,2,1,0:T(8,128)(2,1)S(1)}, f32[4,1,2,32,1024]{4,3,2,1,0:T(8,128)S(1)}, bf16[4,1,2,32,1024]{4,3,2,1,0:T(8,128)(2,1)}) custom-call(s32[8]{0:T(128)S(1)} %get-tuple-element.96.refs_0_, bf16[4,3,2,32,1024]{4,3,2,1,0:T(8,128)(2,1)S(1)} %all-to-all-done.refs_1_, bf16[4,1,2,32,1024]{4,3,2,1,0:T(8,128)(2,1)} %all-to-all-done.1.refs_2_, ...), custom_call_target="tpu_custom_call" | custom-call | tf_op jit(solution)/shard_map/pallas_call | solution.py:79
  129.4 4.3 %shard_map.139 = (f32[2,128,1024]{2,1,0:T(8,128)S(1)}, f32[8,136,128]{2,1,0:T(8,128)S(1)}, f32[8,136,128]{2,1,0:T(8,128)}) custom-call(s32[3]{0:T(128)S(1)} %pad_add_fusion.refs_0_, s32[2]{0:T(128)S(1)} %dynamic_slice.9.refs_1_, f32[2,8,128]{2,1,0:T(8,128)S(1)} %copy-done.29, bf16[2,128,1024]{2,1,0:T(8,128)(2,1)S(1)} %copy-done.2, ...), custom_call_target="tpu_custom_call" | custom-call | tf_op jit(solution)/shard_map/pallas_call | solution.py:79
  134.7 3.4 %collective-permute-start.16 = (f32[8,136,128]{2,1,0:T(8,128)}, f32[8,136,128]{2,1,0:T(8,128)S(1)}, u32[]{:S(2)}, u32[]{:S(2)}) collective-permute-start(f32[8,136,128]{2,1,0:T(8,128)} %get-tuple-element.76), channel_id=1, source_target_pairs={{0,1},{1,0},{2,3},{3,2},{4,5},{5,4},{6,7},{7,6},{8,9},{9,8},{10,11... | collective-permute-start | bytes 1671176 | tf_op jit(solution)/shard_map/ppermute | solution.py:366
  138.1 9.0 %collective-permute-done.20.refs_5_.refs_1_ = bf16[4,1,2,32,1024]{4,3,2,1,0:T(8,128)(2,1)} collective-permute-done((bf16[4,1,2,32,1024]{4,3,2,1,0:T(8,128)(2,1)}, bf16[4,1,2,32,1024]{4,3,2,1,0:T(8,128)(2,1)}, u32[]{:S(2)}, u32[]{:S(2)}) %collective-permute-start.20) | collective-permute-done | bytes 524320 | tf_op jit(solution)/shard_map/ppermute | solution.py:357
  147.1 2.1 %shard_map.143.refs_5_ = bf16[4,2,2,32,1024]{4,3,2,1,0:T(8,128)(2,1)} custom-call(f32[4,1,2,32,1024]{4,3,2,1,0:T(8,128)S(1)} %copy-done.17, bf16[4,1,2,32,1024]{4,3,2,1,0:T(8,128)(2,1)} %collective-permute-done.20.refs_5_.refs_1_, bf16[4,1,2,32,1024]{4,3,2,1,0:T(8,128)(2,1)S(1)} %copy-done.28), custom_call_target="tpu_custom_call" | custom-call | tf_op jit(solution)/shard_map/pallas_call | solution.py:79
  149.2 4.2 %all-to-all-start.4 = ((bf16[4,2,2,32,1024]{4,3,2,1,0:T(8,128)(2,1)}), bf16[4,2,2,32,1024]{4,3,2,1,0:T(8,128)(2,1)}, u32[]{:S(2)}, u32[]{:S(2)}) async-start(bf16[4,2,2,32,1024]{4,3,2,1,0:T(8,128)(2,1)} %shard_map.143.refs_5_), calls=%async_computation.4 | async-start | bytes 2097152 | tf_op jit(solution)/shard_map/all_to_all | solution.py:353
  165.9 3.4 %collective-permute-done.21.refs_2_ = bf16[2,144,128]{2,1,0:T(8,128)(2,1)S(1)} collective-permute-done((bf16[2,144,128]{2,1,0:T(8,128)(2,1)S(1)}, bf16[2,144,128]{2,1,0:T(8,128)(2,1)S(1)}, u32[]{:S(2)}, u32[]{:S(2)}) %collective-permute-start.21) | collective-permute-done | bytes 73760 | tf_op jit(solution)/shard_map/ppermute | solution.py:366
  169.3 5.4 %collective-permute-done.22.refs_3_ = bf16[2,144,128]{2,1,0:T(8,128)(2,1)S(1)} collective-permute-done((bf16[2,144,128]{2,1,0:T(8,128)(2,1)S(1)}, bf16[2,144,128]{2,1,0:T(8,128)(2,1)S(1)}, u32[]{:S(2)}, u32[]{:S(2)}) %collective-permute-start.22) | collective-permute-done | bytes 73760 | tf_op jit(solution)/shard_map/ppermute | solution.py:366
  174.8 2.9 %collective-permute-done.23.refs_4_ = bf16[2,144,128]{2,1,0:T(8,128)(2,1)S(1)} collective-permute-done((bf16[2,144,128]{2,1,0:T(8,128)(2,1)S(1)}, bf16[2,144,128]{2,1,0:T(8,128)(2,1)S(1)}, u32[]{:S(2)}, u32[]{:S(2)}) %collective-permute-start.23) | collective-permute-done | bytes 73760 | tf_op jit(solution)/shard_map/ppermute | solution.py:366
  182.8 6.6 %shard_map.140 = (bf16[2,128,1024]{2,1,0:T(8,128)(2,1)}, f32[2,128,1024]{2,1,0:T(8,128)S(1)}, f32[2,128,1024]{2,1,0:T(8,128)S(1)}) custom-call(s32[3]{0:T(128)S(1)} %pad_add_fusion.refs_0_, s32[2]{0:T(128)S(1)} %dynamic_slice.9.refs_1_, f32[2,8,128]{2,1,0:T(8,128)S(1)} %copy-done.29, bf16[2,128,1024]{2,1,0:T(8,128)(2,1)S(1)} %copy-done.2, ...), custom_call_target="tpu_custom_call" | custom-call | tf_op jit(solution)/shard_map/pallas_call | solution.py:79
  192.3 3.5 %collective-permute-start.27 = (f32[8,128,128]{2,1,0:T(8,128)}, f32[8,128,128]{2,1,0:T(8,128)S(1)}, u32[]{:S(2)}, u32[]{:S(2)}) collective-permute-start(f32[8,128,128]{2,1,0:T(8,128)} %get-tuple-element.90), channel_id=1, source_target_pairs={{0,1},{1,0},{2,3},{3,2},{4,5},{5,4},{6,7},{7,6},{8,9},{9,8},{10,11... | collective-permute-start | bytes 1572872 | tf_op jit(solution)/shard_map/ppermute | solution.py:366
  198.8 2.4 %shard_map.146 = (bf16[2,128,1024]{2,1,0:T(8,128)(2,1)}, bf16[2,128,1024]{2,1,0:T(8,128)(2,1)}) custom-call(s32[3]{0:T(128)S(1)} %pad_add_fusion.refs_0_, s32[2]{0:T(128)S(1)} %dynamic_slice.9.refs_1_, f32[2,8,128]{2,1,0:T(8,128)S(1)} %copy-done.29, bf16[2,128,1024]{2,1,0:T(8,128)(2,1)S(1)} %copy-done, bf16[2,128,1024]{2,1,0:T(8,128)(2,1)S(1)} %copy-done.1, ...), custom_call_target="tpu_custom_call" | custom-call | tf_op jit(solution)/shard_map/pallas_call | solution.py:79
  (126 shorter events, 54.1 us)
Async XLA Ops:
  0.7 21.2 %collective-permute-start.4 = (bf16[2,128,1024]{2,1,0:T(8,128)(2,1)}, bf16[2,128,1024]{2,1,0:T(8,128)(2,1)S(1)}, u32[]{:S(2)}, u32[]{:S(2)}) collective-permute-start(bf16[2,128,1024]{2,1,0:T(8,128)(2,1)} %refs_0_.3), channel_id=1, source_target_pairs={{0,128},{32,160},{64,192},{96,224},{128,0},{160,32},{192,64},{224,... | collective-permute-start | bytes 1572872 | tf_op jit(solution)/shard_map/ppermute | solution.py:357
  10.4 12.9 %all-to-all-start.1 = ((bf16[4,1,2,32,1024]{4,3,2,1,0:T(8,128)(2,1)}), bf16[4,1,2,32,1024]{4,3,2,1,0:T(8,128)(2,1)}, u32[]{:S(2)}, u32[]{:S(2)}) async-start(bf16[4,1,2,32,1024]{4,3,2,1,0:T(8,128)(2,1)} %shard_map.128.refs_5_), calls=%async_computation.1 | async-start | bytes 1048576 | tf_op jit(solution)/shard_map/all_to_all | solution.py:353
  17.5 10.5 %collective-permute-start = (f32[8,136,128]{2,1,0:T(8,128)}, f32[8,136,128]{2,1,0:T(8,128)}, u32[]{:S(2)}, u32[]{:S(2)}) collective-permute-start(f32[8,136,128]{2,1,0:T(8,128)} %get-tuple-element.50), channel_id=1, source_target_pairs={{0,1},{1,0},{2,3},{3,2},{4,5},{5,4},{6,7},{7,6},{8,9},{9,8},{10,11... | collective-permute-start | bytes 1671176 | tf_op jit(solution)/shard_map/ppermute | solution.py:366
  23.2 53.4 %all-to-all-start = ((bf16[4,3,2,32,1024]{4,3,2,1,0:T(8,128)(2,1)}), bf16[4,3,2,32,1024]{4,3,2,1,0:T(8,128)(2,1)S(1)}, u32[]{:S(2)}, u32[]{:S(2)}) async-start(bf16[4,3,2,32,1024]{4,3,2,1,0:T(8,128)(2,1)} %shard_map.132.refs_6_), calls=%async_computation | async-start | bytes 3145728 | tf_op jit(solution)/shard_map/all_to_all | solution.py:353
  29.2 5.5 %collective-permute-start.1 = (f32[2,136,128]{2,1,0:T(8,128)S(1)}, f32[2,136,128]{2,1,0:T(8,128)S(1)}, u32[]{:S(2)}, u32[]{:S(2)}) collective-permute-start(f32[2,136,128]{2,1,0:T(8,128)S(1)} %get-tuple-element.52), channel_id=1, source_target_pairs={{0,2},{1,3},{2,4},{3,5},{4,6},{5,7},{6,0},{7,1},{8,10},{9,11},{10,... | collective-permute-start | bytes 417800 | tf_op jit(solution)/shard_map/ppermute | solution.py:366
  30.5 7.2 %collective-permute-start.2 = (f32[2,136,128]{2,1,0:T(8,128)S(1)}, f32[2,136,128]{2,1,0:T(8,128)S(1)}, u32[]{:S(2)}, u32[]{:S(2)}) collective-permute-start(f32[2,136,128]{2,1,0:T(8,128)S(1)} %get-tuple-element.53), channel_id=1, source_target_pairs={{0,4},{1,5},{2,6},{3,7},{4,0},{5,1},{6,2},{7,3},{8,12},{9,13},{10,... | collective-permute-start | bytes 417800 | tf_op jit(solution)/shard_map/ppermute | solution.py:366
  32.9 5.2 %collective-permute-start.3 = (f32[2,136,128]{2,1,0:T(8,128)S(1)}, f32[2,136,128]{2,1,0:T(8,128)S(1)}, u32[]{:S(2)}, u32[]{:S(2)}) collective-permute-start(f32[2,136,128]{2,1,0:T(8,128)S(1)} %get-tuple-element.54), channel_id=1, source_target_pairs={{0,6},{1,7},{2,0},{3,1},{4,2},{5,3},{6,4},{7,5},{8,14},{9,15},{10,... | collective-permute-start | bytes 417800 | tf_op jit(solution)/shard_map/ppermute | solution.py:366
  39.8 14.8 %collective-permute-start.5 = (bf16[2,144,128]{2,1,0:T(8,128)(2,1)S(1)}, bf16[2,144,128]{2,1,0:T(8,128)(2,1)S(1)}, u32[]{:S(2)}, u32[]{:S(2)}) collective-permute-start(bf16[2,144,128]{2,1,0:T(8,128)(2,1)S(1)} %get-tuple-element.56), channel_id=1, source_target_pairs={{0,24},{1,25},{2,26},{3,27},{4,28},{5,29},{6,30},{7,31},{32,56},{3... | collective-permute-start | bytes 221192 | tf_op jit(solution)/shard_map/ppermute | solution.py:366
  48.5 6.2 %collective-permute-start.6 = (bf16[2,144,128]{2,1,0:T(8,128)(2,1)S(1)}, bf16[2,144,128]{2,1,0:T(8,128)(2,1)S(1)}, u32[]{:S(2)}, u32[]{:S(2)}) collective-permute-start(bf16[2,144,128]{2,1,0:T(8,128)(2,1)S(1)} %get-tuple-element.56), channel_id=1, source_target_pairs={{0,16},{1,17},{2,18},{3,19},{4,20},{5,21},{6,22},{7,23},{8,24},{9,... | collective-permute-start | bytes 221192 | tf_op jit(solution)/shard_map/ppermute | solution.py:366
  56.7 5.1 %collective-permute-start.8 = (f32[2,128,128]{2,1,0:T(8,128)S(1)}, f32[2,128,128]{2,1,0:T(8,128)S(1)}, u32[]{:S(2)}, u32[]{:S(2)}) collective-permute-start(f32[2,128,128]{2,1,0:T(8,128)S(1)} %get-tuple-element.58), channel_id=1, source_target_pairs={{0,2},{1,3},{2,4},{3,5},{4,6},{5,7},{6,0},{7,1},{8,10},{9,11},{10,... | collective-permute-start | bytes 393224 | tf_op jit(solution)/shard_map/ppermute | solution.py:366
  57.3 6.8 %collective-permute-start.9 = (f32[2,128,128]{2,1,0:T(8,128)S(1)}, f32[2,128,128]{2,1,0:T(8,128)S(1)}, u32[]{:S(2)}, u32[]{:S(2)}) collective-permute-start(f32[2,128,128]{2,1,0:T(8,128)S(1)} %get-tuple-element.59), channel_id=1, source_target_pairs={{0,4},{1,5},{2,6},{3,7},{4,0},{5,1},{6,2},{7,3},{8,12},{9,13},{10,... | collective-permute-start | bytes 393224 | tf_op jit(solution)/shard_map/ppermute | solution.py:366
  60.3 4.1 %collective-permute-start.10 = (f32[2,128,128]{2,1,0:T(8,128)S(1)}, f32[2,128,128]{2,1,0:T(8,128)S(1)}, u32[]{:S(2)}, u32[]{:S(2)}) collective-permute-start(f32[2,128,128]{2,1,0:T(8,128)S(1)} %get-tuple-element.60), channel_id=1, source_target_pairs={{0,6},{1,7},{2,0},{3,1},{4,2},{5,3},{6,4},{7,5},{8,14},{9,15},{10,... | collective-permute-start | bytes 393224 | tf_op jit(solution)/shard_map/ppermute | solution.py:366
  67.2 10.8 %collective-permute-start.11 = (f32[8,128,128]{2,1,0:T(8,128)}, f32[8,128,128]{2,1,0:T(8,128)}, u32[]{:S(2)}, u32[]{:S(2)}) collective-permute-start(f32[8,128,128]{2,1,0:T(8,128)} %get-tuple-element.62), channel_id=1, source_target_pairs={{0,1},{1,0},{2,3},{3,2},{4,5},{5,4},{6,7},{7,6},{8,9},{9,8},{10,11... | collective-permute-start | bytes 1572872 | tf_op jit(solution)/shard_map/ppermute | solution.py:366
  71.8 21.3 %collective-permute-start.12 = (bf16[4,1,2,32,1024]{4,3,2,1,0:T(8,128)(2,1)}, bf16[4,1,2,32,1024]{4,3,2,1,0:T(8,128)(2,1)}, u32[]{:S(2)}, u32[]{:S(2)}) collective-permute-start(bf16[4,1,2,32,1024]{4,3,2,1,0:T(8,128)(2,1)} %all-to-all-done.1.refs_2_), channel_id=1, source_target_pairs={{0,128},{32,160},{64,192},{96,224},{128,0},{160,32},{192,64},{224,... | collective-permute-start | bytes 1572872 | tf_op jit(solution)/shard_map/ppermute | solution.py:357
  83.1 21.0 %all-to-all-start.2 = ((bf16[4,1,2,32,1024]{4,3,2,1,0:T(8,128)(2,1)}), bf16[4,1,2,32,1024]{4,3,2,1,0:T(8,128)(2,1)}, u32[]{:S(2)}, u32[]{:S(2)}) async-start(bf16[4,1,2,32,1024]{4,3,2,1,0:T(8,128)(2,1)} %copy-done.23), calls=%async_computation.2 | async-start | bytes 1048576 | tf_op jit(solution)/shard_map/all_to_all | solution.py:353
  87.4 6.8 %collective-permute-start.13 = (f32[16,256]{1,0:T(8,128)S(1)}, f32[16,256]{1,0:T(8,128)S(1)}, u32[]{:S(2)}, u32[]{:S(2)}) collective-permute-start(f32[16,256]{1,0:T(8,128)S(1)} %get-tuple-element.63.refs_8_.refs_5_), channel_id=1, source_target_pairs={{0,128},{32,160},{64,192},{96,224},{128,0},{160,32},{192,64},{224,... | collective-permute-start | bytes 49160 | tf_op jit(solution)/shard_map/ppermute | solution.py:357
  88.2 16.0 %collective-permute-start.14 = (f32[16,256]{1,0:T(8,128)S(1)}, f32[16,256]{1,0:T(8,128)S(1)}, u32[]{:S(2)}, u32[]{:S(2)}) collective-permute-start(f32[16,256]{1,0:T(8,128)S(1)} %get-tuple-element.67.refs_6_), channel_id=1, source_target_pairs={{0,128},{32,160},{64,192},{96,224},{128,0},{160,32},{192,64},{224,... | collective-permute-start | bytes 49160 | tf_op jit(solution)/shard_map/ppermute | solution.py:357
  109.5 18.7 %all-to-all-start.3 = ((bf16[4,1,2,32,1024]{4,3,2,1,0:T(8,128)(2,1)}), bf16[4,1,2,32,1024]{4,3,2,1,0:T(8,128)(2,1)}, u32[]{:S(2)}, u32[]{:S(2)}) async-start(bf16[4,1,2,32,1024]{4,3,2,1,0:T(8,128)(2,1)} %copy-done.22), calls=%async_computation.3 | async-start | bytes 1048576 | tf_op jit(solution)/shard_map/all_to_all | solution.py:353
  113.7 6.6 %collective-permute-start.15 = (f32[16,256]{1,0:T(8,128)S(1)}, f32[16,256]{1,0:T(8,128)S(1)}, u32[]{:S(2)}, u32[]{:S(2)}) collective-permute-start(f32[16,256]{1,0:T(8,128)S(1)} %get-tuple-element.69.refs_10_), channel_id=1, source_target_pairs={{0,128},{32,160},{64,192},{96,224},{128,0},{160,32},{192,64},{224,... | collective-permute-start | bytes 49160 | tf_op jit(solution)/shard_map/ppermute | solution.py:357
  127.8 19.3 %collective-permute-start.20 = (bf16[4,1,2,32,1024]{4,3,2,1,0:T(8,128)(2,1)}, bf16[4,1,2,32,1024]{4,3,2,1,0:T(8,128)(2,1)}, u32[]{:S(2)}, u32[]{:S(2)}) collective-permute-start(bf16[4,1,2,32,1024]{4,3,2,1,0:T(8,128)(2,1)} %get-tuple-element.70.refs_6_), channel_id=1, source_target_pairs={{0,128},{32,160},{64,192},{96,224},{128,0},{160,32},{192,64},{224,... | collective-permute-start | bytes 1572872 | tf_op jit(solution)/shard_map/ppermute | solution.py:357
  134.7 18.8 %collective-permute-start.16 = (f32[8,136,128]{2,1,0:T(8,128)}, f32[8,136,128]{2,1,0:T(8,128)S(1)}, u32[]{:S(2)}, u32[]{:S(2)}) collective-permute-start(f32[8,136,128]{2,1,0:T(8,128)} %get-tuple-element.76), channel_id=1, source_target_pairs={{0,1},{1,0},{2,3},{3,2},{4,5},{5,4},{6,7},{7,6},{8,9},{9,8},{10,11... | collective-permute-start | bytes 1671176 | tf_op jit(solution)/shard_map/ppermute | solution.py:366
  149.2 46.6 %all-to-all-start.4 = ((bf16[4,2,2,32,1024]{4,3,2,1,0:T(8,128)(2,1)}), bf16[4,2,2,32,1024]{4,3,2,1,0:T(8,128)(2,1)}, u32[]{:S(2)}, u32[]{:S(2)}) async-start(bf16[4,2,2,32,1024]{4,3,2,1,0:T(8,128)(2,1)} %shard_map.143.refs_5_), calls=%async_computation.4 | async-start | bytes 2097152 | tf_op jit(solution)/shard_map/all_to_all | solution.py:353
  154.1 5.2 %collective-permute-start.17 = (f32[2,136,128]{2,1,0:T(8,128)S(1)}, f32[2,136,128]{2,1,0:T(8,128)S(1)}, u32[]{:S(2)}, u32[]{:S(2)}) collective-permute-start(f32[2,136,128]{2,1,0:T(8,128)S(1)} %get-tuple-element.78), channel_id=1, source_target_pairs={{0,2},{1,3},{2,4},{3,5},{4,6},{5,7},{6,0},{7,1},{8,10},{9,11},{10,... | collective-permute-start | bytes 417800 | tf_op jit(solution)/shard_map/ppermute | solution.py:366
  155.3 6.0 %collective-permute-start.18 = (f32[2,136,128]{2,1,0:T(8,128)S(1)}, f32[2,136,128]{2,1,0:T(8,128)S(1)}, u32[]{:S(2)}, u32[]{:S(2)}) collective-permute-start(f32[2,136,128]{2,1,0:T(8,128)S(1)} %get-tuple-element.79), channel_id=1, source_target_pairs={{0,4},{1,5},{2,6},{3,7},{4,0},{5,1},{6,2},{7,3},{8,12},{9,13},{10,... | collective-permute-start | bytes 417800 | tf_op jit(solution)/shard_map/ppermute | solution.py:366
  157.3 4.0 %collective-permute-start.19 = (f32[2,136,128]{2,1,0:T(8,128)S(1)}, f32[2,136,128]{2,1,0:T(8,128)S(1)}, u32[]{:S(2)}, u32[]{:S(2)}) collective-permute-start(f32[2,136,128]{2,1,0:T(8,128)S(1)} %get-tuple-element.80), channel_id=1, source_target_pairs={{0,6},{1,7},{2,0},{3,1},{4,2},{5,3},{6,4},{7,5},{8,14},{9,15},{10,... | collective-permute-start | bytes 417800 | tf_op jit(solution)/shard_map/ppermute | solution.py:366
  162.0 7.3 %collective-permute-start.21 = (bf16[2,144,128]{2,1,0:T(8,128)(2,1)S(1)}, bf16[2,144,128]{2,1,0:T(8,128)(2,1)S(1)}, u32[]{:S(2)}, u32[]{:S(2)}) collective-permute-start(bf16[2,144,128]{2,1,0:T(8,128)(2,1)S(1)} %get-tuple-element.82), channel_id=1, source_target_pairs={{24,0},{25,1},{26,2},{27,3},{28,4},{29,5},{30,6},{31,7},{56,32},{5... | collective-permute-start | bytes 221192 | tf_op jit(solution)/shard_map/ppermute | solution.py:366
  163.3 11.4 %collective-permute-start.22 = (bf16[2,144,128]{2,1,0:T(8,128)(2,1)S(1)}, bf16[2,144,128]{2,1,0:T(8,128)(2,1)S(1)}, u32[]{:S(2)}, u32[]{:S(2)}) collective-permute-start(bf16[2,144,128]{2,1,0:T(8,128)(2,1)S(1)} %get-tuple-element.82), channel_id=1, source_target_pairs={{16,0},{17,1},{18,2},{19,3},{20,4},{21,5},{22,6},{23,7},{24,8},{25... | collective-permute-start | bytes 221192 | tf_op jit(solution)/shard_map/ppermute | solution.py:366
  164.6 13.0 %collective-permute-start.23 = (bf16[2,144,128]{2,1,0:T(8,128)(2,1)S(1)}, bf16[2,144,128]{2,1,0:T(8,128)(2,1)S(1)}, u32[]{:S(2)}, u32[]{:S(2)}) collective-permute-start(bf16[2,144,128]{2,1,0:T(8,128)(2,1)S(1)} %get-tuple-element.82), channel_id=1, source_target_pairs={{8,0},{9,1},{10,2},{11,3},{12,4},{13,5},{14,6},{15,7},{16,8},{17,9... | collective-permute-start | bytes 221192 | tf_op jit(solution)/shard_map/ppermute | solution.py:366
  178.3 11.1 %collective-permute-start.24 = (f32[2,128,128]{2,1,0:T(8,128)S(1)}, f32[2,128,128]{2,1,0:T(8,128)S(1)}, u32[]{:S(2)}, u32[]{:S(2)}) collective-permute-start(f32[2,128,128]{2,1,0:T(8,128)S(1)} %get-tuple-element.86), channel_id=1, source_target_pairs={{0,2},{1,3},{2,4},{3,5},{4,6},{5,7},{6,0},{7,1},{8,10},{9,11},{10,... | collective-permute-start | bytes 393224 | tf_op jit(solution)/shard_map/ppermute | solution.py:366
  180.3 9.1 %collective-permute-start.25 = (f32[2,128,128]{2,1,0:T(8,128)S(1)}, f32[2,128,128]{2,1,0:T(8,128)S(1)}, u32[]{:S(2)}, u32[]{:S(2)}) collective-permute-start(f32[2,128,128]{2,1,0:T(8,128)S(1)} %get-tuple-element.87), channel_id=1, source_target_pairs={{0,4},{1,5},{2,6},{3,7},{4,0},{5,1},{6,2},{7,3},{8,12},{9,13},{10,... | collective-permute-start | bytes 393224 | tf_op jit(solution)/shard_map/ppermute | solution.py:366
  182.3 7.1 %collective-permute-start.26 = (f32[2,128,128]{2,1,0:T(8,128)S(1)}, f32[2,128,128]{2,1,0:T(8,128)S(1)}, u32[]{:S(2)}, u32[]{:S(2)}) collective-permute-start(f32[2,128,128]{2,1,0:T(8,128)S(1)} %get-tuple-element.88), channel_id=1, source_target_pairs={{0,6},{1,7},{2,0},{3,1},{4,2},{5,3},{6,4},{7,5},{8,14},{9,15},{10,... | collective-permute-start | bytes 393224 | tf_op jit(solution)/shard_map/ppermute | solution.py:366
  192.3 6.5 %collective-permute-start.27 = (f32[8,128,128]{2,1,0:T(8,128)}, f32[8,128,128]{2,1,0:T(8,128)S(1)}, u32[]{:S(2)}, u32[]{:S(2)}) collective-permute-start(f32[8,128,128]{2,1,0:T(8,128)} %get-tuple-element.90), channel_id=1, source_target_pairs={{0,1},{1,0},{2,3},{3,2},{4,5},{5,4},{6,7},{7,6},{8,9},{9,8},{10,11... | collective-permute-start | bytes 1572872 | tf_op jit(solution)/shard_map/ppermute | solution.py:366
  (32 other events, 257.1 us)

commit v3 on v2

--- a/solution.py
+++ b/solution.py
@@ -75,6 +75,7 @@
         out_specs=jax.tree.map(lambda _: pl.BlockSpec(memory_space=pltpu.VMEM), out_shape),
         scratch_shapes=scratch,
         compiler_params=pltpu.CompilerParams(vmem_limit_bytes=VMEM_LIMIT),
+        name=getattr(body, "func", body).__name__,
     )
     return lambda *args: call(*args, *after)
 
@@ -102,6 +103,12 @@
 def pack(*arrays, after=()):
     n = len(arrays)
     return vmem_call(pack_kernel, shape(NY, n, 2, RY, H * DH, dtype=BF16), 0, n, after=after)(*arrays)
+
+
+def unpack_kernel(in_ref, *out_refs):
+    for i, one in enumerate(out_refs):
+        for y in range(NY):
+            one[:, y * RY : (y + 1) * RY, :] = in_ref[y, i]
 
 
 def block_state_kernel(at, valid, ld_ref, k_ref, v_ref, keep_ref, send_ref):
@@ -207,12 +214,12 @@
     return part.reshape(128, DH)
 
 
-def queries_of(qqk_ref, g, h):
-    return jnp.concatenate([take(qqk_ref, g, h, 0), take(qqk_ref, g, h, 1)], axis=0)
-
-
-def grads_of(g_ref, gx_ref, g, h):
-    return jnp.concatenate([take(g_ref, g, h), take(gx_ref, g, h)], axis=0)
+def queries_of(qkg_ref, qx_ref, g, h):
+    return jnp.concatenate([take(qkg_ref, g, h, 0), take(qx_ref, g, h)], axis=0)
+
+
+def grads_of(qkg_ref, gx_ref, g, h):
+    return jnp.concatenate([take(qkg_ref, g, h, 2), take(gx_ref, g, h)], axis=0)
 
 
 def scaled_logits(key_valid, keys, queries):
@@ -225,41 +232,42 @@
     ref[:, 0, :, g * 16 : (g + 1) * 16, cols(h)] = value
 
 
-def stats_kernel(key_valid, qqk_ref, max_ref, sum_ref):
+def stats_kernel(key_valid, qkg_ref, qx_ref, stats_ref):
     mask = same_time()
     for h in range(H):
         for g in range(RY // 16):
-            logits = scaled_logits(key_valid, take(qqk_ref, g, h, 2), queries_of(qqk_ref, g, h))
+            logits = scaled_logits(key_valid, take(qkg_ref, g, h, 1), queries_of(qkg_ref, qx_ref, g, h))
             top = functools.reduce(jnp.maximum, logits)
             total = functools.reduce(jnp.add, [jnp.exp(one - top) for one in logits])
             r = h * (RY // 16) + g
-            max_ref[r : r + 1, :] = jnp.sum(jnp.where(mask, top, 0.0), axis=0, keepdims=True)
-            sum_ref[r : r + 1, :] = jnp.sum(jnp.where(mask, total, 0.0), axis=0, keepdims=True)
+            stats_ref[0, r : r + 1, :] = jnp.sum(jnp.where(mask, top, 0.0), axis=0, keepdims=True)
+            stats_ref[1, r : r + 1, :] = jnp.sum(jnp.where(mask, total, 0.0), axis=0, keepdims=True)
 
 
 def swap_halves(x):
     return jnp.concatenate([x[:, 128:], x[:, :128]], axis=1)
 
 
-def weights_of(key_valid, k, q, r, max_ref, sum_ref, maxx_ref, sumx_ref, mask):
+def weights_of(key_valid, k, q, r, stats_ref, statsx_ref, mask):
     logits = scaled_logits(key_valid, k, q)
-    m, mx = max_ref[r : r + 1, :], swap_halves(maxx_ref[r : r + 1, :])
+    m, mx = stats_ref[0, r : r + 1, :], swap_halves(statsx_ref[0, r : r + 1, :])
     top = jnp.maximum(m, mx)
-    total = sum_ref[r : r + 1, :] * jnp.exp(m - top) + swap_halves(sumx_ref[r : r + 1, :]) * jnp.exp(mx - top)
+    total = stats_ref[1, r : r + 1, :] * jnp.exp(m - top)
+    total = total + swap_halves(statsx_ref[1, r : r + 1, :]) * jnp.exp(mx - top)
     inverse = 1.0 / total
     return [jnp.where(mask, jnp.exp(one - top) * inverse, 0.0) for one in logits]
 
 
-def mix_kernel(key_valid, qqk_ref, g_ref, gx_ref, n_ref, max_ref, sum_ref, maxx_ref, sumx_ref, vi_ref, gn_ref, rd_ref):
+def mix_kernel(key_valid, qkg_ref, qx_ref, gx_ref, n_ref, stats_ref, statsx_ref, vi_ref, gn_ref, rd_ref):
     mask = same_time()
     vi = vi_ref[0:1, :]
     for h in range(H):
         for g in range(RY // 16):
             r = h * (RY // 16) + g
             weights = weights_of(
-                key_valid, take(qqk_ref, g, h, 2), queries_of(qqk_ref, g, h), r, max_ref, sum_ref, maxx_ref, sumx_ref, mask
+                key_valid, take(qkg_ref, g, h, 1), queries_of(qkg_ref, qx_ref, g, h), r, stats_ref, statsx_ref, mask
             )
-            grads = grads_of(g_ref, gx_ref, g, h)
+            grads = grads_of(qkg_ref, gx_ref, g, h)
             grad_weights = dot(take(n_ref, g, h), grads, NT).reshape(8, 16, 256)
             weights = [one * vi for one in weights]
             put(gn_ref, g, h, dot(jnp.concatenate(weights, axis=0), grads, NN))
@@ -268,7 +276,7 @@
 
 
 def cross_grads_kernel(
-    key_valid, qqk_ref, g_ref, gx_ref, n_ref, max_ref, sum_ref, maxx_ref, sumx_ref, vi_ref, rd_ref, rdx_ref,
+    key_valid, qkg_ref, qx_ref, gx_ref, n_ref, stats_ref, statsx_ref, vi_ref, rd_ref, rdx_ref,
     gk_ref, gq_ref, gqx_ref,
 ):
     mask = same_time()
@@ -276,9 +284,9 @@
     for h in range(H):
         for g in range(RY // 16):
             r = h * (RY // 16) + g
-            keys, queries = take(qqk_ref, g, h, 2), queries_of(qqk_ref, g, h)
-            weights = weights_of(key_valid, keys, queries, r, max_ref, sum_ref, maxx_ref, sumx_ref, mask)
-            grads = grads_of(g_ref, gx_ref, g, h)
+            keys, queries = take(qkg_ref, g, h, 1), queries_of(qkg_ref, qx_ref, g, h)
+            weights = weights_of(key_valid, keys, queries, r, stats_ref, statsx_ref, mask)
+            grads = grads_of(qkg_ref, gx_ref, g, h)
             grad_weights = dot(take(n_ref, g, h), grads, NT).reshape(8, 16, 256)
             along = rd_ref[r : r + 1, :] + swap_halves(rdx_ref[r : r + 1, :])
             scale = vi * (1.0 / float(DH) ** 0.5)
@@ -378,9 +386,11 @@
     return over_tm(x, lambda z, x, c: (z + step, x, c) if 0 <= z + step < NZ else None)
 
 
-def chip_totals(mine, send, at, back):
+def chip_totals(mine, send, at, back, after=()):
     theirs = core_swap(send)
-    totals = vmem_call(functools.partial(chip_total_kernel, back), (shape(2, PR, DH),) * NX, 1, 2)(at, mine, theirs)
+    totals = vmem_call(functools.partial(chip_total_kernel, back), (shape(2, PR, DH),) * NX, 1, 2, after=after)(
+        at, mine, theirs
+    )
     return theirs, [x_shift(one, q) for q, one in enumerate(totals)]
 
 
@@ -432,50 +442,46 @@
     half_whole = shape(2, T, H * DH, dtype=BF16)
     quarter = shape(NY, 1, 2, RY, H * DH, dtype=BF16)
     row_stats = shape(RY // 16 * H, 256)
-
-    raw_qx = swap(cross_q)
-    packed_g = pack(grad_out)
-    gy = over_y(packed_g)
-    mine, send = vmem_call(block_state_kernel, message, 2, 3, after=(packed_g,))(at, own_valid, log_decay, k, v)
+    row_stats2 = shape(2, RY // 16 * H, 256)
+
+    packed = pack(cross_q, cross_k, grad_out)
+    qkg = over_y(packed)
+    mine, send = vmem_call(block_state_kernel, message, 2, 3, after=(packed,))(at, own_valid, log_decay, k, v)
     theirs, totals = chip_totals(mine, send, at, False)
-    row, far = earlier_rows(totals, at, False, (raw_qx,))
-    packed_q = pack(cross_q, raw_qx, cross_k)
-    qqk = over_y(packed_q)
-    starts = chip_starts(row, far, at, initial, False, (packed_q,))
-    gy, _ = lax.optimization_barrier((gy, far[0]))
-    gx = swap(gy)
+    row, far = earlier_rows(totals, at, False, ())
+    starts = chip_starts(row, far, at, initial, False, (qkg,))
+    qkg_, *_ = lax.optimization_barrier((qkg, *far))
+    qx, gx = swap(qkg_[:, :1]), swap(qkg_[:, 2:])
     states = core_starts(starts, mine, theirs, at, False)
-    tops, sums_ = vmem_call(stats_kernel, (row_stats, row_stats), 1, 1)(half_valid, qqk)
-    topsx, sumsx = swap(tops), swap(sums_)
-    out, normed = vmem_call(outputs_kernel, (whole, quarter), 2, 6, after=(tops,))(
-        at, own_valid, log_decay, q, k, v, *states
-    )
+    out, normed = vmem_call(outputs_kernel, (whole, quarter), 2, 6)(at, own_valid, log_decay, q, k, v, *states)
+    stats = vmem_call(stats_kernel, row_stats2, 1, 2)(half_valid, qkg, qx)
+    stats_x = swap(stats)
     nx = over_y(normed)
-    cross_in = (half_valid, qqk, gy, gx, nx, tops, sums_, topsx, sumsx, vi)
-    gn, rd = vmem_call(mix_kernel, (quarter, row_stats), 1, 9)(*cross_in)
+    cross_in = (half_valid, qkg, qx, gx, nx, stats, stats_x, vi)
+    gn, rd = vmem_call(mix_kernel, (quarter, row_stats), 1, 7)(*cross_in)
     gn_t = over_y(gn)
     rdx = swap(rd)
-    gk_x, gq_own, gq_other = vmem_call(cross_grads_kernel, (quarter, shape(NY, 1, 2, RY, H * DH), quarter), 1, 11)(
+    gk_x, gq_own, gq_other = vmem_call(cross_grads_kernel, (quarter, shape(NY, 1, 2, RY, H * DH), quarter), 1, 9)(
         *cross_in, rd, rdx
     )
     gq_back = swap(gq_other)
     go, mine, send = vmem_call(grad_outputs_kernel, (whole, *message), 2, 4, after=(gq_other,))(
         at, own_valid, log_decay, q, out, gn_t
     )
-    theirs, totals = chip_totals(mine, send, at, True)
-    row, far = earlier_rows(totals, at, True, (gq_back,))
     joined = vmem_call(join_kernel, shape(NY, 2, 2, RY, H * DH, dtype=BF16), 0, 3)(gq_own, gq_back, gk_x)
-    starts = chip_starts(row, far, at, None, True, (joined,))
-    joined = over_y(joined)
-    grad_q, gk_local, gv_local = vmem_call(local_grads_kernel, (half_whole, whole, whole), 2, 7)(
+    joined_y = over_y(joined)
+    theirs, totals = chip_totals(mine, send, at, True, (joined,))
+    row, far = earlier_rows(totals, at, True, ())
+    grad_q, gk_local, gv_local = vmem_call(local_grads_kernel, (half_whole, whole, whole), 2, 7, after=(row,))(
         at, own_valid, log_decay, q, k, v, go, *states
     )
-    state_grads = core_starts(starts, mine, theirs, at, True, (grad_q,))
+    starts = chip_starts(row, far, at, None, True, (grad_q,))
+    grad_cq, grad_ck = vmem_call(unpack_kernel, (half_whole, half_whole), 0, 1)(joined_y)
+    state_grads = core_starts(starts, mine, theirs, at, True, (grad_cq,))
     grad_k, grad_v = vmem_call(final_kernel, (half_whole, half_whole), 2, 7)(
         at, own_valid, log_decay, k, v, gk_local, gv_local, *state_grads
     )
-    grad_cross = joined.transpose(1, 2, 0, 3, 4).reshape(2, 2, T, H * DH)
-    return grad_q, grad_k, grad_v, grad_cross[0], grad_cross[1]
+    return grad_q, grad_k, grad_v, grad_cq, grad_ck
 
 
 def solution(mesh):

time: 202 us -> 197 us (0.975)
  starting transfers between devices: 89.2 us -> 68.7 us
  blocking collectives: 0 us -> 12.8 us
  waiting for transfers between devices: 53.6 us -> 58.4 us
  Pallas kernels: 43.1 us -> 39.3 us
    all_to_all x0 -> x1, blocking collectives: none -> 12.8 us  [over_y(): return lax.all_to_all(x, 'track', 0, 0, axis_index_groups=YS, tiled=True)]
    ppermute x22, starting transfers between devices: 48.6 us -> 39.7 us  [over_tm(): return lax.ppermute(x, 'tm', pairs)]
    all_to_all x5 -> x3, starting transfers between devices: 21.7 us -> 13.3 us  [over_y(): return lax.all_to_all(x, 'track', 0, 0, axis_index_groups=YS, tiled=True)]
    ppermute x22, waiting for transfers between devices: 24.3 us -> 32.3 us  [over_tm(): return lax.ppermute(x, 'tm', pairs)]
    pallas_call x19, Pallas kernels: 43.1 us -> 39.3 us  [vmem_call(): return lambda *args: call(*args, *after)]
    unnamed x62 -> x60, local copies, waits for them, and re-layouts: 10.9 us -> 14.6 us
    ppermute x6 -> x5, starting transfers between devices: 18.9 us -> 15.7 us  [swap(): return lax.ppermute(x, 'track', SWAP)]
    ppermute x6 -> x5, waiting for transfers between devices: 29.3 us -> 26 us  [swap(): return lax.ppermute(x, 'track', SWAP)]
  transfers between devices with their start and end apart: 33 -> 30, of which waited for: 19 -> 20; matrix products, arithmetic and copies ran while one was open for 2% -> 1% of each run, Pallas kernels for 18% -> 12%
where the time goes in v3:
time: 197 us; the launch traced here: 196 us
  starting transfers between devices  68.7 us (35%)
  waiting for transfers between devices  58.4 us (30%)
  Pallas kernels  39.3 us (20%)
  local copies, waits for them, and re-layouts  16 us (8%)
  blocking collectives  12.8 us (6%)
    ppermute x22, starting transfers between devices, over_tm(): return lax.ppermute(x, 'tm', pairs)  39.7 us
    pallas_call x19, Pallas kernels, vmem_call(): return lambda *args: call(*args, *after)  39.3 us
    ppermute x22, waiting for transfers between devices, over_tm(): return lax.ppermute(x, 'tm', pairs)  32.3 us
    ppermute x5, waiting for transfers between devices, swap(): return lax.ppermute(x, 'track', SWAP)  26 us
    ppermute x5, starting transfers between devices, swap(): return lax.ppermute(x, 'track', SWAP)  15.7 us
    unnamed x60, local copies, waits for them, and re-layouts  14.6 us
    all_to_all x3, starting transfers between devices, over_y(): return lax.all_to_all(x, 'track', 0, 0, axis_index_groups=YS, tiled=True)  13.3 us
    all_to_all x1, blocking collectives, over_y(): return lax.all_to_all(x, 'track', 0, 0, axis_index_groups=YS, tiled=True)  12.8 us
  transfers between devices with their start and end apart: 30, of which 20 were waited for; matrix products, arithmetic and copies ran while one was open for 1% of the time, Pallas kernels for 12%

profile of v3, /device:TPU:1, one launch (start us, length us, event | category | flops | bytes accessed | tf_op | source)
XLA Modules:
  0.0 196.2 jit_solution(17771138816507950643)
XLA Ops:
  5.0 5.2 %all-to-all-start = ((bf16[4,3,2,32,1024]{4,3,2,1,0:T(8,128)(2,1)}), bf16[4,3,2,32,1024]{4,3,2,1,0:T(8,128)(2,1)S(1)}, u32[]{:S(2)}, u32[]{:S(2)}) async-start(bf16[4,3,2,32,1024]{4,3,2,1,0:T(8,128)(2,1)} %pack_kernel.1.refs_5_), calls=%async_computation | async-start | bytes 3145728 | tf_op jit(solution)/shard_map/all_to_all | solution.py:361
  17.4 2.5 %collective-permute-start.2 = (f32[2,136,128]{2,1,0:T(8,128)S(1)}, f32[2,136,128]{2,1,0:T(8,128)S(1)}, u32[]{:S(2)}, u32[]{:S(2)}) collective-permute-start(f32[2,136,128]{2,1,0:T(8,128)S(1)} %get-tuple-element.53), channel_id=1, source_target_pairs={{0,4},{1,5},{2,6},{3,7},{4,0},{5,1},{6,2},{7,3},{8,12},{9,13},{10,... | collective-permute-start | bytes 417800 | tf_op jit(solution)/shard_map/ppermute | solution.py:374
  21.0 2.2 %collective-permute-done.1.refs_2_ = f32[2,136,128]{2,1,0:T(8,128)S(1)} collective-permute-done((f32[2,136,128]{2,1,0:T(8,128)S(1)}, f32[2,136,128]{2,1,0:T(8,128)S(1)}, u32[]{:S(2)}, u32[]{:S(2)}) %collective-permute-start.1) | collective-permute-done | bytes 139296 | tf_op jit(solution)/shard_map/ppermute | solution.py:374
  23.2 3.1 %collective-permute-done.2.refs_3_ = f32[2,136,128]{2,1,0:T(8,128)S(1)} collective-permute-done((f32[2,136,128]{2,1,0:T(8,128)S(1)}, f32[2,136,128]{2,1,0:T(8,128)S(1)}, u32[]{:S(2)}, u32[]{:S(2)}) %collective-permute-start.2) | collective-permute-done | bytes 139296 | tf_op jit(solution)/shard_map/ppermute | solution.py:374
  27.1 3.4 %collective-permute-start.6 = (bf16[2,144,128]{2,1,0:T(8,128)(2,1)S(1)}, bf16[2,144,128]{2,1,0:T(8,128)(2,1)S(1)}, u32[]{:S(2)}, u32[]{:S(2)}) collective-permute-start(bf16[2,144,128]{2,1,0:T(8,128)(2,1)S(1)} %get-tuple-element.56), channel_id=1, source_target_pairs={{0,8},{1,9},{2,10},{3,11},{4,12},{5,13},{6,14},{7,15},{8,16},{9,17... | collective-permute-start | bytes 221192 | tf_op jit(solution)/shard_map/ppermute | solution.py:374
  30.5 4.9 %collective-permute-start.5 = (bf16[2,144,128]{2,1,0:T(8,128)(2,1)S(1)}, bf16[2,144,128]{2,1,0:T(8,128)(2,1)S(1)}, u32[]{:S(2)}, u32[]{:S(2)}) collective-permute-start(bf16[2,144,128]{2,1,0:T(8,128)(2,1)S(1)} %get-tuple-element.56), channel_id=1, source_target_pairs={{0,16},{1,17},{2,18},{3,19},{4,20},{5,21},{6,22},{7,23},{8,24},{9,... | collective-permute-start | bytes 221192 | tf_op jit(solution)/shard_map/ppermute | solution.py:374
  40.9 2.2 %collective-permute-start.8 = (f32[2,128,128]{2,1,0:T(8,128)S(1)}, f32[2,128,128]{2,1,0:T(8,128)S(1)}, u32[]{:S(2)}, u32[]{:S(2)}) collective-permute-start(f32[2,128,128]{2,1,0:T(8,128)S(1)} %get-tuple-element.59), channel_id=1, source_target_pairs={{0,4},{1,5},{2,6},{3,7},{4,0},{5,1},{6,2},{7,3},{8,12},{9,13},{10,... | collective-permute-start | bytes 393224 | tf_op jit(solution)/shard_map/ppermute | solution.py:374
  45.0 2.0 %collective-permute-done.8.refs_3_ = f32[2,128,128]{2,1,0:T(8,128)S(1)} collective-permute-done((f32[2,128,128]{2,1,0:T(8,128)S(1)}, f32[2,128,128]{2,1,0:T(8,128)S(1)}, u32[]{:S(2)}, u32[]{:S(2)}) %collective-permute-start.8) | collective-permute-done | bytes 131104 | tf_op jit(solution)/shard_map/ppermute | solution.py:374
  49.0 3.8 %collective-permute-start.10 = (f32[8,128,128]{2,1,0:T(8,128)S(1)}, f32[8,128,128]{2,1,0:T(8,128)S(1)}, u32[]{:S(2)}, u32[]{:S(2)}) collective-permute-start(f32[8,128,128]{2,1,0:T(8,128)S(1)} %get-tuple-element.62), channel_id=1, source_target_pairs={{0,1},{1,0},{2,3},{3,2},{4,5},{5,4},{6,7},{7,6},{8,9},{9,8},{10,11... | collective-permute-start | bytes 1572872 | tf_op jit(solution)/shard_map/ppermute | solution.py:374
  53.9 4.2 %collective-permute-start.11 = (bf16[4,1,2,32,1024]{4,3,2,1,0:T(8,128)(2,1)}, bf16[4,1,2,32,1024]{4,3,2,1,0:T(8,128)(2,1)}, u32[]{:S(2)}, u32[]{:S(2)}) collective-permute-start(bf16[4,1,2,32,1024]{4,3,2,1,0:T(8,128)(2,1)} %get-tuple-element.94), channel_id=1, source_target_pairs={{0,128},{32,160},{64,192},{96,224},{128,0},{160,32},{192,64},{224,... | collective-permute-start | bytes 1572872 | tf_op jit(solution)/shard_map/ppermute | solution.py:365
  59.2 2.7 %outputs_kernel.1 = (f32[2,128,1024]{2,1,0:T(8,128)S(1)}, bf16[4,1,2,32,1024]{4,3,2,1,0:T(8,128)(2,1)S(1)}) custom-call(s32[3]{0:T(128)S(1)} %pad_add_fusion.refs_0_, s32[2]{0:T(128)S(1)} %dynamic_slice.9.refs_1_, f32[2,8,128]{2,1,0:T(8,128)S(1)} %copy-done.28, bf16[2,128,1024]{2,1,0:T(8,128)(2,1)S(1)} %copy-done.2, bf16[2,128,1024]{2,1,0:T(8,128)(2,1)S(1)} %copy-done, ...), custom_call_target="tpu_custom_call" | custom-call | tf_op jit(solution)/shard_map/outputs_kernel/pallas_call | solution.py:80
  64.6 4.5 %all-to-all-start.1 = ((bf16[4,1,2,32,1024]{4,3,2,1,0:T(8,128)(2,1)}), bf16[4,1,2,32,1024]{4,3,2,1,0:T(8,128)(2,1)}, u32[]{:S(2)}, u32[]{:S(2)}) async-start(bf16[4,1,2,32,1024]{4,3,2,1,0:T(8,128)(2,1)} %copy-done.23), calls=%async_computation.1 | async-start | bytes 1048576 | tf_op jit(solution)/shard_map/all_to_all | solution.py:361
  69.2 3.3 %collective-permute-done.11.refs_2_ = bf16[4,1,2,32,1024]{4,3,2,1,0:T(8,128)(2,1)} collective-permute-done((bf16[4,1,2,32,1024]{4,3,2,1,0:T(8,128)(2,1)}, bf16[4,1,2,32,1024]{4,3,2,1,0:T(8,128)(2,1)}, u32[]{:S(2)}, u32[]{:S(2)}) %collective-permute-start.11) | collective-permute-done | bytes 524320 | tf_op jit(solution)/shard_map/ppermute | solution.py:365
  74.4 4.7 %collective-permute-start.13 = (f32[2,16,256]{2,1,0:T(8,128)S(1)}, f32[2,16,256]{2,1,0:T(8,128)S(1)}, u32[]{:S(2)}, u32[]{:S(2)}) collective-permute-start(f32[2,16,256]{2,1,0:T(8,128)S(1)} %stats_kernel.1.refs_5_), channel_id=1, source_target_pairs={{0,128},{32,160},{64,192},{96,224},{128,0},{160,32},{192,64},{224,... | collective-permute-start | bytes 98312 | tf_op jit(solution)/shard_map/ppermute | solution.py:365
  79.4 5.4 %collective-permute-done.12.refs_3_ = bf16[4,1,2,32,1024]{4,3,2,1,0:T(8,128)(2,1)} collective-permute-done((bf16[4,1,2,32,1024]{4,3,2,1,0:T(8,128)(2,1)}, bf16[4,1,2,32,1024]{4,3,2,1,0:T(8,128)(2,1)}, u32[]{:S(2)}, u32[]{:S(2)}) %collective-permute-start.12) | collective-permute-done | bytes 524320 | tf_op jit(solution)/shard_map/ppermute | solution.py:365
  85.6 4.6 %mix_kernel.1 = (bf16[4,1,2,32,1024]{4,3,2,1,0:T(8,128)(2,1)S(1)}, f32[16,256]{1,0:T(8,128)S(1)}) custom-call(s32[8]{0:T(128)S(1)} %get-tuple-element.96.refs_0_, bf16[4,3,2,32,1024]{4,3,2,1,0:T(8,128)(2,1)S(1)} %all-to-all-done.refs_6_.refs_1_, bf16[4,1,2,32,1024]{4,3,2,1,0:T(8,128)(2,1)} %collective-permute-done.11.refs_2_, ...), custom_call_target="tpu_custom_call" | custom-call | tf_op jit(solution)/shard_map/mix_kernel/pallas_call | solution.py:80
  90.2 4.4 %collective-permute-start.14 = (f32[16,256]{1,0:T(8,128)S(1)}, f32[16,256]{1,0:T(8,128)S(1)}, u32[]{:S(2)}, u32[]{:S(2)}) collective-permute-start(f32[16,256]{1,0:T(8,128)S(1)} %get-tuple-element.67.refs_8_), channel_id=1, source_target_pairs={{0,128},{32,160},{64,192},{96,224},{128,0},{160,32},{192,64},{224,... | collective-permute-start | bytes 49160 | tf_op jit(solution)/shard_map/ppermute | solution.py:365
  94.5 16.5 %collective-permute-done.14.refs_9_ = f32[16,256]{1,0:T(8,128)S(1)} collective-permute-done((f32[16,256]{1,0:T(8,128)S(1)}, f32[16,256]{1,0:T(8,128)S(1)}, u32[]{:S(2)}, u32[]{:S(2)}) %collective-permute-start.14) | collective-permute-done | bytes 16416 | tf_op jit(solution)/shard_map/ppermute | solution.py:365
  111.0 5.0 %cross_grads_kernel.1 = (bf16[4,1,2,32,1024]{4,3,2,1,0:T(8,128)(2,1)S(1)}, f32[4,1,2,32,1024]{4,3,2,1,0:T(8,128)S(1)}, bf16[4,1,2,32,1024]{4,3,2,1,0:T(8,128)(2,1)S(1)}) custom-call(s32[8]{0:T(128)S(1)} %get-tuple-element.96.refs_0_, bf16[4,3,2,32,1024]{4,3,2,1,0:T(8,128)(2,1)S(1)} %all-to-all-done.refs_6_.refs_1_, ...), custom_call_target="tpu_custom_call" | custom-call | tf_op jit(solution)/shard_map/cross_grads_kernel/pallas_call | solution.py:80
  117.3 12.8 %all_to_all.20.refs_5_ = bf16[4,1,2,32,1024]{4,3,2,1,0:T(8,128)(2,1)S(1)} all-to-all(bf16[4,1,2,32,1024]{4,3,2,1,0:T(8,128)(2,1)S(1)} %get-tuple-element.66), channel_id=1, replica_groups={{0,32,64,96},{128,160,192,224},{1,33,65,97},{129,161,193,225},{2,34,66,..., dimensions={0} | all-to-all | bytes 1048576 | tf_op jit(solution)/shard_map/all_to_all | solution.py:361
  130.1 3.6 %grad_outputs_kernel.1 = (f32[2,128,1024]{2,1,0:T(8,128)S(1)}, f32[8,136,128]{2,1,0:T(8,128)S(1)}, f32[8,136,128]{2,1,0:T(8,128)}) custom-call(s32[3]{0:T(128)S(1)} %pad_add_fusion.refs_0_, s32[2]{0:T(128)S(1)} %dynamic_slice.9.refs_1_, f32[2,8,128]{2,1,0:T(8,128)S(1)} %copy-done.28, bf16[2,128,1024]{2,1,0:T(8,128)(2,1)S(1)} %copy-done.2, ...), custom_call_target="tpu_custom_call" | custom-call | tf_op jit(solution)/shard_map/grad_outputs_kernel/pallas_call | solution.py:80
  138.6 3.6 %all-to-all-start.3 = ((bf16[4,2,2,32,1024]{4,3,2,1,0:T(8,128)(2,1)}), bf16[4,2,2,32,1024]{4,3,2,1,0:T(8,128)(2,1)S(1)}, u32[]{:S(2)}, u32[]{:S(2)}) async-start(bf16[4,2,2,32,1024]{4,3,2,1,0:T(8,128)(2,1)} %join_kernel.1.refs_3_), calls=%async_computation.3 | async-start | bytes 2097152 | tf_op jit(solution)/shard_map/all_to_all | solution.py:361
  145.9 2.2 %collective-permute-start.18 = (f32[2,136,128]{2,1,0:T(8,128)S(1)}, f32[2,136,128]{2,1,0:T(8,128)S(1)}, u32[]{:S(2)}, u32[]{:S(2)}) collective-permute-start(f32[2,136,128]{2,1,0:T(8,128)S(1)} %get-tuple-element.76), channel_id=1, source_target_pairs={{0,4},{1,5},{2,6},{3,7},{4,0},{5,1},{6,2},{7,3},{8,12},{9,13},{10,... | collective-permute-start | bytes 417800 | tf_op jit(solution)/shard_map/ppermute | solution.py:374
  148.6 2.5 %collective-permute-done.17.refs_2_ = f32[2,136,128]{2,1,0:T(8,128)S(1)} collective-permute-done((f32[2,136,128]{2,1,0:T(8,128)S(1)}, f32[2,136,128]{2,1,0:T(8,128)S(1)}, u32[]{:S(2)}, u32[]{:S(2)}) %collective-permute-start.17) | collective-permute-done | bytes 139296 | tf_op jit(solution)/shard_map/ppermute | solution.py:374
  151.1 3.8 %collective-permute-done.18.refs_3_ = f32[2,136,128]{2,1,0:T(8,128)S(1)} collective-permute-done((f32[2,136,128]{2,1,0:T(8,128)S(1)}, f32[2,136,128]{2,1,0:T(8,128)S(1)}, u32[]{:S(2)}, u32[]{:S(2)}) %collective-permute-start.18) | collective-permute-done | bytes 139296 | tf_op jit(solution)/shard_map/ppermute | solution.py:374
  159.7 6.8 %local_grads_kernel.1 = (bf16[2,128,1024]{2,1,0:T(8,128)(2,1)}, f32[2,128,1024]{2,1,0:T(8,128)S(1)}, f32[2,128,1024]{2,1,0:T(8,128)S(1)}) custom-call(s32[3]{0:T(128)S(1)} %pad_add_fusion.refs_0_, s32[2]{0:T(128)S(1)} %dynamic_slice.9.refs_1_, f32[2,8,128]{2,1,0:T(8,128)S(1)} %copy-done.28, bf16[2,128,1024]{2,1,0:T(8,128)(2,1)S(1)} %copy-done.2, ...), custom_call_target="tpu_custom_call" | custom-call | tf_op jit(solution)/shard_map/local_grads_kernel/pallas_call | solution.py:80
  167.5 6.6 %collective-permute-done.21.refs_3_ = bf16[2,144,128]{2,1,0:T(8,128)(2,1)S(1)} collective-permute-done((bf16[2,144,128]{2,1,0:T(8,128)(2,1)S(1)}, bf16[2,144,128]{2,1,0:T(8,128)(2,1)S(1)}, u32[]{:S(2)}, u32[]{:S(2)}) %collective-permute-start.21) | collective-permute-done | bytes 73760 | tf_op jit(solution)/shard_map/ppermute | solution.py:374
  174.0 2.5 %collective-permute-done.20.refs_2_ = bf16[2,144,128]{2,1,0:T(8,128)(2,1)S(1)} collective-permute-done((bf16[2,144,128]{2,1,0:T(8,128)(2,1)S(1)}, bf16[2,144,128]{2,1,0:T(8,128)(2,1)S(1)}, u32[]{:S(2)}, u32[]{:S(2)}) %collective-permute-start.20) | collective-permute-done | bytes 73760 | tf_op jit(solution)/shard_map/ppermute | solution.py:374
  180.2 2.3 %collective-permute-start.24 = (f32[2,128,128]{2,1,0:T(8,128)}, f32[2,128,128]{2,1,0:T(8,128)S(1)}, u32[]{:S(2)}, u32[]{:S(2)}) collective-permute-start(f32[2,128,128]{2,1,0:T(8,128)} %get-tuple-element.85), channel_id=1, source_target_pairs={{0,4},{1,5},{2,6},{3,7},{4,0},{5,1},{6,2},{7,3},{8,12},{9,13},{10,... | collective-permute-start | bytes 393224 | tf_op jit(solution)/shard_map/ppermute | solution.py:374
  184.2 3.3 %collective-permute-done.24.refs_3_ = f32[2,128,128]{2,1,0:T(8,128)S(1)} collective-permute-done((f32[2,128,128]{2,1,0:T(8,128)}, f32[2,128,128]{2,1,0:T(8,128)S(1)}, u32[]{:S(2)}, u32[]{:S(2)}) %collective-permute-start.24) | collective-permute-done | bytes 131104 | tf_op jit(solution)/shard_map/ppermute | solution.py:374
  189.7 2.5 %collective-permute-start.26 = (f32[8,128,128]{2,1,0:T(8,128)S(1)}, f32[8,128,128]{2,1,0:T(8,128)S(1)}, u32[]{:S(2)}, u32[]{:S(2)}) collective-permute-start(f32[8,128,128]{2,1,0:T(8,128)S(1)} %get-tuple-element.89), channel_id=1, source_target_pairs={{0,1},{1,0},{2,3},{3,2},{4,5},{5,4},{6,7},{7,6},{8,9},{9,8},{10,11... | collective-permute-start | bytes 1572872 | tf_op jit(solution)/shard_map/ppermute | solution.py:374
  193.8 2.4 %final_kernel.1 = (bf16[2,128,1024]{2,1,0:T(8,128)(2,1)}, bf16[2,128,1024]{2,1,0:T(8,128)(2,1)}) custom-call(s32[3]{0:T(128)S(1)} %pad_add_fusion.refs_0_, s32[2]{0:T(128)S(1)} %dynamic_slice.9.refs_1_, f32[2,8,128]{2,1,0:T(8,128)S(1)} %copy-done.28, bf16[2,128,1024]{2,1,0:T(8,128)(2,1)S(1)} %copy-done, bf16[2,128,1024]{2,1,0:T(8,128)(2,1)S(1)} %copy-done.1, ...), custom_call_target="tpu_custom_call" | custom-call | tf_op jit(solution)/shard_map/final_kernel/pallas_call | solution.py:80
  (117 shorter events, 56.1 us)
Async XLA Ops:
  5.0 33.0 %all-to-all-start = ((bf16[4,3,2,32,1024]{4,3,2,1,0:T(8,128)(2,1)}), bf16[4,3,2,32,1024]{4,3,2,1,0:T(8,128)(2,1)S(1)}, u32[]{:S(2)}, u32[]{:S(2)}) async-start(bf16[4,3,2,32,1024]{4,3,2,1,0:T(8,128)(2,1)} %pack_kernel.1.refs_5_), calls=%async_computation | async-start | bytes 3145728 | tf_op jit(solution)/shard_map/all_to_all | solution.py:361
  12.1 24.6 %copy-start.6 = (f32[8,136,128]{2,1,0:T(8,128)}, f32[8,136,128]{2,1,0:T(8,128)S(1)}, u32[]{:S(2)}) copy-start(f32[8,136,128]{2,1,0:T(8,128)S(1)} %get-tuple-element.49.refs_1_.refs_5_) | copy-start | bytes 1671172
  12.1 3.5 %collective-permute-start = (f32[8,136,128]{2,1,0:T(8,128)S(1)}, f32[8,136,128]{2,1,0:T(8,128)S(1)}, u32[]{:S(2)}, u32[]{:S(2)}) collective-permute-start(f32[8,136,128]{2,1,0:T(8,128)S(1)} %get-tuple-element.50), channel_id=1, source_target_pairs={{0,1},{1,0},{2,3},{3,2},{4,5},{5,4},{6,7},{7,6},{8,9},{9,8},{10,11... | collective-permute-start | bytes 1671176 | tf_op jit(solution)/shard_map/ppermute | solution.py:374
  17.1 6.1 %collective-permute-start.1 = (f32[2,136,128]{2,1,0:T(8,128)S(1)}, f32[2,136,128]{2,1,0:T(8,128)S(1)}, u32[]{:S(2)}, u32[]{:S(2)}) collective-permute-start(f32[2,136,128]{2,1,0:T(8,128)S(1)} %get-tuple-element.52), channel_id=1, source_target_pairs={{0,2},{1,3},{2,4},{3,5},{4,6},{5,7},{6,0},{7,1},{8,10},{9,11},{10,... | collective-permute-start | bytes 417800 | tf_op jit(solution)/shard_map/ppermute | solution.py:374
  17.4 8.9 %collective-permute-start.2 = (f32[2,136,128]{2,1,0:T(8,128)S(1)}, f32[2,136,128]{2,1,0:T(8,128)S(1)}, u32[]{:S(2)}, u32[]{:S(2)}) collective-permute-start(f32[2,136,128]{2,1,0:T(8,128)S(1)} %get-tuple-element.53), channel_id=1, source_target_pairs={{0,4},{1,5},{2,6},{3,7},{4,0},{5,1},{6,2},{7,3},{8,12},{9,13},{10,... | collective-permute-start | bytes 417800 | tf_op jit(solution)/shard_map/ppermute | solution.py:374
  19.9 6.6 %collective-permute-start.3 = (f32[2,136,128]{2,1,0:T(8,128)S(1)}, f32[2,136,128]{2,1,0:T(8,128)S(1)}, u32[]{:S(2)}, u32[]{:S(2)}) collective-permute-start(f32[2,136,128]{2,1,0:T(8,128)S(1)} %get-tuple-element.54), channel_id=1, source_target_pairs={{0,6},{1,7},{2,0},{3,1},{4,2},{5,3},{6,4},{7,5},{8,14},{9,15},{10,... | collective-permute-start | bytes 417800 | tf_op jit(solution)/shard_map/ppermute | solution.py:374
  27.1 9.6 %collective-permute-start.6 = (bf16[2,144,128]{2,1,0:T(8,128)(2,1)S(1)}, bf16[2,144,128]{2,1,0:T(8,128)(2,1)S(1)}, u32[]{:S(2)}, u32[]{:S(2)}) collective-permute-start(bf16[2,144,128]{2,1,0:T(8,128)(2,1)S(1)} %get-tuple-element.56), channel_id=1, source_target_pairs={{0,8},{1,9},{2,10},{3,11},{4,12},{5,13},{6,14},{7,15},{8,16},{9,17... | collective-permute-start | bytes 221192 | tf_op jit(solution)/shard_map/ppermute | solution.py:374
  30.5 6.3 %collective-permute-start.5 = (bf16[2,144,128]{2,1,0:T(8,128)(2,1)S(1)}, bf16[2,144,128]{2,1,0:T(8,128)(2,1)S(1)}, u32[]{:S(2)}, u32[]{:S(2)}) collective-permute-start(bf16[2,144,128]{2,1,0:T(8,128)(2,1)S(1)} %get-tuple-element.56), channel_id=1, source_target_pairs={{0,16},{1,17},{2,18},{3,19},{4,20},{5,21},{6,22},{7,23},{8,24},{9,... | collective-permute-start | bytes 221192 | tf_op jit(solution)/shard_map/ppermute | solution.py:374
  35.4 2.7 %collective-permute-start.4 = (bf16[2,144,128]{2,1,0:T(8,128)(2,1)S(1)}, bf16[2,144,128]{2,1,0:T(8,128)(2,1)S(1)}, u32[]{:S(2)}, u32[]{:S(2)}) collective-permute-start(bf16[2,144,128]{2,1,0:T(8,128)(2,1)S(1)} %get-tuple-element.56), channel_id=1, source_target_pairs={{0,24},{1,25},{2,26},{3,27},{4,28},{5,29},{6,30},{7,31},{32,56},{3... | collective-permute-start | bytes 221192 | tf_op jit(solution)/shard_map/ppermute | solution.py:374
  39.8 5.1 %collective-permute-start.7 = (f32[2,128,128]{2,1,0:T(8,128)S(1)}, f32[2,128,128]{2,1,0:T(8,128)S(1)}, u32[]{:S(2)}, u32[]{:S(2)}) collective-permute-start(f32[2,128,128]{2,1,0:T(8,128)S(1)} %get-tuple-element.58), channel_id=1, source_target_pairs={{0,2},{1,3},{2,4},{3,5},{4,6},{5,7},{6,0},{7,1},{8,10},{9,11},{10,... | collective-permute-start | bytes 393224 | tf_op jit(solution)/shard_map/ppermute | solution.py:374
  40.9 6.0 %collective-permute-start.8 = (f32[2,128,128]{2,1,0:T(8,128)S(1)}, f32[2,128,128]{2,1,0:T(8,128)S(1)}, u32[]{:S(2)}, u32[]{:S(2)}) collective-permute-start(f32[2,128,128]{2,1,0:T(8,128)S(1)} %get-tuple-element.59), channel_id=1, source_target_pairs={{0,4},{1,5},{2,6},{3,7},{4,0},{5,1},{6,2},{7,3},{8,12},{9,13},{10,... | collective-permute-start | bytes 393224 | tf_op jit(solution)/shard_map/ppermute | solution.py:374
  43.1 4.1 %collective-permute-start.9 = (f32[2,128,128]{2,1,0:T(8,128)S(1)}, f32[2,128,128]{2,1,0:T(8,128)S(1)}, u32[]{:S(2)}, u32[]{:S(2)}) collective-permute-start(f32[2,128,128]{2,1,0:T(8,128)S(1)} %get-tuple-element.60), channel_id=1, source_target_pairs={{0,6},{1,7},{2,0},{3,1},{4,2},{5,3},{6,4},{7,5},{8,14},{9,15},{10,... | collective-permute-start | bytes 393224 | tf_op jit(solution)/shard_map/ppermute | solution.py:374
  49.0 10.2 %collective-permute-start.10 = (f32[8,128,128]{2,1,0:T(8,128)S(1)}, f32[8,128,128]{2,1,0:T(8,128)S(1)}, u32[]{:S(2)}, u32[]{:S(2)}) collective-permute-start(f32[8,128,128]{2,1,0:T(8,128)S(1)} %get-tuple-element.62), channel_id=1, source_target_pairs={{0,1},{1,0},{2,3},{3,2},{4,5},{5,4},{6,7},{7,6},{8,9},{9,8},{10,11... | collective-permute-start | bytes 1572872 | tf_op jit(solution)/shard_map/ppermute | solution.py:374
  53.9 18.6 %collective-permute-start.11 = (bf16[4,1,2,32,1024]{4,3,2,1,0:T(8,128)(2,1)}, bf16[4,1,2,32,1024]{4,3,2,1,0:T(8,128)(2,1)}, u32[]{:S(2)}, u32[]{:S(2)}) collective-permute-start(bf16[4,1,2,32,1024]{4,3,2,1,0:T(8,128)(2,1)} %get-tuple-element.94), channel_id=1, source_target_pairs={{0,128},{32,160},{64,192},{96,224},{128,0},{160,32},{192,64},{224,... | collective-permute-start | bytes 1572872 | tf_op jit(solution)/shard_map/ppermute | solution.py:365
  58.1 26.7 %collective-permute-start.12 = (bf16[4,1,2,32,1024]{4,3,2,1,0:T(8,128)(2,1)}, bf16[4,1,2,32,1024]{4,3,2,1,0:T(8,128)(2,1)}, u32[]{:S(2)}, u32[]{:S(2)}) collective-permute-start(bf16[4,1,2,32,1024]{4,3,2,1,0:T(8,128)(2,1)} %get-tuple-element.93), channel_id=1, source_target_pairs={{0,128},{32,160},{64,192},{96,224},{128,0},{160,32},{192,64},{224,... | collective-permute-start | bytes 1572872 | tf_op jit(solution)/shard_map/ppermute | solution.py:365
  64.6 21.0 %all-to-all-start.1 = ((bf16[4,1,2,32,1024]{4,3,2,1,0:T(8,128)(2,1)}), bf16[4,1,2,32,1024]{4,3,2,1,0:T(8,128)(2,1)}, u32[]{:S(2)}, u32[]{:S(2)}) async-start(bf16[4,1,2,32,1024]{4,3,2,1,0:T(8,128)(2,1)} %copy-done.23), calls=%async_computation.1 | async-start | bytes 1048576 | tf_op jit(solution)/shard_map/all_to_all | solution.py:361
  74.4 11.2 %collective-permute-start.13 = (f32[2,16,256]{2,1,0:T(8,128)S(1)}, f32[2,16,256]{2,1,0:T(8,128)S(1)}, u32[]{:S(2)}, u32[]{:S(2)}) collective-permute-start(f32[2,16,256]{2,1,0:T(8,128)S(1)} %stats_kernel.1.refs_5_), channel_id=1, source_target_pairs={{0,128},{32,160},{64,192},{96,224},{128,0},{160,32},{192,64},{224,... | collective-permute-start | bytes 98312 | tf_op jit(solution)/shard_map/ppermute | solution.py:365
  90.2 39.9 %copy-start.15 = (f32[2,128,1024]{2,1,0:T(8,128)S(1)}, f32[2,128,1024]{2,1,0:T(8,128)}, u32[]{:S(2)}) copy-start(f32[2,128,1024]{2,1,0:T(8,128)} %copy-done.14) | copy-start | bytes 3145732
  90.2 20.8 %collective-permute-start.14 = (f32[16,256]{1,0:T(8,128)S(1)}, f32[16,256]{1,0:T(8,128)S(1)}, u32[]{:S(2)}, u32[]{:S(2)}) collective-permute-start(f32[16,256]{1,0:T(8,128)S(1)} %get-tuple-element.67.refs_8_), channel_id=1, source_target_pairs={{0,128},{32,160},{64,192},{96,224},{128,0},{160,32},{192,64},{224,... | collective-permute-start | bytes 49160 | tf_op jit(solution)/shard_map/ppermute | solution.py:365
  116.0 21.4 %collective-permute-start.16 = (bf16[4,1,2,32,1024]{4,3,2,1,0:T(8,128)(2,1)S(1)}, bf16[4,1,2,32,1024]{4,3,2,1,0:T(8,128)(2,1)S(1)}, u32[]{:S(2)}, u32[]{:S(2)}) collective-permute-start(bf16[4,1,2,32,1024]{4,3,2,1,0:T(8,128)(2,1)S(1)} %get-tuple-element.68.refs_6_), channel_id=1, source_target_pairs={{0,128},{32,160},{64,192},{96,224},{128,0},{160,32},{192,64},{224,... | collective-permute-start | bytes 1572872 | tf_op jit(solution)/shard_map/ppermute | solution.py:365
  135.5 6.8 %collective-permute-start.15 = (f32[8,136,128]{2,1,0:T(8,128)}, f32[8,136,128]{2,1,0:T(8,128)}, u32[]{:S(2)}, u32[]{:S(2)}) collective-permute-start(f32[8,136,128]{2,1,0:T(8,128)} %get-tuple-element.71), channel_id=1, source_target_pairs={{0,1},{1,0},{2,3},{3,2},{4,5},{5,4},{6,7},{7,6},{8,9},{9,8},{10,11... | collective-permute-start | bytes 1671176 | tf_op jit(solution)/shard_map/ppermute | solution.py:374
  138.6 44.0 %all-to-all-start.3 = ((bf16[4,2,2,32,1024]{4,3,2,1,0:T(8,128)(2,1)}), bf16[4,2,2,32,1024]{4,3,2,1,0:T(8,128)(2,1)S(1)}, u32[]{:S(2)}, u32[]{:S(2)}) async-start(bf16[4,2,2,32,1024]{4,3,2,1,0:T(8,128)(2,1)} %join_kernel.1.refs_3_), calls=%async_computation.3 | async-start | bytes 2097152 | tf_op jit(solution)/shard_map/all_to_all | solution.py:361
  144.5 6.6 %collective-permute-start.17 = (f32[2,136,128]{2,1,0:T(8,128)S(1)}, f32[2,136,128]{2,1,0:T(8,128)S(1)}, u32[]{:S(2)}, u32[]{:S(2)}) collective-permute-start(f32[2,136,128]{2,1,0:T(8,128)S(1)} %get-tuple-element.75), channel_id=1, source_target_pairs={{0,2},{1,3},{2,4},{3,5},{4,6},{5,7},{6,0},{7,1},{8,10},{9,11},{10,... | collective-permute-start | bytes 417800 | tf_op jit(solution)/shard_map/ppermute | solution.py:374
  145.9 9.0 %collective-permute-start.18 = (f32[2,136,128]{2,1,0:T(8,128)S(1)}, f32[2,136,128]{2,1,0:T(8,128)S(1)}, u32[]{:S(2)}, u32[]{:S(2)}) collective-permute-start(f32[2,136,128]{2,1,0:T(8,128)S(1)} %get-tuple-element.76), channel_id=1, source_target_pairs={{0,4},{1,5},{2,6},{3,7},{4,0},{5,1},{6,2},{7,3},{8,12},{9,13},{10,... | collective-permute-start | bytes 417800 | tf_op jit(solution)/shard_map/ppermute | solution.py:374
  148.1 6.8 %collective-permute-start.19 = (f32[2,136,128]{2,1,0:T(8,128)S(1)}, f32[2,136,128]{2,1,0:T(8,128)S(1)}, u32[]{:S(2)}, u32[]{:S(2)}) collective-permute-start(f32[2,136,128]{2,1,0:T(8,128)S(1)} %get-tuple-element.77), channel_id=1, source_target_pairs={{0,6},{1,7},{2,0},{3,1},{4,2},{5,3},{6,4},{7,5},{8,14},{9,15},{10,... | collective-permute-start | bytes 417800 | tf_op jit(solution)/shard_map/ppermute | solution.py:374
  155.5 11.9 %collective-permute-start.22 = (bf16[2,144,128]{2,1,0:T(8,128)(2,1)S(1)}, bf16[2,144,128]{2,1,0:T(8,128)(2,1)S(1)}, u32[]{:S(2)}, u32[]{:S(2)}) collective-permute-start(bf16[2,144,128]{2,1,0:T(8,128)(2,1)S(1)} %get-tuple-element.82), channel_id=1, source_target_pairs={{8,0},{9,1},{10,2},{11,3},{12,4},{13,5},{14,6},{15,7},{16,8},{17,9... | collective-permute-start | bytes 221192 | tf_op jit(solution)/shard_map/ppermute | solution.py:374
  156.8 17.2 %collective-permute-start.21 = (bf16[2,144,128]{2,1,0:T(8,128)(2,1)S(1)}, bf16[2,144,128]{2,1,0:T(8,128)(2,1)S(1)}, u32[]{:S(2)}, u32[]{:S(2)}) collective-permute-start(bf16[2,144,128]{2,1,0:T(8,128)(2,1)S(1)} %get-tuple-element.82), channel_id=1, source_target_pairs={{16,0},{17,1},{18,2},{19,3},{20,4},{21,5},{22,6},{23,7},{24,8},{25... | collective-permute-start | bytes 221192 | tf_op jit(solution)/shard_map/ppermute | solution.py:374
  158.1 18.4 %collective-permute-start.20 = (bf16[2,144,128]{2,1,0:T(8,128)(2,1)S(1)}, bf16[2,144,128]{2,1,0:T(8,128)(2,1)S(1)}, u32[]{:S(2)}, u32[]{:S(2)}) collective-permute-start(bf16[2,144,128]{2,1,0:T(8,128)(2,1)S(1)} %get-tuple-element.82), channel_id=1, source_target_pairs={{24,0},{25,1},{26,2},{27,3},{28,4},{29,5},{30,6},{31,7},{56,32},{5... | collective-permute-start | bytes 221192 | tf_op jit(solution)/shard_map/ppermute | solution.py:374
  178.9 5.2 %collective-permute-start.23 = (f32[2,128,128]{2,1,0:T(8,128)}, f32[2,128,128]{2,1,0:T(8,128)S(1)}, u32[]{:S(2)}, u32[]{:S(2)}) collective-permute-start(f32[2,128,128]{2,1,0:T(8,128)} %get-tuple-element.84), channel_id=1, source_target_pairs={{0,2},{1,3},{2,4},{3,5},{4,6},{5,7},{6,0},{7,1},{8,10},{9,11},{10,... | collective-permute-start | bytes 393224 | tf_op jit(solution)/shard_map/ppermute | solution.py:374
  180.2 7.3 %collective-permute-start.24 = (f32[2,128,128]{2,1,0:T(8,128)}, f32[2,128,128]{2,1,0:T(8,128)S(1)}, u32[]{:S(2)}, u32[]{:S(2)}) collective-permute-start(f32[2,128,128]{2,1,0:T(8,128)} %get-tuple-element.85), channel_id=1, source_target_pairs={{0,4},{1,5},{2,6},{3,7},{4,0},{5,1},{6,2},{7,3},{8,12},{9,13},{10,... | collective-permute-start | bytes 393224 | tf_op jit(solution)/shard_map/ppermute | solution.py:374
  182.4 5.1 %collective-permute-start.25 = (f32[2,128,128]{2,1,0:T(8,128)S(1)}, f32[2,128,128]{2,1,0:T(8,128)S(1)}, u32[]{:S(2)}, u32[]{:S(2)}) collective-permute-start(f32[2,128,128]{2,1,0:T(8,128)S(1)} %get-tuple-element.86), channel_id=1, source_target_pairs={{0,6},{1,7},{2,0},{3,1},{4,2},{5,3},{6,4},{7,5},{8,14},{9,15},{10,... | collective-permute-start | bytes 393224 | tf_op jit(solution)/shard_map/ppermute | solution.py:374
  189.7 4.0 %collective-permute-start.26 = (f32[8,128,128]{2,1,0:T(8,128)S(1)}, f32[8,128,128]{2,1,0:T(8,128)S(1)}, u32[]{:S(2)}, u32[]{:S(2)}) collective-permute-start(f32[8,128,128]{2,1,0:T(8,128)S(1)} %get-tuple-element.89), channel_id=1, source_target_pairs={{0,1},{1,0},{2,3},{3,2},{4,5},{5,4},{6,7},{7,6},{8,9},{9,8},{10,11... | collective-permute-start | bytes 1572872 | tf_op jit(solution)/shard_map/ppermute | solution.py:374
  (28 other events, 163.7 us)

commit v4 on v3

--- a/solution.py
+++ b/solution.py
@@ -452,7 +452,7 @@
     starts = chip_starts(row, far, at, initial, False, (qkg,))
     qkg_, *_ = lax.optimization_barrier((qkg, *far))
     qx, gx = swap(qkg_[:, :1]), swap(qkg_[:, 2:])
-    states = core_starts(starts, mine, theirs, at, False)
+    states = core_starts(starts, mine, theirs, at, False, (qx,))
     out, normed = vmem_call(outputs_kernel, (whole, quarter), 2, 6)(at, own_valid, log_decay, q, k, v, *states)
     stats = vmem_call(stats_kernel, row_stats2, 1, 2)(half_valid, qkg, qx)
     stats_x = swap(stats)

time: 197 us -> 181 us (0.919)
  waiting for transfers between devices: 58.4 us -> 43.9 us
  local copies, waits for them, and re-layouts: 16 us -> 12.8 us
  starting transfers between devices: 68.7 us -> 71.1 us
    ppermute x5, waiting for transfers between devices: 26 us -> 15 us  [swap(): return lax.ppermute(x, 'track', SWAP)]
    ppermute x22, waiting for transfers between devices: 32.3 us -> 28.3 us  [over_tm(): return lax.ppermute(x, 'tm', pairs)]
    unnamed x60 -> x62, local copies, waits for them, and re-layouts: 14.6 us -> 11.6 us
  transfers between devices with their start and end apart: 30 -> 30, of which waited for: 20 -> 21; matrix products, arithmetic and copies ran while one was open for 1% -> 0% of each run, Pallas kernels for 12% -> 13%
where the time goes in v4:
time: 181 us; the launch traced here: 180 us
  starting transfers between devices  71.1 us (39%)
  waiting for transfers between devices  43.9 us (24%)
  Pallas kernels  38.5 us (21%)
  local copies, waits for them, and re-layouts  12.8 us (7%)
  blocking collectives  12.8 us (7%)
    ppermute x22, starting transfers between devices, over_tm(): return lax.ppermute(x, 'tm', pairs)  41.5 us
    pallas_call x19, Pallas kernels, vmem_call(): return lambda *args: call(*args, *after)  38.5 us
    ppermute x22, waiting for transfers between devices, over_tm(): return lax.ppermute(x, 'tm', pairs)  28.3 us
    ppermute x5, starting transfers between devices, swap(): return lax.ppermute(x, 'track', SWAP)  16.4 us
    ppermute x5, waiting for transfers between devices, swap(): return lax.ppermute(x, 'track', SWAP)  15 us
    all_to_all x3, starting transfers between devices, over_y(): return lax.all_to_all(x, 'track', 0, 0, axis_index_groups=YS, tiled=True)  13.2 us
    all_to_all x1, blocking collectives, over_y(): return lax.all_to_all(x, 'track', 0, 0, axis_index_groups=YS, tiled=True)  12.8 us
    unnamed x62, local copies, waits for them, and re-layouts  11.6 us
  transfers between devices with their start and end apart: 30, of which 21 were waited for; matrix products, arithmetic and copies ran while one was open for 0% of the time, Pallas kernels for 13%

profile of v4, /device:TPU:1, one launch (start us, length us, event | category | flops | bytes accessed | tf_op | source)
XLA Modules:
  0.0 180.2 jit_solution(8131629842053519151)
XLA Ops:
  5.0 5.2 %all-to-all-start = ((bf16[4,3,2,32,1024]{4,3,2,1,0:T(8,128)(2,1)}), bf16[4,3,2,32,1024]{4,3,2,1,0:T(8,128)(2,1)S(1)}, u32[]{:S(2)}, u32[]{:S(2)}) async-start(bf16[4,3,2,32,1024]{4,3,2,1,0:T(8,128)(2,1)} %pack_kernel.1.refs_5_), calls=%async_computation | async-start | bytes 3145728 | tf_op jit(solution)/shard_map/all_to_all | solution.py:361
  17.4 2.5 %collective-permute-start.2 = (f32[2,136,128]{2,1,0:T(8,128)S(1)}, f32[2,136,128]{2,1,0:T(8,128)S(1)}, u32[]{:S(2)}, u32[]{:S(2)}) collective-permute-start(f32[2,136,128]{2,1,0:T(8,128)S(1)} %get-tuple-element.53), channel_id=1, source_target_pairs={{0,4},{1,5},{2,6},{3,7},{4,0},{5,1},{6,2},{7,3},{8,12},{9,13},{10,... | collective-permute-start | bytes 417800 | tf_op jit(solution)/shard_map/ppermute | solution.py:374
  21.0 2.2 %collective-permute-done.1.refs_2_ = f32[2,136,128]{2,1,0:T(8,128)S(1)} collective-permute-done((f32[2,136,128]{2,1,0:T(8,128)S(1)}, f32[2,136,128]{2,1,0:T(8,128)S(1)}, u32[]{:S(2)}, u32[]{:S(2)}) %collective-permute-start.1) | collective-permute-done | bytes 139296 | tf_op jit(solution)/shard_map/ppermute | solution.py:374
  23.2 3.1 %collective-permute-done.2.refs_3_ = f32[2,136,128]{2,1,0:T(8,128)S(1)} collective-permute-done((f32[2,136,128]{2,1,0:T(8,128)S(1)}, f32[2,136,128]{2,1,0:T(8,128)S(1)}, u32[]{:S(2)}, u32[]{:S(2)}) %collective-permute-start.2) | collective-permute-done | bytes 139296 | tf_op jit(solution)/shard_map/ppermute | solution.py:374
  27.9 3.4 %collective-permute-start.6 = (bf16[2,144,128]{2,1,0:T(8,128)(2,1)S(1)}, bf16[2,144,128]{2,1,0:T(8,128)(2,1)S(1)}, u32[]{:S(2)}, u32[]{:S(2)}) collective-permute-start(bf16[2,144,128]{2,1,0:T(8,128)(2,1)S(1)} %get-tuple-element.56), channel_id=1, source_target_pairs={{0,8},{1,9},{2,10},{3,11},{4,12},{5,13},{6,14},{7,15},{8,16},{9,17... | collective-permute-start | bytes 221192 | tf_op jit(solution)/shard_map/ppermute | solution.py:374
  31.2 4.9 %collective-permute-start.5 = (bf16[2,144,128]{2,1,0:T(8,128)(2,1)S(1)}, bf16[2,144,128]{2,1,0:T(8,128)(2,1)S(1)}, u32[]{:S(2)}, u32[]{:S(2)}) collective-permute-start(bf16[2,144,128]{2,1,0:T(8,128)(2,1)S(1)} %get-tuple-element.56), channel_id=1, source_target_pairs={{0,16},{1,17},{2,18},{3,19},{4,20},{5,21},{6,22},{7,23},{8,24},{9,... | collective-permute-start | bytes 221192 | tf_op jit(solution)/shard_map/ppermute | solution.py:374
  39.7 4.2 %collective-permute-start.10 = (bf16[4,1,2,32,1024]{4,3,2,1,0:T(8,128)(2,1)S(1)}, bf16[4,1,2,32,1024]{4,3,2,1,0:T(8,128)(2,1)S(1)}, u32[]{:S(2)}, u32[]{:S(2)}) collective-permute-start(bf16[4,1,2,32,1024]{4,3,2,1,0:T(8,128)(2,1)S(1)} %get-tuple-element.94), channel_id=1, source_target_pairs={{0,128},{32,160},{64,192},{96,224},{128,0},{160,32},{192,64},{224,... | collective-permute-start | bytes 1572872 | tf_op jit(solution)/shard_map/ppermute | solution.py:365
  46.8 2.2 %collective-permute-start.8 = (f32[2,128,128]{2,1,0:T(8,128)S(1)}, f32[2,128,128]{2,1,0:T(8,128)S(1)}, u32[]{:S(2)}, u32[]{:S(2)}) collective-permute-start(f32[2,128,128]{2,1,0:T(8,128)S(1)} %get-tuple-element.59), channel_id=1, source_target_pairs={{0,4},{1,5},{2,6},{3,7},{4,0},{5,1},{6,2},{7,3},{8,12},{9,13},{10,... | collective-permute-start | bytes 393224 | tf_op jit(solution)/shard_map/ppermute | solution.py:374
  53.1 4.2 %collective-permute-done.10.refs_7_.refs_2_ = bf16[4,1,2,32,1024]{4,3,2,1,0:T(8,128)(2,1)S(1)} collective-permute-done((bf16[4,1,2,32,1024]{4,3,2,1,0:T(8,128)(2,1)S(1)}, bf16[4,1,2,32,1024]{4,3,2,1,0:T(8,128)(2,1)S(1)}, u32[]{:S(2)}, u32[]{:S(2)}) %collective-permute-start.10) | collective-permute-done | bytes 524320 | tf_op jit(solution)/shard_map/ppermute | solution.py:365
  58.0 4.6 %collective-permute-start.11 = (f32[8,128,128]{2,1,0:T(8,128)S(1)}, f32[8,128,128]{2,1,0:T(8,128)S(1)}, u32[]{:S(2)}, u32[]{:S(2)}) collective-permute-start(f32[8,128,128]{2,1,0:T(8,128)S(1)} %get-tuple-element.63), channel_id=1, source_target_pairs={{0,1},{1,0},{2,3},{3,2},{4,5},{5,4},{6,7},{7,6},{8,9},{9,8},{10,11... | collective-permute-start | bytes 1572872 | tf_op jit(solution)/shard_map/ppermute | solution.py:374
  62.6 3.6 %collective-permute-start.12 = (bf16[4,1,2,32,1024]{4,3,2,1,0:T(8,128)(2,1)}, bf16[4,1,2,32,1024]{4,3,2,1,0:T(8,128)(2,1)}, u32[]{:S(2)}, u32[]{:S(2)}) collective-permute-start(bf16[4,1,2,32,1024]{4,3,2,1,0:T(8,128)(2,1)} %get-tuple-element.93), channel_id=1, source_target_pairs={{0,128},{32,160},{64,192},{96,224},{128,0},{160,32},{192,64},{224,... | collective-permute-start | bytes 1572872 | tf_op jit(solution)/shard_map/ppermute | solution.py:365
  66.3 2.7 %outputs_kernel.1 = (f32[2,128,1024]{2,1,0:T(8,128)S(1)}, bf16[4,1,2,32,1024]{4,3,2,1,0:T(8,128)(2,1)S(1)}) custom-call(s32[3]{0:T(128)S(1)} %pad_add_fusion.refs_0_, s32[2]{0:T(128)S(1)} %dynamic_slice.9.refs_1_, f32[2,8,128]{2,1,0:T(8,128)S(1)} %copy-done.29, bf16[2,128,1024]{2,1,0:T(8,128)(2,1)S(1)} %copy-done.2, bf16[2,128,1024]{2,1,0:T(8,128)(2,1)S(1)} %copy-done, ...), custom_call_target="tpu_custom_call" | custom-call | tf_op jit(solution)/shard_map/outputs_kernel/pallas_call | solution.py:80
  70.8 4.5 %all-to-all-start.1 = ((bf16[4,1,2,32,1024]{4,3,2,1,0:T(8,128)(2,1)}), bf16[4,1,2,32,1024]{4,3,2,1,0:T(8,128)(2,1)}, u32[]{:S(2)}, u32[]{:S(2)}) async-start(bf16[4,1,2,32,1024]{4,3,2,1,0:T(8,128)(2,1)} %copy-done.24), calls=%async_computation.1 | async-start | bytes 1048576 | tf_op jit(solution)/shard_map/all_to_all | solution.py:361
  76.9 2.0 %collective-permute-start.13 = (f32[2,16,256]{2,1,0:T(8,128)S(1)}, f32[2,16,256]{2,1,0:T(8,128)S(1)}, u32[]{:S(2)}, u32[]{:S(2)}) collective-permute-start(f32[2,16,256]{2,1,0:T(8,128)S(1)} %stats_kernel.1.refs_5_), channel_id=1, source_target_pairs={{0,128},{32,160},{64,192},{96,224},{128,0},{160,32},{192,64},{224,... | collective-permute-start | bytes 98312 | tf_op jit(solution)/shard_map/ppermute | solution.py:365
  79.1 4.4 %collective-permute-done.12.refs_3_ = bf16[4,1,2,32,1024]{4,3,2,1,0:T(8,128)(2,1)} collective-permute-done((bf16[4,1,2,32,1024]{4,3,2,1,0:T(8,128)(2,1)}, bf16[4,1,2,32,1024]{4,3,2,1,0:T(8,128)(2,1)}, u32[]{:S(2)}, u32[]{:S(2)}) %collective-permute-start.12) | collective-permute-done | bytes 524320 | tf_op jit(solution)/shard_map/ppermute | solution.py:365
  84.4 4.4 %mix_kernel.1 = (bf16[4,1,2,32,1024]{4,3,2,1,0:T(8,128)(2,1)S(1)}, f32[16,256]{1,0:T(8,128)S(1)}) custom-call(s32[8]{0:T(128)S(1)} %get-tuple-element.96.refs_0_, bf16[4,3,2,32,1024]{4,3,2,1,0:T(8,128)(2,1)S(1)} %all-to-all-done.refs_6_.refs_1_, bf16[4,1,2,32,1024]{4,3,2,1,0:T(8,128)(2,1)S(1)} %collective-permute-done.10.refs_7_.refs_2_, ...), custom_call_target="tpu_custom_call" | custom-call | tf_op jit(solution)/shard_map/mix_kernel/pallas_call | solution.py:80
  90.7 6.1 %collective-permute-done.14.refs_9_ = f32[16,256]{1,0:T(8,128)S(1)} collective-permute-done((f32[16,256]{1,0:T(8,128)S(1)}, f32[16,256]{1,0:T(8,128)S(1)}, u32[]{:S(2)}, u32[]{:S(2)}) %collective-permute-start.14) | collective-permute-done | bytes 16416 | tf_op jit(solution)/shard_map/ppermute | solution.py:365
  96.8 4.8 %cross_grads_kernel.1 = (bf16[4,1,2,32,1024]{4,3,2,1,0:T(8,128)(2,1)S(1)}, f32[4,1,2,32,1024]{4,3,2,1,0:T(8,128)S(1)}, bf16[4,1,2,32,1024]{4,3,2,1,0:T(8,128)(2,1)S(1)}) custom-call(s32[8]{0:T(128)S(1)} %get-tuple-element.96.refs_0_, bf16[4,3,2,32,1024]{4,3,2,1,0:T(8,128)(2,1)S(1)} %all-to-all-done.refs_6_.refs_1_, ...), custom_call_target="tpu_custom_call" | custom-call | tf_op jit(solution)/shard_map/cross_grads_kernel/pallas_call | solution.py:80
  101.7 4.7 %collective-permute-start.16 = (bf16[4,1,2,32,1024]{4,3,2,1,0:T(8,128)(2,1)S(1)}, bf16[4,1,2,32,1024]{4,3,2,1,0:T(8,128)(2,1)S(1)}, u32[]{:S(2)}, u32[]{:S(2)}) collective-permute-start(bf16[4,1,2,32,1024]{4,3,2,1,0:T(8,128)(2,1)S(1)} %get-tuple-element.68.refs_6_), channel_id=1, source_target_pairs={{0,128},{32,160},{64,192},{96,224},{128,0},{160,32},{192,64},{224,... | collective-permute-start | bytes 1572872 | tf_op jit(solution)/shard_map/ppermute | solution.py:365
  106.3 12.8 %all_to_all.20.refs_5_ = bf16[4,1,2,32,1024]{4,3,2,1,0:T(8,128)(2,1)S(1)} all-to-all(bf16[4,1,2,32,1024]{4,3,2,1,0:T(8,128)(2,1)S(1)} %get-tuple-element.66), channel_id=1, replica_groups={{0,32,64,96},{128,160,192,224},{1,33,65,97},{129,161,193,225},{2,34,66,..., dimensions={0} | all-to-all | bytes 1048576 | tf_op jit(solution)/shard_map/all_to_all | solution.py:361
  119.1 3.6 %grad_outputs_kernel.1 = (f32[2,128,1024]{2,1,0:T(8,128)S(1)}, f32[8,136,128]{2,1,0:T(8,128)S(1)}, f32[8,136,128]{2,1,0:T(8,128)}) custom-call(s32[3]{0:T(128)S(1)} %pad_add_fusion.refs_0_, s32[2]{0:T(128)S(1)} %dynamic_slice.9.refs_1_, f32[2,8,128]{2,1,0:T(8,128)S(1)} %copy-done.29, bf16[2,128,1024]{2,1,0:T(8,128)(2,1)S(1)} %copy-done.3, ...), custom_call_target="tpu_custom_call" | custom-call | tf_op jit(solution)/shard_map/grad_outputs_kernel/pallas_call | solution.py:80
  126.8 3.5 %all-to-all-start.3 = ((bf16[4,2,2,32,1024]{4,3,2,1,0:T(8,128)(2,1)}), bf16[4,2,2,32,1024]{4,3,2,1,0:T(8,128)(2,1)S(1)}, u32[]{:S(2)}, u32[]{:S(2)}) async-start(bf16[4,2,2,32,1024]{4,3,2,1,0:T(8,128)(2,1)} %join_kernel.1.refs_3_), calls=%async_computation.3 | async-start | bytes 2097152 | tf_op jit(solution)/shard_map/all_to_all | solution.py:361
  132.7 2.2 %collective-permute-start.18 = (f32[2,136,128]{2,1,0:T(8,128)S(1)}, f32[2,136,128]{2,1,0:T(8,128)S(1)}, u32[]{:S(2)}, u32[]{:S(2)}) collective-permute-start(f32[2,136,128]{2,1,0:T(8,128)S(1)} %get-tuple-element.76), channel_id=1, source_target_pairs={{0,4},{1,5},{2,6},{3,7},{4,0},{5,1},{6,2},{7,3},{8,12},{9,13},{10,... | collective-permute-start | bytes 417800 | tf_op jit(solution)/shard_map/ppermute | solution.py:374
  135.8 2.4 %collective-permute-done.17.refs_2_ = f32[2,136,128]{2,1,0:T(8,128)S(1)} collective-permute-done((f32[2,136,128]{2,1,0:T(8,128)S(1)}, f32[2,136,128]{2,1,0:T(8,128)S(1)}, u32[]{:S(2)}, u32[]{:S(2)}) %collective-permute-start.17) | collective-permute-done | bytes 139296 | tf_op jit(solution)/shard_map/ppermute | solution.py:374
  138.2 3.5 %collective-permute-done.18.refs_3_ = f32[2,136,128]{2,1,0:T(8,128)S(1)} collective-permute-done((f32[2,136,128]{2,1,0:T(8,128)S(1)}, f32[2,136,128]{2,1,0:T(8,128)S(1)}, u32[]{:S(2)}, u32[]{:S(2)}) %collective-permute-start.18) | collective-permute-done | bytes 139296 | tf_op jit(solution)/shard_map/ppermute | solution.py:374
  146.5 6.8 %local_grads_kernel.1 = (bf16[2,128,1024]{2,1,0:T(8,128)(2,1)}, f32[2,128,1024]{2,1,0:T(8,128)S(1)}, f32[2,128,1024]{2,1,0:T(8,128)S(1)}) custom-call(s32[3]{0:T(128)S(1)} %pad_add_fusion.refs_0_, s32[2]{0:T(128)S(1)} %dynamic_slice.9.refs_1_, f32[2,8,128]{2,1,0:T(8,128)S(1)} %copy-done.29, bf16[2,128,1024]{2,1,0:T(8,128)(2,1)S(1)} %copy-done.4, ...), custom_call_target="tpu_custom_call" | custom-call | tf_op jit(solution)/shard_map/local_grads_kernel/pallas_call | solution.py:80
  154.3 3.5 %collective-permute-done.21.refs_3_ = bf16[2,144,128]{2,1,0:T(8,128)(2,1)S(1)} collective-permute-done((bf16[2,144,128]{2,1,0:T(8,128)(2,1)S(1)}, bf16[2,144,128]{2,1,0:T(8,128)(2,1)S(1)}, u32[]{:S(2)}, u32[]{:S(2)}) %collective-permute-start.21) | collective-permute-done | bytes 73760 | tf_op jit(solution)/shard_map/ppermute | solution.py:374
  162.1 2.1 %collective-permute-start.23 = (f32[2,128,128]{2,1,0:T(8,128)}, f32[2,128,128]{2,1,0:T(8,128)S(1)}, u32[]{:S(2)}, u32[]{:S(2)}) collective-permute-start(f32[2,128,128]{2,1,0:T(8,128)} %get-tuple-element.84), channel_id=1, source_target_pairs={{0,2},{1,3},{2,4},{3,5},{4,6},{5,7},{6,0},{7,1},{8,10},{9,11},{10,... | collective-permute-start | bytes 393224 | tf_op jit(solution)/shard_map/ppermute | solution.py:374
  164.2 2.2 %collective-permute-start.24 = (f32[2,128,128]{2,1,0:T(8,128)}, f32[2,128,128]{2,1,0:T(8,128)S(1)}, u32[]{:S(2)}, u32[]{:S(2)}) collective-permute-start(f32[2,128,128]{2,1,0:T(8,128)} %get-tuple-element.85), channel_id=1, source_target_pairs={{0,4},{1,5},{2,6},{3,7},{4,0},{5,1},{6,2},{7,3},{8,12},{9,13},{10,... | collective-permute-start | bytes 393224 | tf_op jit(solution)/shard_map/ppermute | solution.py:374
  167.8 3.8 %collective-permute-done.24.refs_3_ = f32[2,128,128]{2,1,0:T(8,128)S(1)} collective-permute-done((f32[2,128,128]{2,1,0:T(8,128)}, f32[2,128,128]{2,1,0:T(8,128)S(1)}, u32[]{:S(2)}, u32[]{:S(2)}) %collective-permute-start.24) | collective-permute-done | bytes 131104 | tf_op jit(solution)/shard_map/ppermute | solution.py:374
  173.8 2.4 %collective-permute-start.26 = (f32[8,128,128]{2,1,0:T(8,128)S(1)}, f32[8,128,128]{2,1,0:T(8,128)S(1)}, u32[]{:S(2)}, u32[]{:S(2)}) collective-permute-start(f32[8,128,128]{2,1,0:T(8,128)S(1)} %get-tuple-element.89), channel_id=1, source_target_pairs={{0,1},{1,0},{2,3},{3,2},{4,5},{5,4},{6,7},{7,6},{8,9},{9,8},{10,11... | collective-permute-start | bytes 1572872 | tf_op jit(solution)/shard_map/ppermute | solution.py:374
  177.8 2.4 %final_kernel.1 = (bf16[2,128,1024]{2,1,0:T(8,128)(2,1)}, bf16[2,128,1024]{2,1,0:T(8,128)(2,1)}) custom-call(s32[3]{0:T(128)S(1)} %pad_add_fusion.refs_0_, s32[2]{0:T(128)S(1)} %dynamic_slice.9.refs_1_, f32[2,8,128]{2,1,0:T(8,128)S(1)} %copy-done.29, bf16[2,128,1024]{2,1,0:T(8,128)(2,1)S(1)} %copy-done, bf16[2,128,1024]{2,1,0:T(8,128)(2,1)S(1)} %copy-done.1, ...), custom_call_target="tpu_custom_call" | custom-call | tf_op jit(solution)/shard_map/final_kernel/pallas_call | solution.py:80
  (119 shorter events, 54.3 us)
Async XLA Ops:
  5.0 33.8 %all-to-all-start = ((bf16[4,3,2,32,1024]{4,3,2,1,0:T(8,128)(2,1)}), bf16[4,3,2,32,1024]{4,3,2,1,0:T(8,128)(2,1)S(1)}, u32[]{:S(2)}, u32[]{:S(2)}) async-start(bf16[4,3,2,32,1024]{4,3,2,1,0:T(8,128)(2,1)} %pack_kernel.1.refs_5_), calls=%async_computation | async-start | bytes 3145728 | tf_op jit(solution)/shard_map/all_to_all | solution.py:361
  12.1 3.5 %collective-permute-start = (f32[8,136,128]{2,1,0:T(8,128)S(1)}, f32[8,136,128]{2,1,0:T(8,128)S(1)}, u32[]{:S(2)}, u32[]{:S(2)}) collective-permute-start(f32[8,136,128]{2,1,0:T(8,128)S(1)} %get-tuple-element.50), channel_id=1, source_target_pairs={{0,1},{1,0},{2,3},{3,2},{4,5},{5,4},{6,7},{7,6},{8,9},{9,8},{10,11... | collective-permute-start | bytes 1671176 | tf_op jit(solution)/shard_map/ppermute | solution.py:374
  17.1 6.1 %collective-permute-start.1 = (f32[2,136,128]{2,1,0:T(8,128)S(1)}, f32[2,136,128]{2,1,0:T(8,128)S(1)}, u32[]{:S(2)}, u32[]{:S(2)}) collective-permute-start(f32[2,136,128]{2,1,0:T(8,128)S(1)} %get-tuple-element.52), channel_id=1, source_target_pairs={{0,2},{1,3},{2,4},{3,5},{4,6},{5,7},{6,0},{7,1},{8,10},{9,11},{10,... | collective-permute-start | bytes 417800 | tf_op jit(solution)/shard_map/ppermute | solution.py:374
  17.4 8.9 %collective-permute-start.2 = (f32[2,136,128]{2,1,0:T(8,128)S(1)}, f32[2,136,128]{2,1,0:T(8,128)S(1)}, u32[]{:S(2)}, u32[]{:S(2)}) collective-permute-start(f32[2,136,128]{2,1,0:T(8,128)S(1)} %get-tuple-element.53), channel_id=1, source_target_pairs={{0,4},{1,5},{2,6},{3,7},{4,0},{5,1},{6,2},{7,3},{8,12},{9,13},{10,... | collective-permute-start | bytes 417800 | tf_op jit(solution)/shard_map/ppermute | solution.py:374
  19.8 6.6 %collective-permute-start.3 = (f32[2,136,128]{2,1,0:T(8,128)S(1)}, f32[2,136,128]{2,1,0:T(8,128)S(1)}, u32[]{:S(2)}, u32[]{:S(2)}) collective-permute-start(f32[2,136,128]{2,1,0:T(8,128)S(1)} %get-tuple-element.54), channel_id=1, source_target_pairs={{0,6},{1,7},{2,0},{3,1},{4,2},{5,3},{6,4},{7,5},{8,14},{9,15},{10,... | collective-permute-start | bytes 417800 | tf_op jit(solution)/shard_map/ppermute | solution.py:374
  27.9 9.6 %collective-permute-start.6 = (bf16[2,144,128]{2,1,0:T(8,128)(2,1)S(1)}, bf16[2,144,128]{2,1,0:T(8,128)(2,1)S(1)}, u32[]{:S(2)}, u32[]{:S(2)}) collective-permute-start(bf16[2,144,128]{2,1,0:T(8,128)(2,1)S(1)} %get-tuple-element.56), channel_id=1, source_target_pairs={{0,8},{1,9},{2,10},{3,11},{4,12},{5,13},{6,14},{7,15},{8,16},{9,17... | collective-permute-start | bytes 221192 | tf_op jit(solution)/shard_map/ppermute | solution.py:374
  31.2 6.3 %collective-permute-start.5 = (bf16[2,144,128]{2,1,0:T(8,128)(2,1)S(1)}, bf16[2,144,128]{2,1,0:T(8,128)(2,1)S(1)}, u32[]{:S(2)}, u32[]{:S(2)}) collective-permute-start(bf16[2,144,128]{2,1,0:T(8,128)(2,1)S(1)} %get-tuple-element.56), channel_id=1, source_target_pairs={{0,16},{1,17},{2,18},{3,19},{4,20},{5,21},{6,22},{7,23},{8,24},{9,... | collective-permute-start | bytes 221192 | tf_op jit(solution)/shard_map/ppermute | solution.py:374
  36.1 2.7 %collective-permute-start.4 = (bf16[2,144,128]{2,1,0:T(8,128)(2,1)S(1)}, bf16[2,144,128]{2,1,0:T(8,128)(2,1)S(1)}, u32[]{:S(2)}, u32[]{:S(2)}) collective-permute-start(bf16[2,144,128]{2,1,0:T(8,128)(2,1)S(1)} %get-tuple-element.56), channel_id=1, source_target_pairs={{0,24},{1,25},{2,26},{3,27},{4,28},{5,29},{6,30},{7,31},{32,56},{3... | collective-permute-start | bytes 221192 | tf_op jit(solution)/shard_map/ppermute | solution.py:374
  39.7 17.6 %collective-permute-start.10 = (bf16[4,1,2,32,1024]{4,3,2,1,0:T(8,128)(2,1)S(1)}, bf16[4,1,2,32,1024]{4,3,2,1,0:T(8,128)(2,1)S(1)}, u32[]{:S(2)}, u32[]{:S(2)}) collective-permute-start(bf16[4,1,2,32,1024]{4,3,2,1,0:T(8,128)(2,1)S(1)} %get-tuple-element.94), channel_id=1, source_target_pairs={{0,128},{32,160},{64,192},{96,224},{128,0},{160,32},{192,64},{224,... | collective-permute-start | bytes 1572872 | tf_op jit(solution)/shard_map/ppermute | solution.py:365
  45.7 5.4 %collective-permute-start.7 = (f32[2,128,128]{2,1,0:T(8,128)S(1)}, f32[2,128,128]{2,1,0:T(8,128)S(1)}, u32[]{:S(2)}, u32[]{:S(2)}) collective-permute-start(f32[2,128,128]{2,1,0:T(8,128)S(1)} %get-tuple-element.58), channel_id=1, source_target_pairs={{0,2},{1,3},{2,4},{3,5},{4,6},{5,7},{6,0},{7,1},{8,10},{9,11},{10,... | collective-permute-start | bytes 393224 | tf_op jit(solution)/shard_map/ppermute | solution.py:374
  46.8 6.2 %collective-permute-start.8 = (f32[2,128,128]{2,1,0:T(8,128)S(1)}, f32[2,128,128]{2,1,0:T(8,128)S(1)}, u32[]{:S(2)}, u32[]{:S(2)}) collective-permute-start(f32[2,128,128]{2,1,0:T(8,128)S(1)} %get-tuple-element.59), channel_id=1, source_target_pairs={{0,4},{1,5},{2,6},{3,7},{4,0},{5,1},{6,2},{7,3},{8,12},{9,13},{10,... | collective-permute-start | bytes 393224 | tf_op jit(solution)/shard_map/ppermute | solution.py:374
  49.0 4.1 %collective-permute-start.9 = (f32[2,128,128]{2,1,0:T(8,128)S(1)}, f32[2,128,128]{2,1,0:T(8,128)S(1)}, u32[]{:S(2)}, u32[]{:S(2)}) collective-permute-start(f32[2,128,128]{2,1,0:T(8,128)S(1)} %get-tuple-element.60), channel_id=1, source_target_pairs={{0,6},{1,7},{2,0},{3,1},{4,2},{5,3},{6,4},{7,5},{8,14},{9,15},{10,... | collective-permute-start | bytes 393224 | tf_op jit(solution)/shard_map/ppermute | solution.py:374
  58.0 8.2 %collective-permute-start.11 = (f32[8,128,128]{2,1,0:T(8,128)S(1)}, f32[8,128,128]{2,1,0:T(8,128)S(1)}, u32[]{:S(2)}, u32[]{:S(2)}) collective-permute-start(f32[8,128,128]{2,1,0:T(8,128)S(1)} %get-tuple-element.63), channel_id=1, source_target_pairs={{0,1},{1,0},{2,3},{3,2},{4,5},{5,4},{6,7},{7,6},{8,9},{9,8},{10,11... | collective-permute-start | bytes 1572872 | tf_op jit(solution)/shard_map/ppermute | solution.py:374
  62.6 20.9 %collective-permute-start.12 = (bf16[4,1,2,32,1024]{4,3,2,1,0:T(8,128)(2,1)}, bf16[4,1,2,32,1024]{4,3,2,1,0:T(8,128)(2,1)}, u32[]{:S(2)}, u32[]{:S(2)}) collective-permute-start(bf16[4,1,2,32,1024]{4,3,2,1,0:T(8,128)(2,1)} %get-tuple-element.93), channel_id=1, source_target_pairs={{0,128},{32,160},{64,192},{96,224},{128,0},{160,32},{192,64},{224,... | collective-permute-start | bytes 1572872 | tf_op jit(solution)/shard_map/ppermute | solution.py:365
  70.8 13.5 %all-to-all-start.1 = ((bf16[4,1,2,32,1024]{4,3,2,1,0:T(8,128)(2,1)}), bf16[4,1,2,32,1024]{4,3,2,1,0:T(8,128)(2,1)}, u32[]{:S(2)}, u32[]{:S(2)}) async-start(bf16[4,1,2,32,1024]{4,3,2,1,0:T(8,128)(2,1)} %copy-done.24), calls=%async_computation.1 | async-start | bytes 1048576 | tf_op jit(solution)/shard_map/all_to_all | solution.py:361
  76.9 6.9 %collective-permute-start.13 = (f32[2,16,256]{2,1,0:T(8,128)S(1)}, f32[2,16,256]{2,1,0:T(8,128)S(1)}, u32[]{:S(2)}, u32[]{:S(2)}) collective-permute-start(f32[2,16,256]{2,1,0:T(8,128)S(1)} %stats_kernel.1.refs_5_), channel_id=1, source_target_pairs={{0,128},{32,160},{64,192},{96,224},{128,0},{160,32},{192,64},{224,... | collective-permute-start | bytes 98312 | tf_op jit(solution)/shard_map/ppermute | solution.py:365
  88.8 30.3 %copy-start.3 = (bf16[2,128,1024]{2,1,0:T(8,128)(2,1)S(1)}, bf16[2,128,1024]{2,1,0:T(8,128)(2,1)}, u32[]{:S(2)}) copy-start(bf16[2,128,1024]{2,1,0:T(8,128)(2,1)} %refs_3_.8) | copy-start | bytes 1572868
  88.8 30.3 %copy-start.14 = (f32[2,128,1024]{2,1,0:T(8,128)S(1)}, f32[2,128,1024]{2,1,0:T(8,128)}, u32[]{:S(2)}) copy-start(f32[2,128,1024]{2,1,0:T(8,128)} %copy-done.13) | copy-start | bytes 3145732
  88.8 8.0 %collective-permute-start.14 = (f32[16,256]{1,0:T(8,128)S(1)}, f32[16,256]{1,0:T(8,128)S(1)}, u32[]{:S(2)}, u32[]{:S(2)}) collective-permute-start(f32[16,256]{1,0:T(8,128)S(1)} %get-tuple-element.67.refs_8_), channel_id=1, source_target_pairs={{0,128},{32,160},{64,192},{96,224},{128,0},{160,32},{192,64},{224,... | collective-permute-start | bytes 49160 | tf_op jit(solution)/shard_map/ppermute | solution.py:365
  101.7 24.0 %collective-permute-start.16 = (bf16[4,1,2,32,1024]{4,3,2,1,0:T(8,128)(2,1)S(1)}, bf16[4,1,2,32,1024]{4,3,2,1,0:T(8,128)(2,1)S(1)}, u32[]{:S(2)}, u32[]{:S(2)}) collective-permute-start(bf16[4,1,2,32,1024]{4,3,2,1,0:T(8,128)(2,1)S(1)} %get-tuple-element.68.refs_6_), channel_id=1, source_target_pairs={{0,128},{32,160},{64,192},{96,224},{128,0},{160,32},{192,64},{224,... | collective-permute-start | bytes 1572872 | tf_op jit(solution)/shard_map/ppermute | solution.py:365
  123.7 6.7 %collective-permute-start.15 = (f32[8,136,128]{2,1,0:T(8,128)}, f32[8,136,128]{2,1,0:T(8,128)}, u32[]{:S(2)}, u32[]{:S(2)}) collective-permute-start(f32[8,136,128]{2,1,0:T(8,128)} %get-tuple-element.71), channel_id=1, source_target_pairs={{0,1},{1,0},{2,3},{3,2},{4,5},{5,4},{6,7},{7,6},{8,9},{9,8},{10,11... | collective-permute-start | bytes 1671176 | tf_op jit(solution)/shard_map/ppermute | solution.py:374
  126.8 39.9 %all-to-all-start.3 = ((bf16[4,2,2,32,1024]{4,3,2,1,0:T(8,128)(2,1)}), bf16[4,2,2,32,1024]{4,3,2,1,0:T(8,128)(2,1)S(1)}, u32[]{:S(2)}, u32[]{:S(2)}) async-start(bf16[4,2,2,32,1024]{4,3,2,1,0:T(8,128)(2,1)} %join_kernel.1.refs_3_), calls=%async_computation.3 | async-start | bytes 2097152 | tf_op jit(solution)/shard_map/all_to_all | solution.py:361
  131.6 6.6 %collective-permute-start.17 = (f32[2,136,128]{2,1,0:T(8,128)S(1)}, f32[2,136,128]{2,1,0:T(8,128)S(1)}, u32[]{:S(2)}, u32[]{:S(2)}) collective-permute-start(f32[2,136,128]{2,1,0:T(8,128)S(1)} %get-tuple-element.75), channel_id=1, source_target_pairs={{0,2},{1,3},{2,4},{3,5},{4,6},{5,7},{6,0},{7,1},{8,10},{9,11},{10,... | collective-permute-start | bytes 417800 | tf_op jit(solution)/shard_map/ppermute | solution.py:374
  132.7 9.0 %collective-permute-start.18 = (f32[2,136,128]{2,1,0:T(8,128)S(1)}, f32[2,136,128]{2,1,0:T(8,128)S(1)}, u32[]{:S(2)}, u32[]{:S(2)}) collective-permute-start(f32[2,136,128]{2,1,0:T(8,128)S(1)} %get-tuple-element.76), channel_id=1, source_target_pairs={{0,4},{1,5},{2,6},{3,7},{4,0},{5,1},{6,2},{7,3},{8,12},{9,13},{10,... | collective-permute-start | bytes 417800 | tf_op jit(solution)/shard_map/ppermute | solution.py:374
  134.9 6.8 %collective-permute-start.19 = (f32[2,136,128]{2,1,0:T(8,128)S(1)}, f32[2,136,128]{2,1,0:T(8,128)S(1)}, u32[]{:S(2)}, u32[]{:S(2)}) collective-permute-start(f32[2,136,128]{2,1,0:T(8,128)S(1)} %get-tuple-element.77), channel_id=1, source_target_pairs={{0,6},{1,7},{2,0},{3,1},{4,2},{5,3},{6,4},{7,5},{8,14},{9,15},{10,... | collective-permute-start | bytes 417800 | tf_op jit(solution)/shard_map/ppermute | solution.py:374
  142.4 11.9 %collective-permute-start.22 = (bf16[2,144,128]{2,1,0:T(8,128)(2,1)S(1)}, bf16[2,144,128]{2,1,0:T(8,128)(2,1)S(1)}, u32[]{:S(2)}, u32[]{:S(2)}) collective-permute-start(bf16[2,144,128]{2,1,0:T(8,128)(2,1)S(1)} %get-tuple-element.82), channel_id=1, source_target_pairs={{8,0},{9,1},{10,2},{11,3},{12,4},{13,5},{14,6},{15,7},{16,8},{17,9... | collective-permute-start | bytes 221192 | tf_op jit(solution)/shard_map/ppermute | solution.py:374
  143.7 14.1 %collective-permute-start.21 = (bf16[2,144,128]{2,1,0:T(8,128)(2,1)S(1)}, bf16[2,144,128]{2,1,0:T(8,128)(2,1)S(1)}, u32[]{:S(2)}, u32[]{:S(2)}) collective-permute-start(bf16[2,144,128]{2,1,0:T(8,128)(2,1)S(1)} %get-tuple-element.82), channel_id=1, source_target_pairs={{16,0},{17,1},{18,2},{19,3},{20,4},{21,5},{22,6},{23,7},{24,8},{25... | collective-permute-start | bytes 221192 | tf_op jit(solution)/shard_map/ppermute | solution.py:374
  145.0 14.7 %collective-permute-start.20 = (bf16[2,144,128]{2,1,0:T(8,128)(2,1)S(1)}, bf16[2,144,128]{2,1,0:T(8,128)(2,1)S(1)}, u32[]{:S(2)}, u32[]{:S(2)}) collective-permute-start(bf16[2,144,128]{2,1,0:T(8,128)(2,1)S(1)} %get-tuple-element.82), channel_id=1, source_target_pairs={{24,0},{25,1},{26,2},{27,3},{28,4},{29,5},{30,6},{31,7},{56,32},{5... | collective-permute-start | bytes 221192 | tf_op jit(solution)/shard_map/ppermute | solution.py:374
  162.1 5.7 %collective-permute-start.23 = (f32[2,128,128]{2,1,0:T(8,128)}, f32[2,128,128]{2,1,0:T(8,128)S(1)}, u32[]{:S(2)}, u32[]{:S(2)}) collective-permute-start(f32[2,128,128]{2,1,0:T(8,128)} %get-tuple-element.84), channel_id=1, source_target_pairs={{0,2},{1,3},{2,4},{3,5},{4,6},{5,7},{6,0},{7,1},{8,10},{9,11},{10,... | collective-permute-start | bytes 393224 | tf_op jit(solution)/shard_map/ppermute | solution.py:374
  164.2 7.3 %collective-permute-start.24 = (f32[2,128,128]{2,1,0:T(8,128)}, f32[2,128,128]{2,1,0:T(8,128)S(1)}, u32[]{:S(2)}, u32[]{:S(2)}) collective-permute-start(f32[2,128,128]{2,1,0:T(8,128)} %get-tuple-element.85), channel_id=1, source_target_pairs={{0,4},{1,5},{2,6},{3,7},{4,0},{5,1},{6,2},{7,3},{8,12},{9,13},{10,... | collective-permute-start | bytes 393224 | tf_op jit(solution)/shard_map/ppermute | solution.py:374
  166.4 5.2 %collective-permute-start.25 = (f32[2,128,128]{2,1,0:T(8,128)S(1)}, f32[2,128,128]{2,1,0:T(8,128)S(1)}, u32[]{:S(2)}, u32[]{:S(2)}) collective-permute-start(f32[2,128,128]{2,1,0:T(8,128)S(1)} %get-tuple-element.86), channel_id=1, source_target_pairs={{0,6},{1,7},{2,0},{3,1},{4,2},{5,3},{6,4},{7,5},{8,14},{9,15},{10,... | collective-permute-start | bytes 393224 | tf_op jit(solution)/shard_map/ppermute | solution.py:374
  173.8 3.9 %collective-permute-start.26 = (f32[8,128,128]{2,1,0:T(8,128)S(1)}, f32[8,128,128]{2,1,0:T(8,128)S(1)}, u32[]{:S(2)}, u32[]{:S(2)}) collective-permute-start(f32[8,128,128]{2,1,0:T(8,128)S(1)} %get-tuple-element.89), channel_id=1, source_target_pairs={{0,1},{1,0},{2,3},{3,2},{4,5},{5,4},{6,7},{7,6},{8,9},{9,8},{10,11... | collective-permute-start | bytes 1572872 | tf_op jit(solution)/shard_map/ppermute | solution.py:374
  (29 other events, 215.7 us)
